TPU v7x, 512 devices: a whole 4x8x8 slice. The times are simulated.
512 devices in a mesh: cls: 64 (over x, y, core), dp: 8 (over z).
Axes of the slice: x: 4, y: 8, z: 8, core: 2. Of those that a mesh axis runs over, the one named last changes fastest.
Arguments:
- features: bfloat16 [65536, 4096], P(('cls', 'dp')), may hold values from -24 to 24
- proj: bfloat16 [4096, 128], replicated, may hold values from -0.09375 to 0.09375
- class_emb: bfloat16 [524288, 128], P('cls'), may hold values from -64 to 64
- lists: int32 [64, 8, 6], P(None, 'dp'), may hold values from -1 to 63, as said below
- labels: int32 [64, 8, 128], P(None, 'dp'), may hold values from 0 to 524287, as said below
Outputs:
- loss: float32 [65536], P(('cls', 'dp'))
- class_grad: float32 [524288, 128], P(('cls', 'dp'))
- proj_grad: float32 [4096, 128], P(('cls', 'dp'))
Inputs may be any that keep to these rules, and one draw needn't show every extreme that they name: Each row block lists 1 to 6 distinct class blocks in the first entries of its row, -1 after. Within one group, each class block is listed by at most 6 row blocks, and in every group some class block is listed by exactly 6 of them. `labels`: each row's label lies in a class block that its row block lists.
All inputs are finite; a program needn't handle non-finite values.
Results may differ from a plain program's by a relative error of at most 0.014.
Values may be sent and summed in bfloat16 or wider, within the bound.
No kernel may reach another device: no remote copies, remote signals or barrier semaphores. Data moves between devices by JAX's collectives and lax.ppermute only.
A program may use at most 128 MiB of HBM per device.

v0:
```python
import jax
import jax.numpy as jnp
from jax import lax
from jax.sharding import PartitionSpec as P

LIST = 6


NEG = -1e30


def merged(value, axis, combine):
    everything = jax.tree.map(lambda part: lax.all_gather(part, axis), value)
    initial = jax.tree.map(lambda part: part[0], everything)

    def hop(k, so_far):
        return combine(so_far, jax.tree.map(lambda part: part[k], everything))

    return lax.fori_loop(1, lax.axis_size(axis), hop, initial)


def block_scores(rows_in, factors):
    return lax.dot_general(
        rows_in, factors, (((1,), (1,)), ((), ())), preferred_element_type=jnp.float32
    )


def combine_stats(first, second):
    peak = jnp.maximum(first[0], second[0])
    mass = first[1] * jnp.exp(first[0] - peak) + second[1] * jnp.exp(second[0] - peak)
    return (peak, mass, jnp.maximum(first[2], second[2]))


def local(features, proj, class_emb, lists, labels):
    block_count = lax.axis_size("cls")
    group_count = lax.axis_size("dp")
    own_block = lax.axis_index("cls")
    own_group = lax.axis_index("dp")
    row_count = features.shape[0]
    block_width = class_emb.shape[0]
    rank_width = class_emb.shape[1]
    hidden = jnp.dot(features, proj, preferred_element_type=jnp.float32).astype(jnp.bfloat16)
    table = lists[:, 0, :]
    group_labels = labels[:, 0, :]
    block_ids = jnp.arange(block_count, dtype=jnp.int32)
    own_list = lax.dynamic_index_in_dim(table, own_block, 0, keepdims=False)
    targets = jnp.any(own_list[None, :] == block_ids[:, None], axis=1)
    listed_by = jnp.any(table == own_block, axis=1)
    list_rank = jnp.cumsum(listed_by.astype(jnp.int32)) - 1
    live_count = jnp.sum(listed_by.astype(jnp.int32))
    slot_ids = jnp.arange(LIST, dtype=jnp.int32)
    chosen = (list_rank[None, :] == slot_ids[:, None]) & listed_by[None, :]
    source_of = jnp.sum(jnp.where(chosen, block_ids[None, :], 0), axis=1)
    outbox = jnp.where(targets[:, None, None], hidden[None], jnp.zeros((), jnp.bfloat16))
    inbox = lax.all_to_all(outbox, "cls", split_axis=0, concat_axis=0, tiled=True)
    arrived = jnp.take(inbox, source_of, axis=0)

    def first_pass(slot_index, carry):
        peak_all, mass_all, label_all = carry
        source = source_of[slot_index]
        scores = block_scores(arrived[slot_index], class_emb)
        peak = jnp.max(scores, axis=1)
        mass = jnp.sum(jnp.exp(scores - peak[:, None]), axis=1)
        label_local = group_labels[source] - own_block * block_width
        inside = (label_local >= 0) & (label_local < block_width)
        label_score = jnp.take_along_axis(
            scores, jnp.clip(label_local, 0, block_width - 1)[:, None], axis=1
        )[:, 0]
        peak_all = peak_all.at[source].set(peak)
        mass_all = mass_all.at[source].set(mass)
        label_all = label_all.at[source].set(jnp.where(inside, label_score, NEG))
        return (peak_all, mass_all, label_all)

    start = (
        jnp.full((block_count, row_count), NEG, jnp.float32),
        jnp.zeros((block_count, row_count), jnp.float32),
        jnp.full((block_count, row_count), NEG, jnp.float32),
    )
    peak_local, mass_local, label_local_all = lax.fori_loop(
        jnp.int32(0), live_count, first_pass, start
    )
    peak_all, mass_all, label_all = merged(
        (peak_local, mass_local, label_local_all), "cls", combine_stats
    )
    log_norm = peak_all + jnp.log(mass_all)
    loss = lax.dynamic_index_in_dim(log_norm - label_all, own_block, 0, keepdims=False)
    class_ids = jnp.arange(block_width, dtype=jnp.int32)

    def second_pass(slot_index, carry):
        class_part, outbox_back = carry
        source = source_of[slot_index]
        rows_in = arrived[slot_index]
        scores = block_scores(rows_in, class_emb)
        probs = jnp.exp(scores - log_norm[source][:, None])
        label_local = group_labels[source] - own_block * block_width
        target = (class_ids[None, :] == label_local[:, None]).astype(jnp.float32)
        weights = (probs - target).astype(jnp.bfloat16)
        class_part = class_part + lax.dot_general(
            weights, rows_in, (((0,), (0,)), ((), ())), preferred_element_type=jnp.float32
        )
        back_rows = jnp.dot(weights, class_emb, preferred_element_type=jnp.float32).astype(
            jnp.bfloat16
        )
        outbox_back = lax.dynamic_update_index_in_dim(outbox_back, back_rows, source, 0)
        return (class_part, outbox_back)

    grad_start = (
        jnp.zeros((block_width, rank_width), jnp.float32),
        jnp.zeros((block_count, row_count, rank_width), jnp.bfloat16),
    )
    class_part, outbox_back = lax.fori_loop(jnp.int32(0), live_count, second_pass, grad_start)
    returned = lax.all_to_all(outbox_back, "cls", split_axis=0, concat_axis=0, tiled=True)
    row_grad = jnp.sum(returned, axis=0, dtype=jnp.float32).astype(jnp.bfloat16)
    class_grad = lax.psum_scatter(
        class_part.astype(jnp.bfloat16), "dp", scatter_dimension=0, tiled=True
    ).astype(jnp.float32)
    proj_part = lax.dot_general(
        features, row_grad, (((0,), (0,)), ((), ())), preferred_element_type=jnp.float32
    )
    summed = lax.psum(proj_part, ("cls", "dp"))
    share = proj_part.shape[0] // (block_count * group_count)
    position = own_block * group_count + own_group
    proj_grad = lax.dynamic_slice_in_dim(summed, position * share, share, 0)
    return (loss, class_grad, proj_grad)


def solution(mesh):
    in_specs = (
        P(("cls", "dp"), None),
        P(),
        P("cls", None),
        P(None, "dp", None),
        P(None, "dp", None),
    )
    out_specs = (P(("cls", "dp")), P(("cls", "dp"), None), P(("cls", "dp"), None))
    return jax.shard_map(local, mesh=mesh, in_specs=in_specs, out_specs=out_specs, check_vma=False)
```

profile of v0, /device:TPU:1, one launch (start us, length us, event | category | flops | bytes accessed | tf_op | source)
XLA Modules:
  0.0 889.4 jit_solution(12144770109047327342)
XLA Ops:
  8.4 1.6 convolution_convert_fusion.1
  10.1 1.5 broadcast_select_fusion.3
  11.6 11.9 %all-to-all-start = ((bf16[64,128,128]{2,1,0:T(8,128)(2,1)}), bf16[64,128,128]{2,1,0:T(8,128)(2,1)}, u32[]{:S(2)}, u32[]{:S(2)}) async-start(bf16[64,128,128]{2,1,0:T(8,128)(2,1)} %broadcast_select_fusion.3), calls=%async_computation | async-start | bytes 4194304 | tf_op jit(solution)/shard_map/all_to_all | solution.py:55
  24.7 50.1 %all-to-all-done = bf16[64,128,128]{2,1,0:T(8,128)(2,1)} async-done(((bf16[64,128,128]{2,1,0:T(8,128)(2,1)}), bf16[64,128,128]{2,1,0:T(8,128)(2,1)}, u32[]{:S(2)}, u32[]{:S(2)}) %all-to-all-start) | async-done | bytes 2097184 | tf_op jit(solution)/shard_map/all_to_all | solution.py:55
  74.8 2.8 gather_fusion.1
  78.7 44.1 %while.53 = (s32[]{:T(128)}, f32[64,128]{1,0:T(8,128)S(1)}, f32[64,128]{1,0:T(8,128)S(1)}, f32[64,128]{1,0:T(8,128)S(1)}, s32[]{:T(128)}, /*index=5*/s32[6]{0:T(...) while((s32[]{:T(128)}, f32[64,128]{1,0:T(8,128)S(1)}, ...), condition=%wide.region_9.10_spmd, body=%wide.region_5.9_spmd.sunk | while | flops 271584512 | bytes 10535716 | solution.py:79
  83.4 2.6 fusion.52
  86.0 2.5 gather_fusion
  88.5 2.9 exponential_reduce_fusion.2
  98.0 2.6 fusion.52
  100.7 2.4 gather_fusion
  103.1 2.9 exponential_reduce_fusion.2
  112.6 2.7 fusion.52
  115.2 2.1 gather_fusion
  117.3 2.9 exponential_reduce_fusion.2
  125.0 124.1 %all-gather.9.cloned.1.call-done = f32[4096,128]{1,0:T(8,128)} async-done(((f32[64,128]{1,0:T(8,128)}), f32[4096,128]{1,0:T(8,128)}) %all-gather.9.cloned.1.call-update) | async-done | bytes 2097168 | tf_op jit(solution)/shard_map/all_gather | solution.py:13
  249.8 83.7 %all-gather.7.cloned.1.call-done = f32[4096,128]{1,0:T(8,128)} async-done(((f32[64,128]{1,0:T(8,128)}), f32[4096,128]{1,0:T(8,128)}) %all-gather.7.cloned.1.call-update) | async-done | bytes 2097168 | tf_op jit(solution)/shard_map/all_gather | solution.py:13
  334.3 83.2 %all-gather.11.cloned.1.call-done = f32[4096,128]{1,0:T(8,128)} async-done(((f32[64,128]{1,0:T(8,128)}), f32[4096,128]{1,0:T(8,128)}) %all-gather.11.cloned.1.call-update) | async-done | bytes 2097168 | tf_op jit(solution)/shard_map/all_gather | solution.py:13
  418.3 53.7 %while.54 = (s32[]{:T(128)}, f32[64,128]{1,0:T(8,128)S(1)}, f32[64,128]{1,0:T(8,128)S(1)}, f32[64,128]{1,0:T(8,128)S(1)}, f32[64,64,128]{2,1,0:T(8,128)}, /*inde...) while((s32[]{:T(128)}, f32[64,128]{1,0:T(8,128)S(1)}, ...), condition=%wide.region_11.12_spmd, body=%wide.region_10.11_spmd.sunk | while | flops 57349 | bytes 295051 | solution.py:19
  472.0 1.9 broadcast_in_dim.85
  473.9 2.3 broadcast_in_dim.87
  476.2 33.1 %while.55 = (s32[]{:T(128)}, f32[8192,128]{1,0:T(8,128)}, bf16[64,128,128]{2,1,0:T(8,128)(2,1)}, s32[]{:T(128)}, bf16[6,128,128]{2,1,0:T(8,128)(2,1)S(1)}, /*ind...) while((s32[]{:T(128)}, f32[8192,128]{1,0:T(8,128)}, ...), condition=%wide.region_13.14_spmd.clone, body=%wide.region_12.13_spmd.clone.sunk | while | flops 811614336 | bytes 52530472 | solution.py:111
  483.6 1.4 convolution_add_fusion.2
  485.0 2.0 copy-done.2
  495.8 2.0 copy-done.2
  506.6 2.0 copy-done.2
  509.3 37.1 %all-to-all-start.1 = ((bf16[64,128,128]{2,1,0:T(8,128)(2,1)}), bf16[64,128,128]{2,1,0:T(8,128)(2,1)S(1)}, u32[]{:S(2)}, u32[]{:S(2)}) async-start(bf16[64,128,128]{2,1,0:T(8,128)(2,1)} %get-tuple-element.476), calls=%async_computation.2 | async-start | bytes 4194304 | tf_op jit(solution)/shard_map/all_to_all | solution.py:112
  546.5 3.7 convert_element_type.48
  550.3 47.4 %all-to-all-done.1 = bf16[64,128,128]{2,1,0:T(8,128)(2,1)S(1)} async-done(((bf16[64,128,128]{2,1,0:T(8,128)(2,1)}), bf16[64,128,128]{2,1,0:T(8,128)(2,1)S(1)}, u32[]{:S(2)}, u32[]{:S(2)}) %all-to-all-start.1) | async-done | bytes 2097184 | tf_op jit(solution)/shard_map/all_to_all | solution.py:112
  598.0 1.8 convolution_bitcast_fusion
  600.3 1.8 convert_element_type.49
  602.1 279.2 %all-reduce.2.cloned.1.call-done = f32[4096,128]{0,1:T(8,128)} async-done(((f32[4096,128]{0,1:T(8,128)}), f32[4096,128]{0,1:T(8,128)}) %all-reduce.2.cloned.1.call-update) | async-done | bytes 2097168 | tf_op jit(solution)/shard_map/psum | solution.py:120
  (171 shorter events, 91.7 us)
Async XLA Ops:
  7.2 1.2 copy-start
  11.6 12.0 %copy-start.8 = (s32[64,1,6]{0,1,2:T(1,128)S(1)}, s32[64,1,6]{0,1,2:T(1,128)}, u32[]{:S(2)}) copy-start(s32[64,1,6]{0,1,2:T(1,128)} %param.20) | copy-start | bytes 4612
  11.6 67.1 %copy-start.3 = (bf16[8192,128]{1,0:T(8,128)(2,1)S(1)}, bf16[8192,128]{1,0:T(8,128)(2,1)}, u32[]{:S(2)}) copy-start(bf16[8192,128]{1,0:T(8,128)(2,1)} %param.19) | copy-start | bytes 6291460
  11.6 67.1 %copy-start.7 = (s32[2]{0:T(128)S(1)}, s32[2]{0:T(128)}, u32[]{:S(2)}) copy-start(s32[2]{0:T(128)} %constant.217.clone.1) | copy-start | bytes 28
  11.6 63.2 %all-to-all-start = ((bf16[64,128,128]{2,1,0:T(8,128)(2,1)}), bf16[64,128,128]{2,1,0:T(8,128)(2,1)}, u32[]{:S(2)}, u32[]{:S(2)}) async-start(bf16[64,128,128]{2,1,0:T(8,128)(2,1)} %broadcast_select_fusion.3), calls=%async_computation | async-start | bytes 4194304 | tf_op jit(solution)/shard_map/all_to_all | solution.py:55
  23.5 225.5 %all-gather.9.cloned.1.call-start = ((), (), s32[]{:S(2)}) async-start(), calls=%async_computation.6 | async-start | bytes 2129920 | tf_op jit(solution)/shard_map/all_gather | solution.py:13
  122.8 0.6 copy-start.6
  122.8 0.7 copy-start.5
  122.9 1.4 copy-start.4
  123.5 210.1 %all-gather.7.cloned.1.call-start = ((), (), s32[]{:S(2)}) async-start(), calls=%async_computation.5 | async-start | bytes 2129920 | tf_op jit(solution)/shard_map/all_gather | solution.py:13
  124.2 293.3 %all-gather.11.cloned.1.call-start = ((), (), s32[]{:S(2)}) async-start(), calls=%async_computation.7 | async-start | bytes 2129920 | tf_op jit(solution)/shard_map/all_gather | solution.py:13
  481.4 2.2 copy-start.1
  485.0 2.0 copy-start.2
  492.2 2.2 copy-start.1
  495.8 2.0 copy-start.2
  503.0 2.2 copy-start.1
  506.6 2.0 copy-start.2
  509.3 88.4 %all-to-all-start.1 = ((bf16[64,128,128]{2,1,0:T(8,128)(2,1)}), bf16[64,128,128]{2,1,0:T(8,128)(2,1)S(1)}, u32[]{:S(2)}, u32[]{:S(2)}) async-start(bf16[64,128,128]{2,1,0:T(8,128)(2,1)} %get-tuple-element.476), calls=%async_computation.2 | async-start | bytes 4194304 | tf_op jit(solution)/shard_map/all_to_all | solution.py:112
  546.4 53.9 %reduce-scatter.2.cloned.1.call-start = ((), (), s32[]{:S(2)}) async-start(), calls=%async_computation.3 | async-start | bytes 2359296 | tf_op jit(solution)/shard_map/reduce_scatter | solution.py:114
  550.3 331.0 %all-reduce.2.cloned.1.call-start = ((), (), s32[]{:S(2)}) async-start(), calls=%async_computation.4 | async-start | bytes 4194304 | tf_op jit(solution)/shard_map/psum | solution.py:120
Sparse Core Ops, SparseCore 0:
  123.6 125.4 all-gather.8
  253.0 80.5 all-gather.6
  336.9 80.5 all-gather.10
  550.4 44.5 reduce-scatter.1
  599.9 281.3 all-reduce.1
where the time goes:
time: 897 us; the launch traced here: 889 us
  waiting for transfers between devices  669 us (75%)
  other arithmetic  83.1 us (9%)
  starting transfers between devices  49.3 us (5%)
  local copies, waits for them, and re-layouts  32.1 us (4%)
  matrix products  23.5 us (3%)
  loops' own time  18.4 us (2%)
  between operations  14 us (2%)
    all_gather x3, waiting for transfers between devices, merged(): everything = jax.tree.map(lambda part: lax.all_gather(part, axis), value)  291 us
    psum x1, waiting for transfers between devices, local(): summed = lax.psum(proj_part, ('cls', 'dp'))  279 us
    add x63, other arithmetic, combine_stats(): first[1] * jnp.exp(first[0] - peak) + second[1] * jnp.exp(second[0] - peak)  52.5 us
    all_to_all x1, waiting for transfers between devices, local(): lax.all_to_all(outbox, 'cls', split_axis=0, concat_axis=0, tiled=True)  50.1 us
    all_to_all x1, waiting for transfers between devices, local(): lax.all_to_all(outbox_back, 'cls', split_axis=0, concat_axis=0, tiled=True)  47.4 us
    all_to_all x1, starting transfers between devices, local(): lax.all_to_all(outbox_back, 'cls', split_axis=0, concat_axis=0, tiled=True)  37.1 us
  transfers between devices with their start and end apart: 7, of which 6 were waited for; matrix products, arithmetic and copies ran while one was open for 1% of the time, Pallas kernels for 0%

commit v1 on v0

v1 whole, which is shorter than its diff:
```python
import jax
import jax.numpy as jnp
from jax import lax
from jax.experimental import pallas as pl
from jax.experimental.pallas import tpu as pltpu
from jax.sharding import PartitionSpec as P

LIST = 6
NX, NY, NK = 4, 8, 2
TILE = 1024
NEG = -1e30
F32 = jnp.float32
BF16 = jnp.bfloat16
GROUP_Y = [[x * 16 + y * 2 + k for y in range(NY)] for x in range(NX) for k in range(NK)]
GROUP_X = [[x * 16 + y * 2 + k for x in range(NX)] for y in range(NY) for k in range(NK)]
SWAP_K = [(c, c ^ 1) for c in range(NX * NY * NK)]


def exchange(value, groups):
    return lax.all_to_all(value, "cls", 0, 0, axis_index_groups=groups, tiled=True)


def spread(value, count):
    return jnp.broadcast_to(value[None], (count,) + value.shape)


def gather_cls(block):
    along_y = exchange(spread(block, NY), GROUP_Y)
    own = exchange(spread(along_y, NX), GROUP_X).reshape((NX * NY,) + block.shape)
    return own, lax.ppermute(own, "cls", SWAP_K)


def scatter_cls(outbox):
    swapped = lax.ppermute(outbox[1], "cls", SWAP_K)
    total = (outbox[0].astype(F32) + swapped.astype(F32)).astype(BF16)
    total = jnp.sum(exchange(total, GROUP_X), axis=0, dtype=F32).astype(BF16)
    return jnp.sum(exchange(total, GROUP_Y), axis=0, dtype=F32).astype(BF16)


def scores_of(factors, rows):
    return lax.dot_general(factors, rows, (((1,), (1,)), ((), ())), preferred_element_type=F32)


def stats_kernel(slots_ref, own_ref, other_ref, label_ref, emb_ref, rows_ref, stat_ref, peak_ref, mass_ref, score_ref):
    step = pl.program_id(0)
    width = rows_ref.shape[0] // LIST

    @pl.when(step == 0)
    def _():
        for slot in range(LIST):
            place = slots_ref[slot]
            near = own_ref[lax.rem(place, NX * NY)]
            far = other_ref[lax.rem(place, NX * NY)]
            rows_ref[slot * width:(slot + 1) * width, :] = jnp.where(place < NX * NY, near, far)
        peak_ref[...] = jnp.full(peak_ref.shape, NEG, F32)
        mass_ref[...] = jnp.zeros(mass_ref.shape, F32)
        score_ref[...] = jnp.zeros(score_ref.shape, F32)

    factors = emb_ref[...]
    tile = factors.shape[0]
    class_ids = lax.broadcasted_iota(jnp.int32, (tile // 8, 8, 2 * width), 0) * 8 + lax.broadcasted_iota(jnp.int32, (tile // 8, 8, 2 * width), 1)
    for pair in range(LIST // 2):
        cut = slice(pair * 2 * width, (pair + 1) * 2 * width)
        scores = scores_of(factors, rows_ref[cut, :]).reshape(tile // 8, 8, 2 * width)
        local_label = label_ref[0:1, cut] - step * tile
        hit = class_ids == local_label[None]
        score_ref[:, cut] += jnp.sum(jnp.where(hit, scores, 0.0), axis=0)
        old = peak_ref[:, cut]
        new = jnp.maximum(old, jnp.max(scores, axis=0))
        mass_ref[:, cut] = mass_ref[:, cut] * jnp.exp(old - new) + jnp.sum(jnp.exp(scores - new[None]), axis=0)
        peak_ref[:, cut] = new

    @pl.when(step == pl.num_programs(0) - 1)
    def _():
        peak = jnp.max(peak_ref[...], axis=0, keepdims=True)
        mass = jnp.sum(mass_ref[...] * jnp.exp(peak_ref[...] - peak), axis=0, keepdims=True)
        norm = peak + jnp.log(mass)
        score = jnp.sum(score_ref[...], axis=0, keepdims=True)
        stat_ref[...] = jnp.zeros(stat_ref.shape, F32)
        for slot in range(LIST):
            stat_ref[slot:slot + 1, :] = norm[:, slot * width:(slot + 1) * width]
            stat_ref[8 + slot:9 + slot, :] = score[:, slot * width:(slot + 1) * width]


def grads_kernel(slots_ref, live_ref, query_ref, stat_ref, label_ref, rows_ref, emb_ref, part_ref, back_ref, loss_ref, norm_ref, total_ref):
    step = pl.program_id(0)
    width = rows_ref.shape[0] // LIST

    def combined(which):
        norms, label_score = [], jnp.zeros((1, width), F32)
        for entry in range(LIST):
            place = query_ref[which * LIST + entry]
            base = jnp.maximum(place, 0)
            norm = stat_ref[pl.ds(base, 1), :]
            score = stat_ref[pl.ds(base + 8, 1), :]
            norms.append(jnp.where(place >= 0, norm, NEG))
            label_score = label_score + jnp.where(place >= 0, score, 0.0)
        peak = norms[0]
        for norm in norms[1:]:
            peak = jnp.maximum(peak, norm)
        mass = jnp.zeros((1, width), F32)
        for norm in norms:
            mass = mass + jnp.exp(norm - peak)
        return peak + jnp.log(mass), label_score

    @pl.when(step == 0)
    def _():
        for slot in range(LIST):
            norm, _ = combined(slot)
            norm_ref[0:1, slot * width:(slot + 1) * width] = jnp.where(slot < live_ref[0], norm, -NEG)
        norm, label_score = combined(LIST)
        loss_ref[...] = norm - label_score
        total_ref[...] = jnp.zeros(total_ref.shape, F32)
        back_ref[...] = jnp.zeros(back_ref.shape, BF16)

    factors = emb_ref[...]
    tile = factors.shape[0]
    rows = rows_ref[...]
    scores = scores_of(factors, rows)
    probs = jnp.exp(scores - norm_ref[0:1, :])
    class_ids = lax.broadcasted_iota(jnp.int32, scores.shape, 0)
    hit = class_ids == label_ref[0:1, :] - step * tile
    weights = jnp.where(hit, probs - 1.0, probs).astype(BF16)
    part_ref[...] = jnp.dot(weights, rows, preferred_element_type=F32).astype(BF16)
    total_ref[...] += lax.dot_general(factors, weights, (((0,), (0,)), ((), ())), preferred_element_type=F32)

    @pl.when(step == pl.num_programs(0) - 1)
    def _():
        for slot in range(LIST):
            @pl.when(slot < live_ref[0])
            def _():
                back_ref[slots_ref[slot]] = total_ref[:, slot * width:(slot + 1) * width].T.astype(BF16)


def column_order(features, parts):
    rows, depth = features.shape
    span = parts * 128
    source = lax.broadcasted_iota(jnp.int32, (span, span), 0)
    target = lax.broadcasted_iota(jnp.int32, (span, span), 1)
    group, rest = target // 128, target % 128
    wanted = (rest // 8) * (8 * parts) + group * 8 + rest % 8
    permutation = (source == wanted).astype(BF16)
    chunks = features.reshape(rows * (depth // span), span)
    moved = jnp.dot(chunks, permutation, preferred_element_type=F32).astype(BF16)
    moved = moved.reshape(rows, depth // span, parts, 128)
    return jnp.transpose(moved, (2, 0, 1, 3)).reshape(parts, rows, depth // parts)


def local(features, proj, class_emb, lists, labels):
    blocks = lax.axis_size("cls")
    groups = lax.axis_size("dp")
    own_block = lax.axis_index("cls")
    width = features.shape[0]
    block_width, rank_width = class_emb.shape
    hidden = jnp.dot(features, proj, preferred_element_type=F32).astype(BF16)
    near, far = gather_cls(hidden)

    table = lists[:, 0, :]
    group_labels = labels[:, 0, :]
    block_ids = jnp.arange(blocks, dtype=jnp.int32)
    places = ((block_ids ^ own_block) & 1) * (NX * NY) + block_ids // 2
    listed_by = jnp.any(table == own_block, axis=1)
    list_rank = jnp.cumsum(listed_by.astype(jnp.int32)) - 1
    live = jnp.sum(listed_by.astype(jnp.int32))
    slot_ids = jnp.arange(LIST, dtype=jnp.int32)
    chosen = (list_rank[None, :] == slot_ids[:, None]) & listed_by[None, :]
    slot_places = jnp.sum(jnp.where(chosen, places[None, :], 0), axis=1)
    same = (table[:, :, None, None] == table[None, None]) & (block_ids[None, None, :, None] < block_ids[:, None, None, None])
    entry_rank = jnp.sum(same.astype(jnp.int32), axis=(2, 3))
    entry_place = (((table ^ own_block) & 1) * (NX * NY) + table // 2) * 16 + entry_rank
    entry_place = jnp.where(table >= 0, entry_place, -1)
    asked = jnp.concatenate([chosen, (block_ids == own_block)[None]], axis=0)
    queries = jnp.sum(jnp.where(asked[:, :, None], entry_place[None], 0), axis=1).reshape(-1)
    slot_labels = jnp.sum(jnp.where(chosen[:, :, None], group_labels[None], 0), axis=1)
    slot_labels = jnp.where(slot_ids[:, None] < live, slot_labels - own_block * block_width, -1)
    slot_labels = spread(slot_labels.reshape(-1), 8)

    steps = block_width // TILE
    all_rows = LIST * width
    smem = pl.BlockSpec(memory_space=pltpu.SMEM)
    whole = pl.BlockSpec(memory_space=pltpu.VMEM)
    tiled = pl.BlockSpec((TILE, rank_width), lambda i: (i, 0))
    fixed = lambda shape: pl.BlockSpec(shape, lambda i: (0,) * len(shape))
    params = pltpu.CompilerParams(vmem_limit_bytes=48 * 1024 * 1024)
    rows, stats = pl.pallas_call(
        stats_kernel,
        grid=(steps,),
        in_specs=[smem, whole, whole, whole, tiled],
        out_specs=[fixed((all_rows, rank_width)), fixed((16, width))],
        out_shape=[jax.ShapeDtypeStruct((all_rows, rank_width), BF16), jax.ShapeDtypeStruct((16, width), F32)],
        scratch_shapes=[pltpu.VMEM((8, all_rows), F32)] * 3,
        compiler_params=params,
    )(slot_places, near, far, slot_labels, class_emb)

    stats_near, stats_far = gather_cls(stats)
    all_stats = jnp.concatenate([stats_near, stats_far], axis=0).reshape(-1, width)
    class_part, outbox, loss = pl.pallas_call(
        grads_kernel,
        grid=(steps,),
        in_specs=[smem, smem, smem, whole, whole, whole, tiled],
        out_specs=[tiled, fixed((blocks, width, rank_width)), fixed((1, width))],
        out_shape=[
            jax.ShapeDtypeStruct((block_width, rank_width), BF16),
            jax.ShapeDtypeStruct((blocks, width, rank_width), BF16),
            jax.ShapeDtypeStruct((1, width), F32),
        ],
        scratch_shapes=[pltpu.VMEM((8, all_rows), F32), pltpu.VMEM((rank_width, all_rows), F32)],
        compiler_params=params,
    )(slot_places, live.reshape(1), queries, all_stats, slot_labels, rows, class_emb)

    class_grad = lax.psum_scatter(class_part, "dp", scatter_dimension=0, tiled=True).astype(F32)
    columns = lax.all_to_all(column_order(features, groups), "dp", 0, 0, tiled=True)
    columns = columns.reshape(groups * width, -1)
    row_grad = scatter_cls(outbox.reshape(NK, NX, NY, width, rank_width))
    row_grads = lax.all_to_all(spread(row_grad, groups), "dp", 0, 0, tiled=True).reshape(groups * width, rank_width)
    proj_part = lax.dot_general(columns, row_grads, (((0,), (0,)), ((), ())), preferred_element_type=F32)
    share = proj_part.shape[0] // blocks
    arrived = lax.all_to_all(proj_part.reshape(blocks, share, rank_width), "cls", 0, 0, tiled=True)
    proj_grad = jnp.sum(arrived, axis=0)
    return loss.reshape(-1), class_grad, proj_grad


def solution(mesh):
    in_specs = (
        P(("cls", "dp"), None),
        P(),
        P("cls", None),
        P(None, "dp", None),
        P(None, "dp", None),
    )
    out_specs = (P(("cls", "dp")), P(("cls", "dp"), None), P(("cls", "dp"), None))
    return jax.shard_map(local, mesh=mesh, in_specs=in_specs, out_specs=out_specs, check_vma=False)
```

time: 897 us -> 234 us (0.26)
  waiting for transfers between devices: 669 us -> 83.2 us
  other arithmetic: 83.1 us -> 7.21 us
  blocking collectives: 0 us -> 41 us
  Pallas kernels: 0 us -> 26.1 us
  local copies, waits for them, and re-layouts: 32.1 us -> 10.1 us
  matrix products: 23.5 us -> 4.92 us
  loops' own time: 18.4 us -> 0 us
    all_gather x3 -> x0, waiting for transfers between devices: 291 us -> none  [merged(): everything = jax.tree.map(lambda part: lax.all_gather(part, axis), value)]
    psum x1 -> x0, waiting for transfers between devices: 279 us -> none  [local(): summed = lax.psum(proj_part, ('cls', 'dp'))]
    add x64 -> x2, other arithmetic: 52.5 us -> 0.01 us  [the longest x1 0.01 us: local(): places = ((block_ids ^ own_block) & 1) * (NX * NY) + block_ids // 2]
    all_to_all x0 -> x2, blocking collectives: none -> 41 us  [the longest x1 24.2 us: local(): lax.all_to_all(proj_part.reshape(blocks, share, rank_width), 'cls', 0, 0,...]
    pallas_call x0 -> x2, Pallas kernels: none -> 26.1 us  [the longest x1 13.5 us: local(): pl.pallas_call(grads_kernel, grid=(steps,), in_specs=[smem, smem, smem, w...]
    all_to_all x2 -> x7, waiting for transfers between devices: 97.5 us -> 78.3 us  [the longest x5 41 us: exchange(): lax.all_to_all(value, 'cls', 0, 0, axis_index_groups=groups, tiled=True)]
    dot_general x14 -> x3, matrix products: 23.5 us -> 4.92 us  [the longest x1 2.83 us: column_order(): jnp.dot(chunks, permutation, preferred_element_type=F32).astype(BF16)]
    another operation x3 -> x0, loops' own time: 18.4 us -> none  [the longest x1 8.58 us: local(): lax.fori_loop(jnp.int32(0), live_count, first_pass, start)]
  transfers between devices with their start and end apart: 7 -> 11, of which waited for: 6 -> 10; matrix products, arithmetic and copies ran while one was open for 1% -> 6% of each run, Pallas kernels for 0% -> 0%
where the time goes in v1:
time: 234 us; the launch traced here: 233 us
  waiting for transfers between devices  83.2 us (36%)
  starting transfers between devices  46.1 us (20%)
  blocking collectives  41 us (18%)
  Pallas kernels  26.1 us (11%)
  between operations  14.3 us (6%)
  local copies, waits for them, and re-layouts  10.1 us (4%)
  other arithmetic  7.21 us (3%)
  matrix products  4.92 us (2%)
    all_to_all x5, waiting for transfers between devices, exchange(): lax.all_to_all(value, 'cls', 0, 0, axis_index_groups=groups, tiled=True)  41 us
    all_to_all x1, waiting for transfers between devices, local(): lax.all_to_all(column_order(features, groups), 'dp', 0, 0, tiled=True)  29.3 us
    all_to_all x1, blocking collectives, local(): lax.all_to_all(proj_part.reshape(blocks, share, rank_width), 'cls', 0, 0,...  24.2 us
    all_to_all x5, starting transfers between devices, exchange(): lax.all_to_all(value, 'cls', 0, 0, axis_index_groups=groups, tiled=True)  18.9 us
    all_to_all x1, blocking collectives, exchange(): lax.all_to_all(value, 'cls', 0, 0, axis_index_groups=groups, tiled=True)  16.9 us
    pallas_call x1, Pallas kernels, local(): pl.pallas_call(grads_kernel, grid=(steps,), in_specs=[smem, smem, smem, w...  13.5 us
    pallas_call x1, Pallas kernels, local(): pl.pallas_call(stats_kernel, grid=(steps,), in_specs=[smem, whole, whole,...  12.6 us
    all_to_all x1, starting transfers between devices, local(): lax.all_to_all(column_order(features, groups), 'dp', 0, 0, tiled=True)  10.7 us
  transfers between devices with their start and end apart: 11, of which 10 were waited for; matrix products, arithmetic and copies ran while one was open for 6% of the time, Pallas kernels for 0%

profile of v1, /device:TPU:1, one launch (start us, length us, event | category | flops | bytes accessed | tf_op | source)
XLA Modules:
  0.0 233.0 jit_solution(1050585370562285898)
XLA Ops:
  7.2 1.2 copy-done
  8.4 1.6 convolution_convert_fusion
  10.1 16.9 %all_to_all.45 = bf16[8,128,128]{2,1,0:T(8,128)(2,1)S(1)} all-to-all(bf16[8,128,128]{2,1,0:T(8,128)(2,1)S(1)} %broadcast_in_dim.119), channel_id=1, replica_groups={{0,16,32,48,64,80,96,112},{8,24,40,56,72,88,104,120},{128,144,160,176,1..., dimensions={0} | all-to-all | bytes 524288 | tf_op jit(solution)/shard_map/all_to_all | solution.py:20
  27.0 1.3 broadcast_in_dim.120
  28.3 5.1 %all-to-all-start.1 = ((bf16[4,8,128,128]{3,2,1,0:T(8,128)(2,1)}), bf16[4,8,128,128]{3,2,1,0:T(8,128)(2,1)}, u32[]{:S(2)}, u32[]{:S(2)}) async-start(bf16[4,8,128,128]{3,2,1,0:T(8,128)(2,1)} %broadcast_in_dim.120), calls=%async_computation.1 | async-start | bytes 2097152 | tf_op jit(solution)/shard_map/all_to_all | solution.py:20
  34.0 11.5 %all-to-all-done.1 = bf16[4,8,128,128]{3,2,1,0:T(8,128)(2,1)} async-done(((bf16[4,8,128,128]{3,2,1,0:T(8,128)(2,1)}), bf16[4,8,128,128]{3,2,1,0:T(8,128)(2,1)}, u32[]{:S(2)}, u32[]{:S(2)}) %all-to-all-start.1) | async-done | bytes 1048608 | tf_op jit(solution)/shard_map/all_to_all | solution.py:20
  45.6 5.9 %collective-permute-start = (bf16[32,128,128]{2,1,0:T(8,128)(2,1)}, bf16[32,128,128]{2,1,0:T(8,128)(2,1)}, u32[]{:S(2)}, u32[]{:S(2)}) collective-permute-start(bf16[32,128,128]{2,1,0:T(8,128)(2,1)} %bitcast.2.own_ref), channel_id=1, source_target_pairs={{0,8},{8,0},{16,24},{24,16},{32,40},{40,32},{48,56},{56,48},{64,72... | collective-permute-start | bytes 3145736 | tf_op jit(solution)/shard_map/ppermute | solution.py:30
  52.8 1.2 collective-permute-done.other_ref
  54.0 12.6 %shard_map.76 = (bf16[768,128]{1,0:T(8,128)(2,1)S(1)}, f32[16,128]{1,0:T(8,128)S(1)}) custom-call(s32[6]{0:T(128)S(1)} %select_reduce_fusion.2.slots_ref, bf16[32,128,128]{2,1,0:T(8,128)(2,1)} %bitcast.2.own_ref, bf16[32,128,128]{2,1,0:T(8,128)(2,1)} %collective-permute-done.other_ref, s32[8,768]{1,0:T(8,128)S(1)} %broadcast_in_dim.127.label_ref, ...), custom_call_target="tpu_custom_call" | custom-call | tf_op jit(solution)/shard_map/pallas_call | solution.py:185
  67.2 3.4 %all-to-all-start.2 = ((f32[8,16,128]{2,1,0:T(8,128)}), f32[8,16,128]{2,1,0:T(8,128)S(1)}, u32[]{:S(2)}, u32[]{:S(2)}) async-start(f32[8,16,128]{2,1,0:T(8,128)} %broadcast_in_dim.128), calls=%async_computation.2 | async-start | bytes 131072 | tf_op jit(solution)/shard_map/all_to_all | solution.py:20
  71.0 6.7 %all-to-all-done.2 = f32[8,16,128]{2,1,0:T(8,128)S(1)} async-done(((f32[8,16,128]{2,1,0:T(8,128)}), f32[8,16,128]{2,1,0:T(8,128)S(1)}, u32[]{:S(2)}, u32[]{:S(2)}) %all-to-all-start.2) | async-done | bytes 65568 | tf_op jit(solution)/shard_map/all_to_all | solution.py:20
  78.4 3.4 %all-to-all-start.3 = ((f32[4,8,16,128]{3,2,1,0:T(8,128)}), f32[4,8,16,128]{3,2,1,0:T(8,128)S(1)}, u32[]{:S(2)}, u32[]{:S(2)}) async-start(f32[4,8,16,128]{3,2,1,0:T(8,128)} %broadcast_in_dim.129), calls=%async_computation.3 | async-start | bytes 524288 | tf_op jit(solution)/shard_map/all_to_all | solution.py:20
  81.8 5.5 %all-to-all-done.3 = f32[4,8,16,128]{3,2,1,0:T(8,128)S(1)} async-done(((f32[4,8,16,128]{3,2,1,0:T(8,128)}), f32[4,8,16,128]{3,2,1,0:T(8,128)S(1)}, u32[]{:S(2)}, u32[]{:S(2)}) %all-to-all-start.3) | async-done | bytes 262176 | tf_op jit(solution)/shard_map/all_to_all | solution.py:20
  87.3 4.7 %collective-permute-start.1 = (f32[32,16,128]{2,1,0:T(8,128)S(1)}, f32[32,16,128]{2,1,0:T(8,128)S(1)}, u32[]{:S(2)}, u32[]{:S(2)}) collective-permute-start(f32[32,16,128]{2,1,0:T(8,128)S(1)} %bitcast.46), channel_id=1, source_target_pairs={{0,8},{8,0},{16,24},{24,16},{32,40},{40,32},{48,56},{56,48},{64,72... | collective-permute-start | bytes 786440 | tf_op jit(solution)/shard_map/ppermute | solution.py:30
  93.2 13.5 %shard_map.77 = (bf16[8192,128]{1,0:T(8,128)(2,1)}, bf16[64,128,128]{2,1,0:T(8,128)(2,1)S(1)}, f32[1,128]{1,0:T(1,128)}) custom-call(s32[6]{0:T(128)S(1)} %select_reduce_fusion.2.slots_ref, s32[1]{0:T(128)} %bitcast.1.live_ref, s32[42]{0:T(128)S(1)} %reshape.225.query_ref, f32[1024,128]{1,0:T(8,128)S(1)} %bitcast.41, ...), custom_call_target="tpu_custom_call" | custom-call | tf_op jit(solution)/shard_map/pallas_call | solution.py:197
  106.8 2.5 %collective-permute-start.2 = (bf16[4,8,128,128]{3,2,1,0:T(8,128)(2,1)S(1)}, bf16[4,8,128,128]{3,2,1,0:T(8,128)(2,1)S(1)}, u32[]{:S(2)}, u32[]{:S(2)}) collective-permute-start(bf16[4,8,128,128]{3,2,1,0:T(8,128)(2,1)S(1)} %bitcast.49), channel_id=1, source_target_pairs={{0,8},{8,0},{16,24},{24,16},{32,40},{40,32},{48,56},{56,48},{64,72... | collective-permute-start | bytes 3145736 | tf_op jit(solution)/shard_map/ppermute | solution.py:34
  109.3 2.3 collective-permute-done.2
  111.5 1.4 fusion.11
  112.9 3.6 %all-to-all-start.5 = ((bf16[4,8,128,128]{3,2,1,0:T(8,128)(2,1)}), bf16[4,8,128,128]{3,2,1,0:T(8,128)(2,1)S(1)}, u32[]{:S(2)}, u32[]{:S(2)}) async-start(bf16[4,8,128,128]{3,2,1,0:T(8,128)(2,1)} %fusion.11), calls=%async_computation.6 | async-start | bytes 2097152 | tf_op jit(solution)/shard_map/all_to_all | solution.py:20
  117.3 1.5 reshape.230
  118.8 12.6 %all-to-all-done.5 = bf16[4,8,128,128]{3,2,1,0:T(8,128)(2,1)S(1)} async-done(((bf16[4,8,128,128]{3,2,1,0:T(8,128)(2,1)}), bf16[4,8,128,128]{3,2,1,0:T(8,128)(2,1)S(1)}, u32[]{:S(2)}, u32[]{:S(2)}) %all-to-all-start.5) | async-done | bytes 1048608 | tf_op jit(solution)/shard_map/all_to_all | solution.py:20
  131.4 0.9 reduce_sum.83
  132.3 3.4 %all-to-all-start.6 = ((bf16[8,128,128]{2,1,0:T(8,128)(2,1)}), bf16[8,128,128]{2,1,0:T(8,128)(2,1)S(1)}, u32[]{:S(2)}, u32[]{:S(2)}) async-start(bf16[8,128,128]{2,1,0:T(8,128)(2,1)} %reduce_sum.83), calls=%async_computation.7 | async-start | bytes 524288 | tf_op jit(solution)/shard_map/all_to_all | solution.py:20
  135.7 2.8 %fusion.28 = bf16[512,1024]{0,1:T(8,128)(2,1)S(1)} fusion(bf16[512,1024]{1,0:T(8,128)(2,1)} %reshape.230, s32[1024]{0:T(1024)S(1)} %get-tuple-element.15, s32[1024]{0:T(1024)S(1)} %get-tuple-element.18, s32[1024]{0:T(1024)S(1)} %get-tuple-element.16, s32[1024]{0:T(1024)S(1)} %get-tuple-element.17, pred[1024]{0:T(1024)(128)(4,1)S(1)} %get-tuple-element.19, ...), kind=kOutput, calls=%fused_computation.34 | convolution fusion | flops 1102577664 | bytes 2115584 | tf_op jit(solution)/shard_map/dot_general | solution.py:144
  139.4 1.7 copy.29
  141.1 4.7 %all-to-all-done.6 = bf16[8,128,128]{2,1,0:T(8,128)(2,1)S(1)} async-done(((bf16[8,128,128]{2,1,0:T(8,128)(2,1)}), bf16[8,128,128]{2,1,0:T(8,128)(2,1)S(1)}, u32[]{:S(2)}, u32[]{:S(2)}) %all-to-all-start.6) | async-done | bytes 262176 | tf_op jit(solution)/shard_map/all_to_all | solution.py:20
  145.7 10.7 %all-to-all-start.4 = ((bf16[8,128,512]{1,2,0:T(8,128)(2,1)}), bf16[8,128,512]{1,2,0:T(8,128)(2,1)S(1)}, u32[]{:S(2)}, u32[]{:S(2)}) async-start(bf16[8,128,512]{1,2,0:T(8,128)(2,1)} %bitcast.10), calls=%async_computation.5 | async-start | bytes 2097152 | tf_op jit(solution)/shard_map/all_to_all | solution.py:212
  156.5 29.3 %all-to-all-done.4 = bf16[8,128,512]{1,2,0:T(8,128)(2,1)S(1)} async-done(((bf16[8,128,512]{1,2,0:T(8,128)(2,1)}), bf16[8,128,512]{1,2,0:T(8,128)(2,1)S(1)}, u32[]{:S(2)}, u32[]{:S(2)}) %all-to-all-start.4) | async-done | bytes 1048608 | tf_op jit(solution)/shard_map/all_to_all | solution.py:212
  186.5 3.4 %all-to-all-start.7 = ((bf16[8,128,128]{2,1,0:T(8,128)(2,1)}), bf16[8,128,128]{2,1,0:T(8,128)(2,1)S(1)}, u32[]{:S(2)}, u32[]{:S(2)}) async-start(bf16[8,128,128]{2,1,0:T(8,128)(2,1)} %broadcast_in_dim.130), calls=%async_computation.8 | async-start | bytes 524288 | tf_op jit(solution)/shard_map/all_to_all | solution.py:215
  191.0 8.0 %all-to-all-done.7 = bf16[8,128,128]{2,1,0:T(8,128)(2,1)S(1)} async-done(((bf16[8,128,128]{2,1,0:T(8,128)(2,1)}), bf16[8,128,128]{2,1,0:T(8,128)(2,1)S(1)}, u32[]{:S(2)}, u32[]{:S(2)}) %all-to-all-start.7) | async-done | bytes 262176 | tf_op jit(solution)/shard_map/all_to_all | solution.py:215
  199.5 24.2 %all_to_all.46 = f32[64,8,128]{2,1,0:T(8,128)S(1)} all-to-all(f32[64,8,128]{2,1,0:T(8,128)S(1)} %fusion.31), channel_id=1, replica_groups=mesh['cls'=64,'dp'=8] {'cls'}, dimensions={0} | all-to-all | bytes 524288 | tf_op jit(solution)/shard_map/all_to_all | solution.py:218
  224.3 1.8 convert_element_type.55
  (51 shorter events, 9.5 us)
Async XLA Ops:
  7.2 1.2 copy-start
  10.0 23.3 %copy-start.4 = (s32[64,1,6]{0,1,2:T(1,128)S(1)}, s32[64,1,6]{0,1,2:T(1,128)}, u32[]{:S(2)}) copy-start(s32[64,1,6]{0,1,2:T(1,128)} %param.8) | copy-start | bytes 4612
  10.1 42.5 %copy-start.3 = (s32[64,1,128]{2,1,0:T(1,128)S(1)}, s32[64,1,128]{2,1,0:T(1,128)}, u32[]{:S(2)}) copy-start(s32[64,1,128]{2,1,0:T(1,128)} %param.9) | copy-start | bytes 98308
  10.1 43.9 %copy-start.1 = (bf16[8192,128]{1,0:T(8,128)(2,1)S(1)}, bf16[8192,128]{1,0:T(8,128)(2,1)}, u32[]{:S(2)}) copy-start(bf16[8192,128]{1,0:T(8,128)(2,1)} %emb_ref.3) | copy-start | bytes 6291460
  28.3 17.3 %all-to-all-start.1 = ((bf16[4,8,128,128]{3,2,1,0:T(8,128)(2,1)}), bf16[4,8,128,128]{3,2,1,0:T(8,128)(2,1)}, u32[]{:S(2)}, u32[]{:S(2)}) async-start(bf16[4,8,128,128]{3,2,1,0:T(8,128)(2,1)} %broadcast_in_dim.120), calls=%async_computation.1 | async-start | bytes 2097152 | tf_op jit(solution)/shard_map/all_to_all | solution.py:20
  45.6 8.5 %collective-permute-start = (bf16[32,128,128]{2,1,0:T(8,128)(2,1)}, bf16[32,128,128]{2,1,0:T(8,128)(2,1)}, u32[]{:S(2)}, u32[]{:S(2)}) collective-permute-start(bf16[32,128,128]{2,1,0:T(8,128)(2,1)} %bitcast.2.own_ref), channel_id=1, source_target_pairs={{0,8},{8,0},{16,24},{24,16},{32,40},{40,32},{48,56},{56,48},{64,72... | collective-permute-start | bytes 3145736 | tf_op jit(solution)/shard_map/ppermute | solution.py:30
  67.2 10.4 %all-to-all-start.2 = ((f32[8,16,128]{2,1,0:T(8,128)}), f32[8,16,128]{2,1,0:T(8,128)S(1)}, u32[]{:S(2)}, u32[]{:S(2)}) async-start(f32[8,16,128]{2,1,0:T(8,128)} %broadcast_in_dim.128), calls=%async_computation.2 | async-start | bytes 131072 | tf_op jit(solution)/shard_map/all_to_all | solution.py:20
  78.4 8.9 %all-to-all-start.3 = ((f32[4,8,16,128]{3,2,1,0:T(8,128)}), f32[4,8,16,128]{3,2,1,0:T(8,128)S(1)}, u32[]{:S(2)}, u32[]{:S(2)}) async-start(f32[4,8,16,128]{3,2,1,0:T(8,128)} %broadcast_in_dim.129), calls=%async_computation.3 | async-start | bytes 524288 | tf_op jit(solution)/shard_map/all_to_all | solution.py:20
  87.3 5.8 %collective-permute-start.1 = (f32[32,16,128]{2,1,0:T(8,128)S(1)}, f32[32,16,128]{2,1,0:T(8,128)S(1)}, u32[]{:S(2)}, u32[]{:S(2)}) collective-permute-start(f32[32,16,128]{2,1,0:T(8,128)S(1)} %bitcast.46), channel_id=1, source_target_pairs={{0,8},{8,0},{16,24},{24,16},{32,40},{40,32},{48,56},{56,48},{64,72... | collective-permute-start | bytes 786440 | tf_op jit(solution)/shard_map/ppermute | solution.py:30
  106.8 4.7 %collective-permute-start.2 = (bf16[4,8,128,128]{3,2,1,0:T(8,128)(2,1)S(1)}, bf16[4,8,128,128]{3,2,1,0:T(8,128)(2,1)S(1)}, u32[]{:S(2)}, u32[]{:S(2)}) collective-permute-start(bf16[4,8,128,128]{3,2,1,0:T(8,128)(2,1)S(1)} %bitcast.49), channel_id=1, source_target_pairs={{0,8},{8,0},{16,24},{24,16},{32,40},{40,32},{48,56},{56,48},{64,72... | collective-permute-start | bytes 3145736 | tf_op jit(solution)/shard_map/ppermute | solution.py:34
  112.9 4.4 %copy-start.2 = (bf16[128,4096]{1,0:T(8,128)(2,1)S(1)}, bf16[128,4096]{1,0:T(8,128)(2,1)}, u32[]{:S(2)}) copy-start(bf16[128,4096]{1,0:T(8,128)(2,1)} %param.5) | copy-start | bytes 3145732
  112.9 18.5 %all-to-all-start.5 = ((bf16[4,8,128,128]{3,2,1,0:T(8,128)(2,1)}), bf16[4,8,128,128]{3,2,1,0:T(8,128)(2,1)S(1)}, u32[]{:S(2)}, u32[]{:S(2)}) async-start(bf16[4,8,128,128]{3,2,1,0:T(8,128)(2,1)} %fusion.11), calls=%async_computation.6 | async-start | bytes 2097152 | tf_op jit(solution)/shard_map/all_to_all | solution.py:20
  116.5 107.8 %reduce-scatter.2.cloned.1.call-start = ((), (), s32[]{:S(2)}) async-start(), calls=%async_computation.10 | async-start | bytes 2359296 | tf_op jit(solution)/shard_map/reduce_scatter | solution.py:211
  132.3 13.5 %all-to-all-start.6 = ((bf16[8,128,128]{2,1,0:T(8,128)(2,1)}), bf16[8,128,128]{2,1,0:T(8,128)(2,1)S(1)}, u32[]{:S(2)}, u32[]{:S(2)}) async-start(bf16[8,128,128]{2,1,0:T(8,128)(2,1)} %reduce_sum.83), calls=%async_computation.7 | async-start | bytes 524288 | tf_op jit(solution)/shard_map/all_to_all | solution.py:20
  145.7 40.0 %all-to-all-start.4 = ((bf16[8,128,512]{1,2,0:T(8,128)(2,1)}), bf16[8,128,512]{1,2,0:T(8,128)(2,1)S(1)}, u32[]{:S(2)}, u32[]{:S(2)}) async-start(bf16[8,128,512]{1,2,0:T(8,128)(2,1)} %bitcast.10), calls=%async_computation.5 | async-start | bytes 2097152 | tf_op jit(solution)/shard_map/all_to_all | solution.py:212
  186.5 12.5 %all-to-all-start.7 = ((bf16[8,128,128]{2,1,0:T(8,128)(2,1)}), bf16[8,128,128]{2,1,0:T(8,128)(2,1)S(1)}, u32[]{:S(2)}, u32[]{:S(2)}) async-start(bf16[8,128,128]{2,1,0:T(8,128)(2,1)} %broadcast_in_dim.130), calls=%async_computation.8 | async-start | bytes 524288 | tf_op jit(solution)/shard_map/all_to_all | solution.py:215
Sparse Core Ops, SparseCore 0:
  120.2 41.0 reduce-scatter.1

commit v2 on v1

--- a/solution.py
+++ b/solution.py
@@ -25,14 +25,21 @@
 
 
 def gather_cls(block):
-    along_y = exchange(spread(block, NY), GROUP_Y)
-    own = exchange(spread(along_y, NX), GROUP_X).reshape((NX * NY,) + block.shape)
+    return gather_xk(exchange(spread(block, NY), GROUP_Y), block.shape)
+
+
+def gather_xk(along_y, shape):
+    own = exchange(spread(along_y, NX), GROUP_X).reshape((NX * NY,) + shape)
     return own, lax.ppermute(own, "cls", SWAP_K)
 
 
-def scatter_cls(outbox):
-    swapped = lax.ppermute(outbox[1], "cls", SWAP_K)
-    total = (outbox[0].astype(F32) + swapped.astype(F32)).astype(BF16)
+def swap_bit(buffer, axis, bit):
+    arrived = lax.ppermute(lax.index_in_dim(buffer, 1, axis, keepdims=False), "dp", [(z, z ^ bit) for z in range(8)])
+    return jnp.stack([lax.index_in_dim(buffer, 0, axis, keepdims=False), arrived], axis=axis)
+
+
+def scatter_cls(kept, swapped):
+    total = (kept.astype(F32) + swapped.astype(F32)).astype(BF16)
     total = jnp.sum(exchange(total, GROUP_X), axis=0, dtype=F32).astype(BF16)
     return jnp.sum(exchange(total, GROUP_Y), axis=0, dtype=F32).astype(BF16)
 
@@ -41,7 +48,7 @@
     return lax.dot_general(factors, rows, (((1,), (1,)), ((), ())), preferred_element_type=F32)
 
 
-def stats_kernel(slots_ref, own_ref, other_ref, label_ref, emb_ref, rows_ref, stat_ref, peak_ref, mass_ref, score_ref):
+def stats_kernel(slots_ref, own_ref, other_ref, target_ref, emb_ref, rows_ref, stat_ref, peak_ref, mass_ref):
     step = pl.program_id(0)
     width = rows_ref.shape[0] // LIST
 
@@ -54,17 +61,12 @@
             rows_ref[slot * width:(slot + 1) * width, :] = jnp.where(place < NX * NY, near, far)
         peak_ref[...] = jnp.full(peak_ref.shape, NEG, F32)
         mass_ref[...] = jnp.zeros(mass_ref.shape, F32)
-        score_ref[...] = jnp.zeros(score_ref.shape, F32)
 
     factors = emb_ref[...]
     tile = factors.shape[0]
-    class_ids = lax.broadcasted_iota(jnp.int32, (tile // 8, 8, 2 * width), 0) * 8 + lax.broadcasted_iota(jnp.int32, (tile // 8, 8, 2 * width), 1)
     for pair in range(LIST // 2):
         cut = slice(pair * 2 * width, (pair + 1) * 2 * width)
         scores = scores_of(factors, rows_ref[cut, :]).reshape(tile // 8, 8, 2 * width)
-        local_label = label_ref[0:1, cut] - step * tile
-        hit = class_ids == local_label[None]
-        score_ref[:, cut] += jnp.sum(jnp.where(hit, scores, 0.0), axis=0)
         old = peak_ref[:, cut]
         new = jnp.maximum(old, jnp.max(scores, axis=0))
         mass_ref[:, cut] = mass_ref[:, cut] * jnp.exp(old - new) + jnp.sum(jnp.exp(scores - new[None]), axis=0)
@@ -75,14 +77,30 @@
         peak = jnp.max(peak_ref[...], axis=0, keepdims=True)
         mass = jnp.sum(mass_ref[...] * jnp.exp(peak_ref[...] - peak), axis=0, keepdims=True)
         norm = peak + jnp.log(mass)
-        score = jnp.sum(score_ref[...], axis=0, keepdims=True)
+        products = rows_ref[...].astype(F32) * target_ref[...].astype(F32)
+        ones = jnp.ones((8, products.shape[1]), F32)
+        score = lax.dot_general(ones, products, (((1,), (1,)), ((), ())), precision=lax.Precision.HIGHEST, preferred_element_type=F32)
         stat_ref[...] = jnp.zeros(stat_ref.shape, F32)
         for slot in range(LIST):
             stat_ref[slot:slot + 1, :] = norm[:, slot * width:(slot + 1) * width]
-            stat_ref[8 + slot:9 + slot, :] = score[:, slot * width:(slot + 1) * width]
-
-
-def grads_kernel(slots_ref, live_ref, query_ref, stat_ref, label_ref, rows_ref, emb_ref, part_ref, back_ref, loss_ref, norm_ref, total_ref):
+            stat_ref[8 + slot:9 + slot, :] = score[0:1, slot * width:(slot + 1) * width]
+
+
+def weights_of(step, factors, rows, norm_ref, label_ref):
+    scores = scores_of(factors, rows)
+    probs = jnp.exp(scores - norm_ref[0:1, :])
+    class_ids = lax.broadcasted_iota(jnp.int32, scores.shape, 0)
+    hit = class_ids == label_ref[0:1, :] - step * factors.shape[0]
+    return jnp.where(hit, probs - 1.0, probs).astype(BF16)
+
+
+def part_kernel(norm_ref, label_ref, rows_ref, emb_ref, part_ref):
+    rows = rows_ref[...]
+    weights = weights_of(pl.program_id(0), emb_ref[...], rows, norm_ref, label_ref)
+    part_ref[...] = jnp.dot(weights, rows, preferred_element_type=F32).astype(BF16)
+
+
+def back_kernel(slots_ref, live_ref, query_ref, stat_ref, label_ref, rows_ref, emb_ref, back_ref, loss_ref, norm_ref, total_ref):
     step = pl.program_id(0)
     width = rows_ref.shape[0] // LIST
 
@@ -114,14 +132,7 @@
         back_ref[...] = jnp.zeros(back_ref.shape, BF16)
 
     factors = emb_ref[...]
-    tile = factors.shape[0]
-    rows = rows_ref[...]
-    scores = scores_of(factors, rows)
-    probs = jnp.exp(scores - norm_ref[0:1, :])
-    class_ids = lax.broadcasted_iota(jnp.int32, scores.shape, 0)
-    hit = class_ids == label_ref[0:1, :] - step * tile
-    weights = jnp.where(hit, probs - 1.0, probs).astype(BF16)
-    part_ref[...] = jnp.dot(weights, rows, preferred_element_type=F32).astype(BF16)
+    weights = weights_of(step, factors, rows_ref[...], norm_ref, label_ref)
     total_ref[...] += lax.dot_general(factors, weights, (((0,), (0,)), ((), ())), preferred_element_type=F32)
 
     @pl.when(step == pl.num_programs(0) - 1)
@@ -132,12 +143,12 @@
                 back_ref[slots_ref[slot]] = total_ref[:, slot * width:(slot + 1) * width].T.astype(BF16)
 
 
-def column_order(features, parts):
+def column_order(features, parts, own):
     rows, depth = features.shape
     span = parts * 128
     source = lax.broadcasted_iota(jnp.int32, (span, span), 0)
     target = lax.broadcasted_iota(jnp.int32, (span, span), 1)
-    group, rest = target // 128, target % 128
+    group, rest = (target // 128) ^ own, target % 128
     wanted = (rest // 8) * (8 * parts) + group * 8 + rest % 8
     permutation = (source == wanted).astype(BF16)
     chunks = features.reshape(rows * (depth // span), span)
@@ -153,7 +164,13 @@
     width = features.shape[0]
     block_width, rank_width = class_emb.shape
     hidden = jnp.dot(features, proj, preferred_element_type=F32).astype(BF16)
-    near, far = gather_cls(hidden)
+    own_group = lax.axis_index("dp")
+    along_y = exchange(spread(hidden, NY), GROUP_Y)
+    late_features, along_y = lax.optimization_barrier((features, along_y))
+    columns = column_order(late_features, groups, own_group).reshape(2, 2, 2, width, -1)
+    near, far = gather_xk(along_y, hidden.shape)
+    columns, far = lax.optimization_barrier((columns, far))
+    columns = swap_bit(columns, 0, 4)
 
     table = lists[:, 0, :]
     group_labels = labels[:, 0, :]
@@ -173,7 +190,11 @@
     queries = jnp.sum(jnp.where(asked[:, :, None], entry_place[None], 0), axis=1).reshape(-1)
     slot_labels = jnp.sum(jnp.where(chosen[:, :, None], group_labels[None], 0), axis=1)
     slot_labels = jnp.where(slot_ids[:, None] < live, slot_labels - own_block * block_width, -1)
-    slot_labels = spread(slot_labels.reshape(-1), 8)
+    slot_labels = slot_labels.reshape(-1)
+    inside = (slot_labels >= 0) & (slot_labels < block_width)
+    targets = jnp.take(class_emb, jnp.clip(slot_labels, 0, block_width - 1), axis=0, mode="clip")
+    targets = jnp.where(inside[:, None], targets, jnp.zeros((), BF16))
+    slot_labels = spread(slot_labels, 8)
 
     steps = block_width // TILE
     all_rows = LIST * width
@@ -188,30 +209,45 @@
         in_specs=[smem, whole, whole, whole, tiled],
         out_specs=[fixed((all_rows, rank_width)), fixed((16, width))],
         out_shape=[jax.ShapeDtypeStruct((all_rows, rank_width), BF16), jax.ShapeDtypeStruct((16, width), F32)],
-        scratch_shapes=[pltpu.VMEM((8, all_rows), F32)] * 3,
+        scratch_shapes=[pltpu.VMEM((8, all_rows), F32)] * 2,
         compiler_params=params,
-    )(slot_places, near, far, slot_labels, class_emb)
-
+    )(slot_places, near, far, targets, class_emb)
+
+    columns, stats = lax.optimization_barrier((columns, stats))
+    columns = swap_bit(columns, 1, 2)
     stats_near, stats_far = gather_cls(stats)
+    columns, stats_far = lax.optimization_barrier((columns, stats_far))
     all_stats = jnp.concatenate([stats_near, stats_far], axis=0).reshape(-1, width)
-    class_part, outbox, loss = pl.pallas_call(
-        grads_kernel,
+    outbox, loss, norms = pl.pallas_call(
+        back_kernel,
         grid=(steps,),
         in_specs=[smem, smem, smem, whole, whole, whole, tiled],
-        out_specs=[tiled, fixed((blocks, width, rank_width)), fixed((1, width))],
+        out_specs=[fixed((blocks, width, rank_width)), fixed((1, width)), fixed((8, all_rows))],
         out_shape=[
-            jax.ShapeDtypeStruct((block_width, rank_width), BF16),
             jax.ShapeDtypeStruct((blocks, width, rank_width), BF16),
             jax.ShapeDtypeStruct((1, width), F32),
+            jax.ShapeDtypeStruct((8, all_rows), F32),
         ],
-        scratch_shapes=[pltpu.VMEM((8, all_rows), F32), pltpu.VMEM((rank_width, all_rows), F32)],
+        scratch_shapes=[pltpu.VMEM((rank_width, all_rows), F32)],
         compiler_params=params,
     )(slot_places, live.reshape(1), queries, all_stats, slot_labels, rows, class_emb)
 
+    outbox = outbox.reshape(NK, NX, NY, width, rank_width)
+    swapped, columns, rows = lax.optimization_barrier((lax.ppermute(outbox[1], "cls", SWAP_K), columns, rows))
+    columns = swap_bit(columns, 2, 1)
+    class_part = pl.pallas_call(
+        part_kernel,
+        grid=(steps,),
+        in_specs=[whole, whole, whole, tiled],
+        out_specs=tiled,
+        out_shape=jax.ShapeDtypeStruct((block_width, rank_width), BF16),
+        compiler_params=params,
+    )(norms, slot_labels, rows, class_emb)
     class_grad = lax.psum_scatter(class_part, "dp", scatter_dimension=0, tiled=True).astype(F32)
-    columns = lax.all_to_all(column_order(features, groups), "dp", 0, 0, tiled=True)
-    columns = columns.reshape(groups * width, -1)
-    row_grad = scatter_cls(outbox.reshape(NK, NX, NY, width, rank_width))
+    row_grad = scatter_cls(outbox[0], swapped)
+    columns, row_grad = lax.optimization_barrier((columns, row_grad))
+    columns = columns.reshape(groups, width, -1)
+    columns = jnp.take(columns, jnp.arange(groups, dtype=jnp.int32) ^ own_group, axis=0, mode="clip").reshape(groups * width, -1)
     row_grads = lax.all_to_all(spread(row_grad, groups), "dp", 0, 0, tiled=True).reshape(groups * width, rank_width)
     proj_part = lax.dot_general(columns, row_grads, (((0,), (0,)), ((), ())), preferred_element_type=F32)
     share = proj_part.shape[0] // blocks

time: 234 us -> 249 us (1.064)
  starting transfers between devices: 46.1 us -> 77.5 us
  waiting for transfers between devices: 83.2 us -> 60.6 us
  blocking collectives: 41 us -> 20.3 us
  local copies, waits for them, and re-layouts: 10.1 us -> 25.7 us
  other arithmetic: 7.21 us -> 14.2 us
  Pallas kernels: 26.1 us -> 30.3 us
    all_to_all x1 -> x0, waiting for transfers between devices: 29.3 us -> none  [local(): lax.all_to_all(column_order(features, groups), 'dp', 0, 0, tiled=True)]
    ppermute x3 -> x6, starting transfers between devices: 13 us -> 40.8 us  [the longest x3 28 us: swap_bit(): lax.ppermute(lax.index_in_dim(buffer, 1, axis, keepdims=False), 'dp', [(z...]
    all_to_all x1 -> x0, blocking collectives: 16.9 us -> none  [exchange(): lax.all_to_all(value, 'cls', 0, 0, axis_index_groups=groups, tiled=True)]
    all_to_all x5 -> x6, starting transfers between devices: 18.9 us -> 30.6 us  [exchange(): lax.all_to_all(value, 'cls', 0, 0, axis_index_groups=groups, tiled=True)]
    all_to_all x1 -> x0, starting transfers between devices: 10.7 us -> none  [local(): lax.all_to_all(column_order(features, groups), 'dp', 0, 0, tiled=True)]
    ppermute x3 -> x6, waiting for transfers between devices: 4.27 us -> 13.3 us  [the longest x3 11 us: swap_bit(): lax.ppermute(lax.index_in_dim(buffer, 1, axis, keepdims=False), 'dp', [(z...]
    pallas_call x1 -> x2, Pallas kernels: 13.5 us -> 20.3 us  [the longest x1 11.6 us: local(): pl.pallas_call(back_kernel, grid=(steps,), in_specs=[smem, smem, smem, wh...]
    unnamed x12 -> x18, local copies, waits for them, and re-layouts: 1.52 us -> 6.01 us
  transfers between devices with their start and end apart: 11 -> 14, of which waited for: 10 -> 10; matrix products, arithmetic and copies ran while one was open for 6% -> 12% of each run, Pallas kernels for 0% -> 4%
where the time goes in v2:
time: 249 us; the launch traced here: 248 us
  starting transfers between devices  77.5 us (31%)
  waiting for transfers between devices  60.6 us (24%)
  Pallas kernels  30.3 us (12%)
  local copies, waits for them, and re-layouts  25.7 us (10%)
  blocking collectives  20.3 us (8%)
  between operations  14.4 us (6%)
  other arithmetic  14.2 us (6%)
  matrix products  4.93 us (2%)
    all_to_all x6, waiting for transfers between devices, exchange(): lax.all_to_all(value, 'cls', 0, 0, axis_index_groups=groups, tiled=True)  39.7 us
    all_to_all x6, starting transfers between devices, exchange(): lax.all_to_all(value, 'cls', 0, 0, axis_index_groups=groups, tiled=True)  30.6 us
    ppermute x3, starting transfers between devices, swap_bit(): lax.ppermute(lax.index_in_dim(buffer, 1, axis, keepdims=False), 'dp', [(z...  28 us
    all_to_all x1, blocking collectives, local(): lax.all_to_all(proj_part.reshape(blocks, share, rank_width), 'cls', 0, 0,...  20.3 us
    pallas_call x1, Pallas kernels, local(): pl.pallas_call(back_kernel, grid=(steps,), in_specs=[smem, smem, smem, wh...  11.6 us
    ppermute x3, waiting for transfers between devices, swap_bit(): lax.ppermute(lax.index_in_dim(buffer, 1, axis, keepdims=False), 'dp', [(z...  11 us
    pallas_call x1, Pallas kernels, local(): pl.pallas_call(stats_kernel, grid=(steps,), in_specs=[smem, whole, whole,...  9.97 us
    ppermute x2, starting transfers between devices, gather_xk(): return (own, lax.ppermute(own, 'cls', SWAP_K))  9.84 us
  transfers between devices with their start and end apart: 14, of which 10 were waited for; matrix products, arithmetic and copies ran while one was open for 12% of the time, Pallas kernels for 4%

profile of v2, /device:TPU:1, one launch (start us, length us, event | category | flops | bytes accessed | tf_op | source)
XLA Modules:
  0.0 247.9 jit_solution(15442069023606051573)
XLA Ops:
  10.8 7.8 %all-to-all-start = ((bf16[8,128,128]{2,1,0:T(8,128)(2,1)}), bf16[8,128,128]{2,1,0:T(8,128)(2,1)S(1)}, u32[]{:S(2)}, u32[]{:S(2)}) async-start(bf16[8,128,128]{2,1,0:T(8,128)(2,1)} %broadcast_in_dim.136), calls=%async_computation | async-start | bytes 524288 | tf_op jit(solution)/shard_map/all_to_all | solution.py:20
  20.4 7.5 %all-to-all-done = bf16[8,128,128]{2,1,0:T(8,128)(2,1)S(1)} async-done(((bf16[8,128,128]{2,1,0:T(8,128)(2,1)}), bf16[8,128,128]{2,1,0:T(8,128)(2,1)S(1)}, u32[]{:S(2)}, u32[]{:S(2)}) %all-to-all-start) | async-done | bytes 262176 | tf_op jit(solution)/shard_map/all_to_all | solution.py:20
  29.2 5.0 %all-to-all-start.1 = ((bf16[4,8,128,128]{3,2,1,0:T(8,128)(2,1)}), bf16[4,8,128,128]{3,2,1,0:T(8,128)(2,1)}, u32[]{:S(2)}, u32[]{:S(2)}) async-start(bf16[4,8,128,128]{3,2,1,0:T(8,128)(2,1)} %broadcast_in_dim.137), calls=%async_computation.1 | async-start | bytes 2097152 | tf_op jit(solution)/shard_map/all_to_all | solution.py:20
  34.2 1.9 gather_fusion
  36.5 2.5 %reshape.275 = bf16[512,1024]{1,0:T(8,128)(2,1)} reshape(bf16[128,4096]{1,0:T(8,128)(2,1)} %param.5) | data formatting | bytes 2097152 | tf_op jit(solution)/shard_map/reshape | solution.py:154
  39.0 7.3 %all-to-all-done.1 = bf16[4,8,128,128]{3,2,1,0:T(8,128)(2,1)} async-done(((bf16[4,8,128,128]{3,2,1,0:T(8,128)(2,1)}), bf16[4,8,128,128]{3,2,1,0:T(8,128)(2,1)}, u32[]{:S(2)}, u32[]{:S(2)}) %all-to-all-start.1) | async-done | bytes 1048608 | tf_op jit(solution)/shard_map/all_to_all | solution.py:20
  46.3 6.0 %collective-permute-start = (bf16[32,128,128]{2,1,0:T(8,128)(2,1)}, bf16[32,128,128]{2,1,0:T(8,128)(2,1)}, u32[]{:S(2)}, u32[]{:S(2)}) collective-permute-start(bf16[32,128,128]{2,1,0:T(8,128)(2,1)} %bitcast.4.own_ref), channel_id=1, source_target_pairs={{0,8},{8,0},{16,24},{24,16},{32,40},{40,32},{48,56},{56,48},{64,72... | collective-permute-start | bytes 3145736 | tf_op jit(solution)/shard_map/ppermute | solution.py:33
  52.3 2.9 %fusion.28 = bf16[64,8,8,128]{3,1,2,0:T(8,128)(2,1)S(1)} fusion(bf16[512,1024]{1,0:T(8,128)(2,1)} %reshape.275, s32[]{:T(128)S(6)} %axis_index.25, s32[1024]{0:T(1024)S(1)} %get-tuple-element.45, s32[1024]{0:T(1024)S(1)} %get-tuple-element.48, s32[1024]{0:T(1024)S(1)} %get-tuple-element.46, s32[1024]{0:T(1024)S(1)} %get-tuple-element.47, ...), kind=kOutput, calls=%fused_computation.36 | convolution fusion | flops 1102577664 | bytes 2115588 | tf_op jit(solution)/shard_map/dot_general | solution.py:155
  56.4 2.7 %copy.25 = bf16[128,4,8,128]{0,3,1,2:T(8,128)(2,1)} copy(bf16[128,4,8,128]{3,2,1,0:T(8,128)(2,1)} %bitcast.60) | data formatting | bytes 2097152 | tf_op jit(solution)/shard_map/reshape | solution.py:156
  60.4 10.8 %collective-permute-start.1 = (bf16[2,2,128,512]{2,3,1,0:T(8,128)(2,1)S(1)}, bf16[2,2,128,512]{2,3,1,0:T(8,128)(2,1)S(1)}, u32[]{:S(2)}, u32[]{:S(2)}) collective-permute-start(bf16[2,2,128,512]{2,3,1,0:T(8,128)(2,1)S(1)} %get-tuple-element.44), channel_id=1, source_target_pairs={{0,4},{1,5},{2,6},{3,7},{4,0},{5,1},{6,2},{7,3},{8,12},{9,13},{10,... | collective-permute-start | bytes 1572872 | tf_op jit(solution)/shard_map/ppermute | solution.py:37
  71.6 10.0 %shard_map.76 = (bf16[768,128]{1,0:T(8,128)(2,1)S(1)}, f32[16,128]{1,0:T(8,128)S(1)}) custom-call(s32[6]{0:T(128)S(1)} %select_reduce_fusion.2.slots_ref, bf16[32,128,128]{2,1,0:T(8,128)(2,1)} %bitcast.4.own_ref, bf16[32,128,128]{2,1,0:T(8,128)(2,1)} %collective-permute-done.other_ref, bf16[768,128]{1,0:T(8,128)(2,1)S(1)} %broadcast_select_fusion.target_ref, ...), custom_call_target="tpu_custom_call" | custom-call | tf_op jit(solution)/shard_map/pallas_call | solution.py:206
  81.5 2.0 collective-permute-done.1
  85.3 3.3 %all-to-all-start.2 = ((f32[8,16,128]{2,1,0:T(8,128)}), f32[8,16,128]{2,1,0:T(8,128)S(1)}, u32[]{:S(2)}, u32[]{:S(2)}) async-start(f32[8,16,128]{2,1,0:T(8,128)} %broadcast_in_dim.146), calls=%async_computation.2 | async-start | bytes 131072 | tf_op jit(solution)/shard_map/all_to_all | solution.py:20
  90.5 15.3 %collective-permute-start.2 = (bf16[2,2,128,512]{2,3,1,0:T(8,128)(2,1)}, bf16[2,2,128,512]{2,3,1,0:T(8,128)(2,1)}, u32[]{:S(2)}, u32[]{:S(2)}) collective-permute-start(bf16[2,2,128,512]{2,3,1,0:T(8,128)(2,1)} %slice_bitcast_fusion.1), channel_id=1, source_target_pairs={{0,2},{1,3},{2,0},{3,1},{4,6},{5,7},{6,4},{7,5},{8,10},{9,11},{10,... | collective-permute-start | bytes 1572872 | tf_op jit(solution)/shard_map/ppermute | solution.py:37
  106.5 4.0 %all-to-all-start.3 = ((f32[4,8,16,128]{3,2,1,0:T(8,128)}), f32[4,8,16,128]{3,2,1,0:T(8,128)}, u32[]{:S(2)}, u32[]{:S(2)}) async-start(f32[4,8,16,128]{3,2,1,0:T(8,128)} %broadcast_in_dim.147), calls=%async_computation.3 | async-start | bytes 524288 | tf_op jit(solution)/shard_map/all_to_all | solution.py:20
  110.6 5.6 %all-to-all-done.3 = f32[4,8,16,128]{3,2,1,0:T(8,128)} async-done(((f32[4,8,16,128]{3,2,1,0:T(8,128)}), f32[4,8,16,128]{3,2,1,0:T(8,128)}, u32[]{:S(2)}, u32[]{:S(2)}) %all-to-all-start.3) | async-done | bytes 262176 | tf_op jit(solution)/shard_map/all_to_all | solution.py:20
  116.3 3.9 %collective-permute-start.3 = (f32[32,16,128]{2,1,0:T(8,128)}, f32[32,16,128]{2,1,0:T(8,128)}, u32[]{:S(2)}, u32[]{:S(2)}) collective-permute-start(f32[32,16,128]{2,1,0:T(8,128)} %bitcast.10), channel_id=1, source_target_pairs={{0,8},{8,0},{16,24},{24,16},{32,40},{40,32},{48,56},{56,48},{64,72... | collective-permute-start | bytes 786440 | tf_op jit(solution)/shard_map/ppermute | solution.py:33
  121.9 7.3 %collective-permute-done.2 = bf16[2,2,128,512]{2,3,1,0:T(8,128)(2,1)} collective-permute-done((bf16[2,2,128,512]{2,3,1,0:T(8,128)(2,1)}, bf16[2,2,128,512]{2,3,1,0:T(8,128)(2,1)}, u32[]{:S(2)}, u32[]{:S(2)}) %collective-permute-start.2) | collective-permute-done | bytes 524320 | tf_op jit(solution)/shard_map/ppermute | solution.py:37
  129.2 2.1 pad_maximum_fusion.1
  132.4 11.6 %shard_map.77 = (bf16[64,128,128]{2,1,0:T(8,128)(2,1)S(1)}, f32[1,128]{1,0:T(1,128)}, f32[8,768]{1,0:T(8,128)S(1)}) custom-call(s32[6]{0:T(128)S(1)} %select_reduce_fusion.2.slots_ref, s32[1]{0:T(128)} %bitcast.1.live_ref, s32[42]{0:T(128)S(1)} %reshape.274.query_ref, f32[1024,128]{1,0:T(8,128)S(1)} %bitcast.55, s32[8,768]{1,0:T(8,128)S(1)} %broadcast_in_dim.148.label_ref, ...), custom_call_target="tpu_custom_call" | custom-call | tf_op jit(solution)/shard_map/pallas_call | solution.py:221
  145.1 2.9 %collective-permute-start.4 = (bf16[4,8,128,128]{3,2,1,0:T(8,128)(2,1)S(1)}, bf16[4,8,128,128]{3,2,1,0:T(8,128)(2,1)S(1)}, u32[]{:S(2)}, u32[]{:S(2)}) collective-permute-start(bf16[4,8,128,128]{3,2,1,0:T(8,128)(2,1)S(1)} %bitcast.62), channel_id=1, source_target_pairs={{0,8},{8,0},{16,24},{24,16},{32,40},{40,32},{48,56},{56,48},{64,72... | collective-permute-start | bytes 3145736 | tf_op jit(solution)/shard_map/ppermute | solution.py:236
  148.0 2.3 collective-permute-done.4
  151.3 8.8 %shard_map.78 = bf16[8192,128]{1,0:T(8,128)(2,1)S(1)} custom-call(f32[8,768]{1,0:T(8,128)S(1)} %get-tuple-element.31.norm_ref, s32[8,768]{1,0:T(8,128)S(1)} %broadcast_in_dim.148.label_ref, bf16[768,128]{1,0:T(8,128)(2,1)S(1)} %get-tuple-element.34.rows_ref, bf16[8192,128]{1,0:T(8,128)(2,1)S(1)} %copy-done.1), custom_call_target="tpu_custom_call" | custom-call | tf_op jit(solution)/shard_map/pallas_call | solution.py:238
  162.6 2.7 %fusion.10 = bf16[4,8,128,128]{3,2,1,0:T(8,128)(2,1)} fusion(bf16[4,8,128,128]{3,2,1,0:T(8,128)(2,1)S(1)} %bitcast.58, bf16[4,8,128,128]{3,2,1,0:T(8,128)(2,1)} %copy-done.5), kind=kLoop, calls=%fused_computation.20 | loop fusion | flops 2097152 | bytes 3145728 | tf_op jit(solution)/shard_map/convert_element_type | solution.py:42
  165.4 3.5 %all-to-all-start.4 = ((bf16[4,8,128,128]{3,2,1,0:T(8,128)(2,1)}), bf16[4,8,128,128]{3,2,1,0:T(8,128)(2,1)S(1)}, u32[]{:S(2)}, u32[]{:S(2)}) async-start(bf16[4,8,128,128]{3,2,1,0:T(8,128)(2,1)} %fusion.10), calls=%async_computation.5 | async-start | bytes 2097152 | tf_op jit(solution)/shard_map/all_to_all | solution.py:20
  169.7 1.9 collective-permute-start.5
  171.7 12.1 %all-to-all-done.4 = bf16[4,8,128,128]{3,2,1,0:T(8,128)(2,1)S(1)} async-done(((bf16[4,8,128,128]{3,2,1,0:T(8,128)(2,1)}), bf16[4,8,128,128]{3,2,1,0:T(8,128)(2,1)S(1)}, u32[]{:S(2)}, u32[]{:S(2)}) %all-to-all-start.4) | async-done | bytes 1048608 | tf_op jit(solution)/shard_map/all_to_all | solution.py:20
  184.6 6.9 %all-to-all-start.5 = ((bf16[8,128,128]{2,1,0:T(8,128)(2,1)}), bf16[8,128,128]{2,1,0:T(8,128)(2,1)S(1)}, u32[]{:S(2)}, u32[]{:S(2)}) async-start(bf16[8,128,128]{2,1,0:T(8,128)(2,1)} %reduce_sum.83), calls=%async_computation.6 | async-start | bytes 524288 | tf_op jit(solution)/shard_map/all_to_all | solution.py:20
  194.6 7.2 %all-to-all-done.5 = bf16[8,128,128]{2,1,0:T(8,128)(2,1)S(1)} async-done(((bf16[8,128,128]{2,1,0:T(8,128)(2,1)}), bf16[8,128,128]{2,1,0:T(8,128)(2,1)S(1)}, u32[]{:S(2)}, u32[]{:S(2)}) %all-to-all-start.5) | async-done | bytes 262176 | tf_op jit(solution)/shard_map/all_to_all | solution.py:20
  202.5 6.0 %all-to-all-start.6 = ((bf16[8,128,128]{2,1,0:T(8,128)(2,1)}), bf16[8,128,128]{2,1,0:T(8,128)(2,1)S(1)}, u32[]{:S(2)}, u32[]{:S(2)}) async-start(bf16[8,128,128]{2,1,0:T(8,128)(2,1)} %broadcast_in_dim.149), calls=%async_computation.7 | async-start | bytes 524288 | tf_op jit(solution)/shard_map/all_to_all | solution.py:251
  210.2 7.7 %all-to-all-done.6 = bf16[8,128,128]{2,1,0:T(8,128)(2,1)S(1)} async-done(((bf16[8,128,128]{2,1,0:T(8,128)(2,1)}), bf16[8,128,128]{2,1,0:T(8,128)(2,1)S(1)}, u32[]{:S(2)}, u32[]{:S(2)}) %all-to-all-start.6) | async-done | bytes 262176 | tf_op jit(solution)/shard_map/all_to_all | solution.py:251
  218.4 20.3 %all_to_all.40 = f32[64,8,128]{2,1,0:T(8,128)S(1)} all-to-all(f32[64,8,128]{2,1,0:T(8,128)S(1)} %fusion.31), channel_id=1, replica_groups=mesh['cls'=64,'dp'=8] {'cls'}, dimensions={0} | all-to-all | bytes 524288 | tf_op jit(solution)/shard_map/all_to_all | solution.py:254
  (79 shorter events, 31.9 us)
Async XLA Ops:
  7.2 1.2 copy-start
  7.2 11.4 %copy-start.7 = (s32[64,1,6]{0,1,2:T(1,128)S(1)}, s32[64,1,6]{0,1,2:T(1,128)}, u32[]{:S(2)}) copy-start(s32[64,1,6]{0,1,2:T(1,128)} %param.8) | copy-start | bytes 4612
  7.2 13.0 %copy-start.6 = (s32[64,1,128]{2,1,0:T(1,128)S(1)}, s32[64,1,128]{2,1,0:T(1,128)}, u32[]{:S(2)}) copy-start(s32[64,1,128]{2,1,0:T(1,128)} %param.9) | copy-start | bytes 98308
  10.8 23.4 %copy-start.1 = (bf16[8192,128]{1,0:T(8,128)(2,1)S(1)}, bf16[8192,128]{1,0:T(8,128)(2,1)}, u32[]{:S(2)}) copy-start(bf16[8192,128]{1,0:T(8,128)(2,1)} %emb_ref.5) | copy-start | bytes 6291460
  10.8 17.2 %all-to-all-start = ((bf16[8,128,128]{2,1,0:T(8,128)(2,1)}), bf16[8,128,128]{2,1,0:T(8,128)(2,1)S(1)}, u32[]{:S(2)}, u32[]{:S(2)}) async-start(bf16[8,128,128]{2,1,0:T(8,128)(2,1)} %broadcast_in_dim.136), calls=%async_computation | async-start | bytes 524288 | tf_op jit(solution)/shard_map/all_to_all | solution.py:20
  29.2 17.1 %all-to-all-start.1 = ((bf16[4,8,128,128]{3,2,1,0:T(8,128)(2,1)}), bf16[4,8,128,128]{3,2,1,0:T(8,128)(2,1)}, u32[]{:S(2)}, u32[]{:S(2)}) async-start(bf16[4,8,128,128]{3,2,1,0:T(8,128)(2,1)} %broadcast_in_dim.137), calls=%async_computation.1 | async-start | bytes 2097152 | tf_op jit(solution)/shard_map/all_to_all | solution.py:20
  46.3 12.8 %collective-permute-start = (bf16[32,128,128]{2,1,0:T(8,128)(2,1)}, bf16[32,128,128]{2,1,0:T(8,128)(2,1)}, u32[]{:S(2)}, u32[]{:S(2)}) collective-permute-start(bf16[32,128,128]{2,1,0:T(8,128)(2,1)} %bitcast.4.own_ref), channel_id=1, source_target_pairs={{0,8},{8,0},{16,24},{24,16},{32,40},{40,32},{48,56},{56,48},{64,72... | collective-permute-start | bytes 3145736 | tf_op jit(solution)/shard_map/ppermute | solution.py:33
  60.4 23.2 %collective-permute-start.1 = (bf16[2,2,128,512]{2,3,1,0:T(8,128)(2,1)S(1)}, bf16[2,2,128,512]{2,3,1,0:T(8,128)(2,1)S(1)}, u32[]{:S(2)}, u32[]{:S(2)}) collective-permute-start(bf16[2,2,128,512]{2,3,1,0:T(8,128)(2,1)S(1)} %get-tuple-element.44), channel_id=1, source_target_pairs={{0,4},{1,5},{2,6},{3,7},{4,0},{5,1},{6,2},{7,3},{8,12},{9,13},{10,... | collective-permute-start | bytes 1572872 | tf_op jit(solution)/shard_map/ppermute | solution.py:37
  85.3 20.5 %all-to-all-start.2 = ((f32[8,16,128]{2,1,0:T(8,128)}), f32[8,16,128]{2,1,0:T(8,128)S(1)}, u32[]{:S(2)}, u32[]{:S(2)}) async-start(f32[8,16,128]{2,1,0:T(8,128)} %broadcast_in_dim.146), calls=%async_computation.2 | async-start | bytes 131072 | tf_op jit(solution)/shard_map/all_to_all | solution.py:20
  90.5 38.7 %collective-permute-start.2 = (bf16[2,2,128,512]{2,3,1,0:T(8,128)(2,1)}, bf16[2,2,128,512]{2,3,1,0:T(8,128)(2,1)}, u32[]{:S(2)}, u32[]{:S(2)}) collective-permute-start(bf16[2,2,128,512]{2,3,1,0:T(8,128)(2,1)} %slice_bitcast_fusion.1), channel_id=1, source_target_pairs={{0,2},{1,3},{2,0},{3,1},{4,6},{5,7},{6,4},{7,5},{8,10},{9,11},{10,... | collective-permute-start | bytes 1572872 | tf_op jit(solution)/shard_map/ppermute | solution.py:37
  106.5 9.7 %all-to-all-start.3 = ((f32[4,8,16,128]{3,2,1,0:T(8,128)}), f32[4,8,16,128]{3,2,1,0:T(8,128)}, u32[]{:S(2)}, u32[]{:S(2)}) async-start(f32[4,8,16,128]{3,2,1,0:T(8,128)} %broadcast_in_dim.147), calls=%async_computation.3 | async-start | bytes 524288 | tf_op jit(solution)/shard_map/all_to_all | solution.py:20
  110.6 128.7 %reduce-scatter.2.cloned.1.call-start = ((), (), s32[]{:S(2)}) async-start(), calls=%async_computation.9 | async-start | bytes 2359296 | tf_op jit(solution)/shard_map/reduce_scatter | solution.py:246
  116.3 15.0 %collective-permute-start.3 = (f32[32,16,128]{2,1,0:T(8,128)}, f32[32,16,128]{2,1,0:T(8,128)}, u32[]{:S(2)}, u32[]{:S(2)}) collective-permute-start(f32[32,16,128]{2,1,0:T(8,128)} %bitcast.10), channel_id=1, source_target_pairs={{0,8},{8,0},{16,24},{24,16},{32,40},{40,32},{48,56},{56,48},{64,72... | collective-permute-start | bytes 786440 | tf_op jit(solution)/shard_map/ppermute | solution.py:33
  145.1 5.2 %collective-permute-start.4 = (bf16[4,8,128,128]{3,2,1,0:T(8,128)(2,1)S(1)}, bf16[4,8,128,128]{3,2,1,0:T(8,128)(2,1)S(1)}, u32[]{:S(2)}, u32[]{:S(2)}) collective-permute-start(bf16[4,8,128,128]{3,2,1,0:T(8,128)(2,1)S(1)} %bitcast.62), channel_id=1, source_target_pairs={{0,8},{8,0},{16,24},{24,16},{32,40},{40,32},{48,56},{56,48},{64,72... | collective-permute-start | bytes 3145736 | tf_op jit(solution)/shard_map/ppermute | solution.py:236
  150.3 1.0 copy-start.5
  160.1 1.3 copy-start.2
  161.4 1.2 copy-start.4
  162.6 6.3 %copy-start.3 = (bf16[2,2,2,128,512]{3,4,2,0,1:T(8,128)(2,1)S(1)}, bf16[2,2,2,128,512]{3,4,2,0,1:T(8,128)(2,1)}, u32[]{:S(2)}) copy-start(bf16[2,2,2,128,512]{3,4,2,0,1:T(8,128)(2,1)} %pad_maximum_fusion.1) | copy-start | bytes 3145732
  165.4 18.3 %all-to-all-start.4 = ((bf16[4,8,128,128]{3,2,1,0:T(8,128)(2,1)}), bf16[4,8,128,128]{3,2,1,0:T(8,128)(2,1)S(1)}, u32[]{:S(2)}, u32[]{:S(2)}) async-start(bf16[4,8,128,128]{3,2,1,0:T(8,128)(2,1)} %fusion.10), calls=%async_computation.5 | async-start | bytes 2097152 | tf_op jit(solution)/shard_map/all_to_all | solution.py:20
  169.7 23.7 %collective-permute-start.5 = (bf16[2,2,128,512]{2,3,0,1:T(8,128)(2,1)}, bf16[2,2,128,512]{2,3,0,1:T(8,128)(2,1)}, u32[]{:S(2)}, u32[]{:S(2)}) collective-permute-start(bf16[2,2,128,512]{2,3,0,1:T(8,128)(2,1)} %slice_bitcast_fusion), channel_id=1, source_target_pairs={{0,1},{1,0},{2,3},{3,2},{4,5},{5,4},{6,7},{7,6},{8,9},{9,8},{10,11... | collective-permute-start | bytes 1572872 | tf_op jit(solution)/shard_map/ppermute | solution.py:37
  184.6 17.1 %all-to-all-start.5 = ((bf16[8,128,128]{2,1,0:T(8,128)(2,1)}), bf16[8,128,128]{2,1,0:T(8,128)(2,1)S(1)}, u32[]{:S(2)}, u32[]{:S(2)}) async-start(bf16[8,128,128]{2,1,0:T(8,128)(2,1)} %reduce_sum.83), calls=%async_computation.6 | async-start | bytes 524288 | tf_op jit(solution)/shard_map/all_to_all | solution.py:20
  202.5 15.4 %all-to-all-start.6 = ((bf16[8,128,128]{2,1,0:T(8,128)(2,1)}), bf16[8,128,128]{2,1,0:T(8,128)(2,1)S(1)}, u32[]{:S(2)}, u32[]{:S(2)}) async-start(bf16[8,128,128]{2,1,0:T(8,128)(2,1)} %broadcast_in_dim.149), calls=%async_computation.7 | async-start | bytes 524288 | tf_op jit(solution)/shard_map/all_to_all | solution.py:251
Sparse Core Ops, SparseCore 0:
  161.5 47.6 reduce-scatter.1

commit v3 on v1

--- a/solution.py
+++ b/solution.py
@@ -41,7 +41,7 @@
     return lax.dot_general(factors, rows, (((1,), (1,)), ((), ())), preferred_element_type=F32)
 
 
-def stats_kernel(slots_ref, own_ref, other_ref, label_ref, emb_ref, rows_ref, stat_ref, peak_ref, mass_ref, score_ref):
+def stats_kernel(slots_ref, own_ref, other_ref, target_ref, emb_ref, rows_ref, stat_ref, peak_ref, mass_ref):
     step = pl.program_id(0)
     width = rows_ref.shape[0] // LIST
 
@@ -54,17 +54,12 @@
             rows_ref[slot * width:(slot + 1) * width, :] = jnp.where(place < NX * NY, near, far)
         peak_ref[...] = jnp.full(peak_ref.shape, NEG, F32)
         mass_ref[...] = jnp.zeros(mass_ref.shape, F32)
-        score_ref[...] = jnp.zeros(score_ref.shape, F32)
 
     factors = emb_ref[...]
     tile = factors.shape[0]
-    class_ids = lax.broadcasted_iota(jnp.int32, (tile // 8, 8, 2 * width), 0) * 8 + lax.broadcasted_iota(jnp.int32, (tile // 8, 8, 2 * width), 1)
     for pair in range(LIST // 2):
         cut = slice(pair * 2 * width, (pair + 1) * 2 * width)
         scores = scores_of(factors, rows_ref[cut, :]).reshape(tile // 8, 8, 2 * width)
-        local_label = label_ref[0:1, cut] - step * tile
-        hit = class_ids == local_label[None]
-        score_ref[:, cut] += jnp.sum(jnp.where(hit, scores, 0.0), axis=0)
         old = peak_ref[:, cut]
         new = jnp.maximum(old, jnp.max(scores, axis=0))
         mass_ref[:, cut] = mass_ref[:, cut] * jnp.exp(old - new) + jnp.sum(jnp.exp(scores - new[None]), axis=0)
@@ -75,11 +70,12 @@
         peak = jnp.max(peak_ref[...], axis=0, keepdims=True)
         mass = jnp.sum(mass_ref[...] * jnp.exp(peak_ref[...] - peak), axis=0, keepdims=True)
         norm = peak + jnp.log(mass)
-        score = jnp.sum(score_ref[...], axis=0, keepdims=True)
-        stat_ref[...] = jnp.zeros(stat_ref.shape, F32)
+        products = rows_ref[...].astype(F32) * target_ref[...].astype(F32)
+        ones = jnp.ones((8, products.shape[1]), F32)
+        score = lax.dot_general(ones, products, (((1,), (1,)), ((), ())), precision=lax.Precision.HIGHEST, preferred_element_type=F32)
         for slot in range(LIST):
             stat_ref[slot:slot + 1, :] = norm[:, slot * width:(slot + 1) * width]
-            stat_ref[8 + slot:9 + slot, :] = score[:, slot * width:(slot + 1) * width]
+            stat_ref[LIST + slot:LIST + 1 + slot, :] = score[0:1, slot * width:(slot + 1) * width]
 
 
 def grads_kernel(slots_ref, live_ref, query_ref, stat_ref, label_ref, rows_ref, emb_ref, part_ref, back_ref, loss_ref, norm_ref, total_ref):
@@ -91,8 +87,9 @@
         for entry in range(LIST):
             place = query_ref[which * LIST + entry]
             base = jnp.maximum(place, 0)
-            norm = stat_ref[pl.ds(base, 1), :]
-            score = stat_ref[pl.ds(base + 8, 1), :]
+            block, rank = base // (2 * LIST), lax.rem(base, 2 * LIST)
+            norm = stat_ref[block, pl.ds(rank, 1), :]
+            score = stat_ref[block, pl.ds(rank + LIST, 1), :]
             norms.append(jnp.where(place >= 0, norm, NEG))
             label_score = label_score + jnp.where(place >= 0, score, 0.0)
         peak = norms[0]
@@ -130,20 +127,6 @@
             @pl.when(slot < live_ref[0])
             def _():
                 back_ref[slots_ref[slot]] = total_ref[:, slot * width:(slot + 1) * width].T.astype(BF16)
-
-
-def column_order(features, parts):
-    rows, depth = features.shape
-    span = parts * 128
-    source = lax.broadcasted_iota(jnp.int32, (span, span), 0)
-    target = lax.broadcasted_iota(jnp.int32, (span, span), 1)
-    group, rest = target // 128, target % 128
-    wanted = (rest // 8) * (8 * parts) + group * 8 + rest % 8
-    permutation = (source == wanted).astype(BF16)
-    chunks = features.reshape(rows * (depth // span), span)
-    moved = jnp.dot(chunks, permutation, preferred_element_type=F32).astype(BF16)
-    moved = moved.reshape(rows, depth // span, parts, 128)
-    return jnp.transpose(moved, (2, 0, 1, 3)).reshape(parts, rows, depth // parts)
 
 
 def local(features, proj, class_emb, lists, labels):
@@ -167,13 +150,17 @@
     slot_places = jnp.sum(jnp.where(chosen, places[None, :], 0), axis=1)
     same = (table[:, :, None, None] == table[None, None]) & (block_ids[None, None, :, None] < block_ids[:, None, None, None])
     entry_rank = jnp.sum(same.astype(jnp.int32), axis=(2, 3))
-    entry_place = (((table ^ own_block) & 1) * (NX * NY) + table // 2) * 16 + entry_rank
+    entry_place = table * (2 * LIST) + entry_rank
     entry_place = jnp.where(table >= 0, entry_place, -1)
     asked = jnp.concatenate([chosen, (block_ids == own_block)[None]], axis=0)
     queries = jnp.sum(jnp.where(asked[:, :, None], entry_place[None], 0), axis=1).reshape(-1)
     slot_labels = jnp.sum(jnp.where(chosen[:, :, None], group_labels[None], 0), axis=1)
     slot_labels = jnp.where(slot_ids[:, None] < live, slot_labels - own_block * block_width, -1)
-    slot_labels = spread(slot_labels.reshape(-1), 8)
+    slot_labels = slot_labels.reshape(-1)
+    inside = (slot_labels >= 0) & (slot_labels < block_width)
+    targets = jnp.take(class_emb, jnp.clip(slot_labels, 0, block_width - 1), axis=0, mode="clip")
+    targets = jnp.where(inside[:, None], targets, jnp.zeros((), BF16))
+    slot_labels = spread(slot_labels, 8)
 
     steps = block_width // TILE
     all_rows = LIST * width
@@ -186,14 +173,13 @@
         stats_kernel,
         grid=(steps,),
         in_specs=[smem, whole, whole, whole, tiled],
-        out_specs=[fixed((all_rows, rank_width)), fixed((16, width))],
-        out_shape=[jax.ShapeDtypeStruct((all_rows, rank_width), BF16), jax.ShapeDtypeStruct((16, width), F32)],
-        scratch_shapes=[pltpu.VMEM((8, all_rows), F32)] * 3,
+        out_specs=[fixed((all_rows, rank_width)), fixed((2 * LIST, width))],
+        out_shape=[jax.ShapeDtypeStruct((all_rows, rank_width), BF16), jax.ShapeDtypeStruct((2 * LIST, width), F32)],
+        scratch_shapes=[pltpu.VMEM((8, all_rows), F32)] * 2,
         compiler_params=params,
-    )(slot_places, near, far, slot_labels, class_emb)
-
-    stats_near, stats_far = gather_cls(stats)
-    all_stats = jnp.concatenate([stats_near, stats_far], axis=0).reshape(-1, width)
+    )(slot_places, near, far, targets, class_emb)
+
+    all_stats = lax.all_to_all(spread(stats, blocks), "cls", 0, 0, tiled=True)
     class_part, outbox, loss = pl.pallas_call(
         grads_kernel,
         grid=(steps,),
@@ -209,14 +195,18 @@
     )(slot_places, live.reshape(1), queries, all_stats, slot_labels, rows, class_emb)
 
     class_grad = lax.psum_scatter(class_part, "dp", scatter_dimension=0, tiled=True).astype(F32)
-    columns = lax.all_to_all(column_order(features, groups), "dp", 0, 0, tiled=True)
-    columns = columns.reshape(groups * width, -1)
     row_grad = scatter_cls(outbox.reshape(NK, NX, NY, width, rank_width))
-    row_grads = lax.all_to_all(spread(row_grad, groups), "dp", 0, 0, tiled=True).reshape(groups * width, rank_width)
-    proj_part = lax.dot_general(columns, row_grads, (((0,), (0,)), ((), ())), preferred_element_type=F32)
-    share = proj_part.shape[0] // blocks
-    arrived = lax.all_to_all(proj_part.reshape(blocks, share, rank_width), "cls", 0, 0, tiled=True)
-    proj_grad = jnp.sum(arrived, axis=0)
+    proj_part = lax.dot_general(features, row_grad, (((0,), (0,)), ((), ())), preferred_element_type=F32)
+    share = proj_part.shape[0] // (blocks * groups)
+    proj_part = proj_part.reshape(NX * NY, NK, groups * share, rank_width)
+    core = own_block % NK
+    kept = lax.dynamic_index_in_dim(proj_part, core, 1, keepdims=False)
+    given = lax.dynamic_index_in_dim(proj_part, 1 - core, 1, keepdims=False)
+    total = kept + lax.ppermute(given, "cls", SWAP_K)
+    total = jnp.sum(exchange(total.reshape(NX, NY, groups * share, rank_width), GROUP_X), axis=0)
+    total = jnp.sum(exchange(total, GROUP_Y), axis=0)
+    total = total.reshape(groups, share, rank_width)
+    proj_grad = jnp.sum(lax.all_to_all(total, "dp", 0, 0, tiled=True), axis=0)
     return loss.reshape(-1), class_grad, proj_grad
 
 

time: 234 us -> 212 us (0.906)
  waiting for transfers between devices: 83.2 us -> 71.9 us
  blocking collectives: 41 us -> 29.8 us
  Pallas kernels: 26.1 us -> 23.7 us
    all_to_all x1 -> x0, blocking collectives: 24.2 us -> none  [local(): lax.all_to_all(proj_part.reshape(blocks, share, rank_width), 'cls', 0, 0,...]
    all_to_all x2, waiting for transfers between devices: 37.3 us -> 21.6 us  [the longest x1 16.6 us: local(): all_stats = lax.all_to_all(spread(stats, blocks), 'cls', 0, 0, tiled=True)]
    all_to_all x1 -> x2, blocking collectives: 16.9 us -> 29.8 us  [exchange(): lax.all_to_all(value, 'cls', 0, 0, axis_index_groups=groups, tiled=True)]
    ppermute x0 -> x1, starting transfers between devices: none -> 4.65 us  [local(): total = kept + lax.ppermute(given, 'cls', SWAP_K)]
    ppermute x2 -> x1, starting transfers between devices: 10.5 us -> 5.97 us  [gather_cls(): return (own, lax.ppermute(own, 'cls', SWAP_K))]
    all_to_all x5 -> x4, waiting for transfers between devices: 41 us -> 44.5 us  [exchange(): lax.all_to_all(value, 'cls', 0, 0, axis_index_groups=groups, tiled=True)]
    ppermute x0 -> x1, waiting for transfers between devices: none -> 2.6 us  [local(): total = kept + lax.ppermute(given, 'cls', SWAP_K)]
    pallas_call x1, Pallas kernels: 12.6 us -> 10 us  [local(): pl.pallas_call(stats_kernel, grid=(steps,), in_specs=[smem, whole, whole,...]
  transfers between devices with their start and end apart: 11 -> 10, of which waited for: 10 -> 8; matrix products, arithmetic and copies ran while one was open for 6% -> 7% of each run, Pallas kernels for 0% -> 0%
where the time goes in v3:
time: 212 us; the launch traced here: 210 us
  waiting for transfers between devices  71.9 us (34%)
  starting transfers between devices  47.9 us (23%)
  blocking collectives  29.8 us (14%)
  Pallas kernels  23.7 us (11%)
  between operations  14.2 us (7%)
  other arithmetic  9.42 us (4%)
  local copies, waits for them, and re-layouts  9.36 us (4%)
  matrix products  3.4 us (2%)
    all_to_all x4, waiting for transfers between devices, exchange(): lax.all_to_all(value, 'cls', 0, 0, axis_index_groups=groups, tiled=True)  44.5 us
    all_to_all x2, blocking collectives, exchange(): lax.all_to_all(value, 'cls', 0, 0, axis_index_groups=groups, tiled=True)  29.8 us
    all_to_all x4, starting transfers between devices, exchange(): lax.all_to_all(value, 'cls', 0, 0, axis_index_groups=groups, tiled=True)  20.4 us
    all_to_all x1, waiting for transfers between devices, local(): all_stats = lax.all_to_all(spread(stats, blocks), 'cls', 0, 0, tiled=True)  16.6 us
    pallas_call x1, Pallas kernels, local(): pl.pallas_call(grads_kernel, grid=(steps,), in_specs=[smem, smem, smem, w...  13.6 us
    all_to_all x1, starting transfers between devices, local(): proj_grad = jnp.sum(lax.all_to_all(total, 'dp', 0, 0, tiled=True), axis=0)  10.4 us
    pallas_call x1, Pallas kernels, local(): pl.pallas_call(stats_kernel, grid=(steps,), in_specs=[smem, whole, whole,...  10 us
    ppermute x1, starting transfers between devices, gather_cls(): return (own, lax.ppermute(own, 'cls', SWAP_K))  5.97 us
  transfers between devices with their start and end apart: 10, of which 8 were waited for; matrix products, arithmetic and copies ran while one was open for 7% of the time, Pallas kernels for 0%

profile of v3, /device:TPU:1, one launch (start us, length us, event | category | flops | bytes accessed | tf_op | source)
XLA Modules:
  0.0 209.7 jit_solution(15888326293187577239)
XLA Ops:
  7.2 1.2 copy-done
  8.4 1.6 convolution_convert_fusion
  10.8 7.8 %all-to-all-start = ((bf16[8,128,128]{2,1,0:T(8,128)(2,1)}), bf16[8,128,128]{2,1,0:T(8,128)(2,1)S(1)}, u32[]{:S(2)}, u32[]{:S(2)}) async-start(bf16[8,128,128]{2,1,0:T(8,128)(2,1)} %broadcast_in_dim.125), calls=%async_computation | async-start | bytes 524288 | tf_op jit(solution)/shard_map/all_to_all | solution.py:20
  18.6 9.4 %all-to-all-done = bf16[8,128,128]{2,1,0:T(8,128)(2,1)S(1)} async-done(((bf16[8,128,128]{2,1,0:T(8,128)(2,1)}), bf16[8,128,128]{2,1,0:T(8,128)(2,1)S(1)}, u32[]{:S(2)}, u32[]{:S(2)}) %all-to-all-start) | async-done | bytes 262176 | tf_op jit(solution)/shard_map/all_to_all | solution.py:20
  28.0 1.3 broadcast_in_dim.126
  29.3 5.0 %all-to-all-start.1 = ((bf16[4,8,128,128]{3,2,1,0:T(8,128)(2,1)}), bf16[4,8,128,128]{3,2,1,0:T(8,128)(2,1)}, u32[]{:S(2)}, u32[]{:S(2)}) async-start(bf16[4,8,128,128]{3,2,1,0:T(8,128)(2,1)} %broadcast_in_dim.126), calls=%async_computation.1 | async-start | bytes 2097152 | tf_op jit(solution)/shard_map/all_to_all | solution.py:20
  35.3 11.0 %all-to-all-done.1 = bf16[4,8,128,128]{3,2,1,0:T(8,128)(2,1)} async-done(((bf16[4,8,128,128]{3,2,1,0:T(8,128)(2,1)}), bf16[4,8,128,128]{3,2,1,0:T(8,128)(2,1)}, u32[]{:S(2)}, u32[]{:S(2)}) %all-to-all-start.1) | async-done | bytes 1048608 | tf_op jit(solution)/shard_map/all_to_all | solution.py:20
  46.3 6.0 %collective-permute-start = (bf16[32,128,128]{2,1,0:T(8,128)(2,1)}, bf16[32,128,128]{2,1,0:T(8,128)(2,1)}, u32[]{:S(2)}, u32[]{:S(2)}) collective-permute-start(bf16[32,128,128]{2,1,0:T(8,128)(2,1)} %bitcast.2.own_ref), channel_id=1, source_target_pairs={{0,8},{8,0},{16,24},{24,16},{32,40},{40,32},{48,56},{56,48},{64,72... | collective-permute-start | bytes 3145736 | tf_op jit(solution)/shard_map/ppermute | solution.py:30
  53.1 1.9 gather_fusion
  55.3 10.0 %shard_map.76 = (bf16[768,128]{1,0:T(8,128)(2,1)S(1)}, f32[12,128]{1,0:T(8,128)S(1)}) custom-call(s32[6]{0:T(128)S(1)} %select_reduce_fusion.2.slots_ref, bf16[32,128,128]{2,1,0:T(8,128)(2,1)} %bitcast.2.own_ref, bf16[32,128,128]{2,1,0:T(8,128)(2,1)} %collective-permute-done.other_ref, bf16[768,128]{1,0:T(8,128)(2,1)S(1)} %broadcast_select_fusion.target_ref, ...), custom_call_target="tpu_custom_call" | custom-call | tf_op jit(solution)/shard_map/pallas_call | solution.py:172
  66.3 4.3 %all-to-all-start.2 = ((f32[64,12,128]{2,1,0:T(8,128)}), f32[64,12,128]{2,1,0:T(8,128)S(1)}, u32[]{:S(2)}, u32[]{:S(2)}) async-start(f32[64,12,128]{2,1,0:T(8,128)} %broadcast_in_dim.135), calls=%async_computation.2 | async-start | bytes 1048576 | tf_op jit(solution)/shard_map/all_to_all | solution.py:182
  71.3 16.6 %all-to-all-done.2.stat_ref = f32[64,12,128]{2,1,0:T(8,128)S(1)} async-done(((f32[64,12,128]{2,1,0:T(8,128)}), f32[64,12,128]{2,1,0:T(8,128)S(1)}, u32[]{:S(2)}, u32[]{:S(2)}) %all-to-all-start.2) | async-done | bytes 393248 | tf_op jit(solution)/shard_map/all_to_all | solution.py:182
  87.9 13.6 %shard_map.77 = (bf16[8192,128]{1,0:T(8,128)(2,1)}, bf16[64,128,128]{2,1,0:T(8,128)(2,1)S(1)}, f32[1,128]{1,0:T(1,128)}) custom-call(s32[6]{0:T(128)S(1)} %select_reduce_fusion.2.slots_ref, s32[1]{0:T(128)} %bitcast.1.live_ref, s32[42]{0:T(128)S(1)} %reshape.220.query_ref, f32[64,12,128]{2,1,0:T(8,128)S(1)} %all-to-all-done.2.stat_ref, ...), custom_call_target="tpu_custom_call" | custom-call | tf_op jit(solution)/shard_map/pallas_call | solution.py:183
  101.7 2.1 %collective-permute-start.1 = (bf16[4,8,128,128]{3,2,1,0:T(8,128)(2,1)S(1)}, bf16[4,8,128,128]{3,2,1,0:T(8,128)(2,1)S(1)}, u32[]{:S(2)}, u32[]{:S(2)}) collective-permute-start(bf16[4,8,128,128]{3,2,1,0:T(8,128)(2,1)S(1)} %bitcast.38), channel_id=1, source_target_pairs={{0,8},{8,0},{16,24},{24,16},{32,40},{40,32},{48,56},{56,48},{64,72... | collective-permute-start | bytes 3145736 | tf_op jit(solution)/shard_map/ppermute | solution.py:34
  103.8 2.4 %collective-permute-done.1 = bf16[4,8,128,128]{3,2,1,0:T(8,128)(2,1)S(1)} collective-permute-done((bf16[4,8,128,128]{3,2,1,0:T(8,128)(2,1)S(1)}, bf16[4,8,128,128]{3,2,1,0:T(8,128)(2,1)S(1)}, u32[]{:S(2)}, u32[]{:S(2)}) %collective-permute-start.1) | collective-permute-done | bytes 1048608 | tf_op jit(solution)/shard_map/ppermute | solution.py:34
  106.2 1.4 fusion
  107.6 3.9 %all-to-all-start.3 = ((bf16[4,8,128,128]{3,2,1,0:T(8,128)(2,1)}), bf16[4,8,128,128]{3,2,1,0:T(8,128)(2,1)S(1)}, u32[]{:S(2)}, u32[]{:S(2)}) async-start(bf16[4,8,128,128]{3,2,1,0:T(8,128)(2,1)} %fusion), calls=%async_computation.4 | async-start | bytes 2097152 | tf_op jit(solution)/shard_map/all_to_all | solution.py:20
  112.2 14.1 %all-to-all-done.3 = bf16[4,8,128,128]{3,2,1,0:T(8,128)(2,1)S(1)} async-done(((bf16[4,8,128,128]{3,2,1,0:T(8,128)(2,1)}), bf16[4,8,128,128]{3,2,1,0:T(8,128)(2,1)S(1)}, u32[]{:S(2)}, u32[]{:S(2)}) %all-to-all-start.3) | async-done | bytes 1048608 | tf_op jit(solution)/shard_map/all_to_all | solution.py:20
  126.3 0.9 reduce_sum.101
  127.2 3.7 %all-to-all-start.4 = ((bf16[8,128,128]{2,1,0:T(8,128)(2,1)}), bf16[8,128,128]{2,1,0:T(8,128)(2,1)S(1)}, u32[]{:S(2)}, u32[]{:S(2)}) async-start(bf16[8,128,128]{2,1,0:T(8,128)(2,1)} %reduce_sum.101), calls=%async_computation.5 | async-start | bytes 524288 | tf_op jit(solution)/shard_map/all_to_all | solution.py:20
  130.9 10.1 %all-to-all-done.4 = bf16[8,128,128]{2,1,0:T(8,128)(2,1)S(1)} async-done(((bf16[8,128,128]{2,1,0:T(8,128)(2,1)}), bf16[8,128,128]{2,1,0:T(8,128)(2,1)S(1)}, u32[]{:S(2)}, u32[]{:S(2)}) %all-to-all-start.4) | async-done | bytes 262176 | tf_op jit(solution)/shard_map/all_to_all | solution.py:20
  141.1 1.8 convolution_bitcast_fusion
  142.8 1.9 copy.19
  144.7 1.1 dynamic-slice_bitcast_fusion
  145.8 4.6 %collective-permute-start.2 = (f32[32,64,128]{2,1,0:T(8,128)}, f32[32,64,128]{2,1,0:T(8,128)}, u32[]{:S(2)}, u32[]{:S(2)}) collective-permute-start(f32[32,64,128]{2,1,0:T(8,128)} %dynamic-slice_bitcast_fusion), channel_id=1, source_target_pairs={{0,8},{8,0},{16,24},{24,16},{32,40},{40,32},{48,56},{56,48},{64,72... | collective-permute-start | bytes 3145736 | tf_op jit(solution)/shard_map/ppermute | solution.py:205
  150.5 2.6 %collective-permute-done.2 = f32[32,64,128]{2,1,0:T(8,128)} collective-permute-done((f32[32,64,128]{2,1,0:T(8,128)}, f32[32,64,128]{2,1,0:T(8,128)}, u32[]{:S(2)}, u32[]{:S(2)}) %collective-permute-start.2) | collective-permute-done | bytes 1048608 | tf_op jit(solution)/shard_map/ppermute | solution.py:205
  153.1 1.4 bitcast_add_fusion
  154.4 17.3 %all_to_all.40 = f32[4,8,64,128]{3,2,1,0:T(8,128)S(1)} all-to-all(f32[4,8,64,128]{3,2,1,0:T(8,128)S(1)} %bitcast.37), channel_id=1, replica_groups={{0,128,256,384},{8,136,264,392},{16,144,272,400},{24,152,280,408},{32,1..., dimensions={0} | all-to-all | bytes 2097152 | tf_op jit(solution)/shard_map/all_to_all | solution.py:20
  171.8 12.5 %all_to_all.41 = f32[8,64,128]{2,1,0:T(8,128)S(1)} all-to-all(f32[8,64,128]{2,1,0:T(8,128)S(1)} %reduce_sum.103), channel_id=1, replica_groups={{0,16,32,48,64,80,96,112},{8,24,40,56,72,88,104,120},{128,144,160,176,1..., dimensions={0} | all-to-all | bytes 524288 | tf_op jit(solution)/shard_map/all_to_all | solution.py:20
  184.9 10.4 %all-to-all-start.7 = ((f32[8,8,128]{2,1,0:T(8,128)}), f32[8,8,128]{2,1,0:T(8,128)S(1)}, u32[]{:S(2)}, u32[]{:S(2)}) async-start(f32[8,8,128]{2,1,0:T(8,128)} %bitcast.14), calls=%async_computation.8 | async-start | bytes 65536 | tf_op jit(solution)/shard_map/all_to_all | solution.py:209
  195.4 1.8 convert_element_type.48
  197.2 5.1 %all-to-all-done.7 = f32[8,8,128]{2,1,0:T(8,128)S(1)} async-done(((f32[8,8,128]{2,1,0:T(8,128)}), f32[8,8,128]{2,1,0:T(8,128)S(1)}, u32[]{:S(2)}, u32[]{:S(2)}) %all-to-all-start.7) | async-done | bytes 32800 | tf_op jit(solution)/shard_map/all_to_all | solution.py:209
  (43 shorter events, 6.8 us)
Async XLA Ops:
  7.2 1.2 copy-start
  7.2 11.4 %copy-start.3 = (s32[64,1,6]{0,1,2:T(1,128)S(1)}, s32[64,1,6]{0,1,2:T(1,128)}, u32[]{:S(2)}) copy-start(s32[64,1,6]{0,1,2:T(1,128)} %param.8) | copy-start | bytes 4612
  10.8 24.4 %copy-start.2 = (s32[64,1,128]{2,1,0:T(1,128)S(1)}, s32[64,1,128]{2,1,0:T(1,128)}, u32[]{:S(2)}) copy-start(s32[64,1,128]{2,1,0:T(1,128)} %param.9) | copy-start | bytes 98308
  10.8 42.3 %copy-start.1 = (bf16[8192,128]{1,0:T(8,128)(2,1)S(1)}, bf16[8192,128]{1,0:T(8,128)(2,1)}, u32[]{:S(2)}) copy-start(bf16[8192,128]{1,0:T(8,128)(2,1)} %emb_ref.3) | copy-start | bytes 6291460
  10.8 17.2 %all-to-all-start = ((bf16[8,128,128]{2,1,0:T(8,128)(2,1)}), bf16[8,128,128]{2,1,0:T(8,128)(2,1)S(1)}, u32[]{:S(2)}, u32[]{:S(2)}) async-start(bf16[8,128,128]{2,1,0:T(8,128)(2,1)} %broadcast_in_dim.125), calls=%async_computation | async-start | bytes 524288 | tf_op jit(solution)/shard_map/all_to_all | solution.py:20
  29.3 17.1 %all-to-all-start.1 = ((bf16[4,8,128,128]{3,2,1,0:T(8,128)(2,1)}), bf16[4,8,128,128]{3,2,1,0:T(8,128)(2,1)}, u32[]{:S(2)}, u32[]{:S(2)}) async-start(bf16[4,8,128,128]{3,2,1,0:T(8,128)(2,1)} %broadcast_in_dim.126), calls=%async_computation.1 | async-start | bytes 2097152 | tf_op jit(solution)/shard_map/all_to_all | solution.py:20
  46.3 9.0 %collective-permute-start = (bf16[32,128,128]{2,1,0:T(8,128)(2,1)}, bf16[32,128,128]{2,1,0:T(8,128)(2,1)}, u32[]{:S(2)}, u32[]{:S(2)}) collective-permute-start(bf16[32,128,128]{2,1,0:T(8,128)(2,1)} %bitcast.2.own_ref), channel_id=1, source_target_pairs={{0,8},{8,0},{16,24},{24,16},{32,40},{40,32},{48,56},{56,48},{64,72... | collective-permute-start | bytes 3145736 | tf_op jit(solution)/shard_map/ppermute | solution.py:30
  66.3 21.6 %all-to-all-start.2 = ((f32[64,12,128]{2,1,0:T(8,128)}), f32[64,12,128]{2,1,0:T(8,128)S(1)}, u32[]{:S(2)}, u32[]{:S(2)}) async-start(f32[64,12,128]{2,1,0:T(8,128)} %broadcast_in_dim.135), calls=%async_computation.2 | async-start | bytes 1048576 | tf_op jit(solution)/shard_map/all_to_all | solution.py:182
  101.7 4.6 %collective-permute-start.1 = (bf16[4,8,128,128]{3,2,1,0:T(8,128)(2,1)S(1)}, bf16[4,8,128,128]{3,2,1,0:T(8,128)(2,1)S(1)}, u32[]{:S(2)}, u32[]{:S(2)}) collective-permute-start(bf16[4,8,128,128]{3,2,1,0:T(8,128)(2,1)S(1)} %bitcast.38), channel_id=1, source_target_pairs={{0,8},{8,0},{16,24},{24,16},{32,40},{40,32},{48,56},{56,48},{64,72... | collective-permute-start | bytes 3145736 | tf_op jit(solution)/shard_map/ppermute | solution.py:34
  107.6 18.7 %all-to-all-start.3 = ((bf16[4,8,128,128]{3,2,1,0:T(8,128)(2,1)}), bf16[4,8,128,128]{3,2,1,0:T(8,128)(2,1)S(1)}, u32[]{:S(2)}, u32[]{:S(2)}) async-start(bf16[4,8,128,128]{3,2,1,0:T(8,128)(2,1)} %fusion), calls=%async_computation.4 | async-start | bytes 2097152 | tf_op jit(solution)/shard_map/all_to_all | solution.py:20
  111.5 83.9 %reduce-scatter.2.cloned.1.call-start = ((), (), s32[]{:S(2)}) async-start(), calls=%async_computation.9 | async-start | bytes 2359296 | tf_op jit(solution)/shard_map/reduce_scatter | solution.py:197
  127.2 13.8 %all-to-all-start.4 = ((bf16[8,128,128]{2,1,0:T(8,128)(2,1)}), bf16[8,128,128]{2,1,0:T(8,128)(2,1)S(1)}, u32[]{:S(2)}, u32[]{:S(2)}) async-start(bf16[8,128,128]{2,1,0:T(8,128)(2,1)} %reduce_sum.101), calls=%async_computation.5 | async-start | bytes 524288 | tf_op jit(solution)/shard_map/all_to_all | solution.py:20
  145.8 7.3 %collective-permute-start.2 = (f32[32,64,128]{2,1,0:T(8,128)}, f32[32,64,128]{2,1,0:T(8,128)}, u32[]{:S(2)}, u32[]{:S(2)}) collective-permute-start(f32[32,64,128]{2,1,0:T(8,128)} %dynamic-slice_bitcast_fusion), channel_id=1, source_target_pairs={{0,8},{8,0},{16,24},{24,16},{32,40},{40,32},{48,56},{56,48},{64,72... | collective-permute-start | bytes 3145736 | tf_op jit(solution)/shard_map/ppermute | solution.py:205
  184.9 17.3 %all-to-all-start.7 = ((f32[8,8,128]{2,1,0:T(8,128)}), f32[8,8,128]{2,1,0:T(8,128)S(1)}, u32[]{:S(2)}, u32[]{:S(2)}) async-start(f32[8,8,128]{2,1,0:T(8,128)} %bitcast.14), calls=%async_computation.8 | async-start | bytes 65536 | tf_op jit(solution)/shard_map/all_to_all | solution.py:209
Sparse Core Ops, SparseCore 0:
  115.2 43.1 reduce-scatter.1

commit v4 on v3

--- a/solution.py
+++ b/solution.py
@@ -7,7 +7,9 @@
 
 LIST = 6
 NX, NY, NK = 4, 8, 2
+STATS_TILE = 2048
 TILE = 1024
+PIECE = 256
 NEG = -1e30
 F32 = jnp.float32
 BF16 = jnp.bfloat16
@@ -55,15 +57,13 @@
         peak_ref[...] = jnp.full(peak_ref.shape, NEG, F32)
         mass_ref[...] = jnp.zeros(mass_ref.shape, F32)
 
-    factors = emb_ref[...]
-    tile = factors.shape[0]
-    for pair in range(LIST // 2):
-        cut = slice(pair * 2 * width, (pair + 1) * 2 * width)
-        scores = scores_of(factors, rows_ref[cut, :]).reshape(tile // 8, 8, 2 * width)
-        old = peak_ref[:, cut]
+    for start in range(0, emb_ref.shape[0], PIECE):
+        factors = emb_ref[start:start + PIECE, :]
+        scores = scores_of(factors, rows_ref[...]).reshape(PIECE // 8, 8, rows_ref.shape[0])
+        old = peak_ref[...]
         new = jnp.maximum(old, jnp.max(scores, axis=0))
-        mass_ref[:, cut] = mass_ref[:, cut] * jnp.exp(old - new) + jnp.sum(jnp.exp(scores - new[None]), axis=0)
-        peak_ref[:, cut] = new
+        mass_ref[...] = mass_ref[...] * jnp.exp(old - new) + jnp.sum(jnp.exp(scores - new[None]), axis=0)
+        peak_ref[...] = new
 
     @pl.when(step == pl.num_programs(0) - 1)
     def _():
@@ -110,16 +110,18 @@
         total_ref[...] = jnp.zeros(total_ref.shape, F32)
         back_ref[...] = jnp.zeros(back_ref.shape, BF16)
 
-    factors = emb_ref[...]
-    tile = factors.shape[0]
+    tile = emb_ref.shape[0]
     rows = rows_ref[...]
-    scores = scores_of(factors, rows)
-    probs = jnp.exp(scores - norm_ref[0:1, :])
-    class_ids = lax.broadcasted_iota(jnp.int32, scores.shape, 0)
-    hit = class_ids == label_ref[0:1, :] - step * tile
-    weights = jnp.where(hit, probs - 1.0, probs).astype(BF16)
-    part_ref[...] = jnp.dot(weights, rows, preferred_element_type=F32).astype(BF16)
-    total_ref[...] += lax.dot_general(factors, weights, (((0,), (0,)), ((), ())), preferred_element_type=F32)
+    class_ids = lax.broadcasted_iota(jnp.int32, (PIECE, rows.shape[0]), 0)
+    total = total_ref[...]
+    for start in range(0, tile, PIECE):
+        factors = emb_ref[start:start + PIECE, :]
+        probs = jnp.exp(scores_of(factors, rows) - norm_ref[0:1, :])
+        hit = class_ids == label_ref[0:1, :] - (step * tile + start)
+        weights = jnp.where(hit, probs - 1.0, probs).astype(BF16)
+        part_ref[start:start + PIECE, :] = jnp.dot(weights, rows, preferred_element_type=F32).astype(BF16)
+        total = total + lax.dot_general(factors, weights, (((0,), (0,)), ((), ())), preferred_element_type=F32)
+    total_ref[...] = total
 
     @pl.when(step == pl.num_programs(0) - 1)
     def _():
@@ -171,8 +173,8 @@
     params = pltpu.CompilerParams(vmem_limit_bytes=48 * 1024 * 1024)
     rows, stats = pl.pallas_call(
         stats_kernel,
-        grid=(steps,),
-        in_specs=[smem, whole, whole, whole, tiled],
+        grid=(block_width // STATS_TILE,),
+        in_specs=[smem, whole, whole, whole, pl.BlockSpec((STATS_TILE, rank_width), lambda i: (i, 0))],
         out_specs=[fixed((all_rows, rank_width)), fixed((2 * LIST, width))],
         out_shape=[jax.ShapeDtypeStruct((all_rows, rank_width), BF16), jax.ShapeDtypeStruct((2 * LIST, width), F32)],
         scratch_shapes=[pltpu.VMEM((8, all_rows), F32)] * 2,
@@ -196,16 +198,16 @@
 
     class_grad = lax.psum_scatter(class_part, "dp", scatter_dimension=0, tiled=True).astype(F32)
     row_grad = scatter_cls(outbox.reshape(NK, NX, NY, width, rank_width))
-    proj_part = lax.dot_general(features, row_grad, (((0,), (0,)), ((), ())), preferred_element_type=F32)
+    proj_part = lax.dot_general(features, row_grad, (((0,), (0,)), ((), ())), preferred_element_type=F32).astype(BF16)
     share = proj_part.shape[0] // (blocks * groups)
     proj_part = proj_part.reshape(NX * NY, NK, groups * share, rank_width)
     core = own_block % NK
     kept = lax.dynamic_index_in_dim(proj_part, core, 1, keepdims=False)
     given = lax.dynamic_index_in_dim(proj_part, 1 - core, 1, keepdims=False)
-    total = kept + lax.ppermute(given, "cls", SWAP_K)
-    total = jnp.sum(exchange(total.reshape(NX, NY, groups * share, rank_width), GROUP_X), axis=0)
-    total = jnp.sum(exchange(total, GROUP_Y), axis=0)
-    total = total.reshape(groups, share, rank_width)
+    total = (kept.astype(F32) + lax.ppermute(given, "cls", SWAP_K).astype(F32)).astype(BF16)
+    total = exchange(total.reshape(NX, NY, groups * share, rank_width), GROUP_X)
+    total = exchange(jnp.sum(total, axis=0, dtype=F32).astype(BF16), GROUP_Y)
+    total = jnp.sum(total, axis=0, dtype=F32).reshape(groups, share, rank_width)
     proj_grad = jnp.sum(lax.all_to_all(total, "dp", 0, 0, tiled=True), axis=0)
     return loss.reshape(-1), class_grad, proj_grad
 

time: 212 us -> 200 us (0.943)
  blocking collectives: 29.8 us -> 57.8 us
  waiting for transfers between devices: 71.9 us -> 50.9 us
  starting transfers between devices: 47.9 us -> 33.3 us
  other arithmetic: 9.42 us -> 6.66 us
    all_to_all x0 -> x1, blocking collectives: none -> 17.1 us  [local(): proj_grad = jnp.sum(lax.all_to_all(total, 'dp', 0, 0, tiled=True), axis=0)]
    all_to_all x4 -> x3, waiting for transfers between devices: 44.5 us -> 30.4 us  [exchange(): lax.all_to_all(value, 'cls', 0, 0, axis_index_groups=groups, tiled=True)]
    all_to_all x2 -> x3, blocking collectives: 29.8 us -> 40.7 us  [exchange(): lax.all_to_all(value, 'cls', 0, 0, axis_index_groups=groups, tiled=True)]
    all_to_all x1 -> x0, starting transfers between devices: 10.4 us -> none  [local(): proj_grad = jnp.sum(lax.all_to_all(total, 'dp', 0, 0, tiled=True), axis=0)]
    all_to_all x1 -> x0, waiting for transfers between devices: 5.08 us -> none  [local(): proj_grad = jnp.sum(lax.all_to_all(total, 'dp', 0, 0, tiled=True), axis=0)]
    all_to_all x4 -> x3, starting transfers between devices: 20.4 us -> 16.2 us  [exchange(): lax.all_to_all(value, 'cls', 0, 0, axis_index_groups=groups, tiled=True)]
    pallas_call x1, Pallas kernels: 13.6 us -> 15.8 us  [local(): pl.pallas_call(grads_kernel, grid=(steps,), in_specs=[smem, smem, smem, w...]
  transfers between devices with their start and end apart: 10 -> 8, of which waited for: 8 -> 6; matrix products, arithmetic and copies ran while one was open for 7% -> 4% of each run, Pallas kernels for 0% -> 0%
where the time goes in v4:
time: 200 us; the launch traced here: 198 us
  blocking collectives  57.8 us (29%)
  waiting for transfers between devices  50.9 us (25%)
  starting transfers between devices  33.3 us (17%)
  Pallas kernels  24.5 us (12%)
  between operations  14.3 us (7%)
  local copies, waits for them, and re-layouts  8.14 us (4%)
  other arithmetic  6.66 us (3%)
  matrix products  2.1 us (1%)
    all_to_all x3, blocking collectives, exchange(): lax.all_to_all(value, 'cls', 0, 0, axis_index_groups=groups, tiled=True)  40.7 us
    all_to_all x3, waiting for transfers between devices, exchange(): lax.all_to_all(value, 'cls', 0, 0, axis_index_groups=groups, tiled=True)  30.4 us
    all_to_all x1, blocking collectives, local(): proj_grad = jnp.sum(lax.all_to_all(total, 'dp', 0, 0, tiled=True), axis=0)  17.1 us
    all_to_all x1, waiting for transfers between devices, local(): all_stats = lax.all_to_all(spread(stats, blocks), 'cls', 0, 0, tiled=True)  16.5 us
    all_to_all x3, starting transfers between devices, exchange(): lax.all_to_all(value, 'cls', 0, 0, axis_index_groups=groups, tiled=True)  16.2 us
    pallas_call x1, Pallas kernels, local(): pl.pallas_call(grads_kernel, grid=(steps,), in_specs=[smem, smem, smem, w...  15.8 us
    pallas_call x1, Pallas kernels, local(): pl.pallas_call(stats_kernel, grid=(block_width // STATS_TILE,), in_specs=...  8.63 us
    ppermute x1, starting transfers between devices, gather_cls(): return (own, lax.ppermute(own, 'cls', SWAP_K))  5.97 us
  transfers between devices with their start and end apart: 8, of which 6 were waited for; matrix products, arithmetic and copies ran while one was open for 4% of the time, Pallas kernels for 0%

profile of v4, /device:TPU:1, one launch (start us, length us, event | category | flops | bytes accessed | tf_op | source)
XLA Modules:
  0.0 197.7 jit_solution(1479078297317138122)
XLA Ops:
  7.2 1.2 copy-done
  8.4 1.6 convolution_convert_fusion.1
  10.0 0.7 broadcast_in_dim.125
  10.8 7.8 %all-to-all-start = ((bf16[8,128,128]{2,1,0:T(8,128)(2,1)}), bf16[8,128,128]{2,1,0:T(8,128)(2,1)S(1)}, u32[]{:S(2)}, u32[]{:S(2)}) async-start(bf16[8,128,128]{2,1,0:T(8,128)(2,1)} %broadcast_in_dim.125), calls=%async_computation | async-start | bytes 524288 | tf_op jit(solution)/shard_map/all_to_all | solution.py:22
  18.6 9.4 %all-to-all-done = bf16[8,128,128]{2,1,0:T(8,128)(2,1)S(1)} async-done(((bf16[8,128,128]{2,1,0:T(8,128)(2,1)}), bf16[8,128,128]{2,1,0:T(8,128)(2,1)S(1)}, u32[]{:S(2)}, u32[]{:S(2)}) %all-to-all-start) | async-done | bytes 262176 | tf_op jit(solution)/shard_map/all_to_all | solution.py:22
  28.0 1.3 broadcast_in_dim.126
  29.3 5.0 %all-to-all-start.1 = ((bf16[4,8,128,128]{3,2,1,0:T(8,128)(2,1)}), bf16[4,8,128,128]{3,2,1,0:T(8,128)(2,1)}, u32[]{:S(2)}, u32[]{:S(2)}) async-start(bf16[4,8,128,128]{3,2,1,0:T(8,128)(2,1)} %broadcast_in_dim.126), calls=%async_computation.1 | async-start | bytes 2097152 | tf_op jit(solution)/shard_map/all_to_all | solution.py:22
  34.4 0.6 convert_reduce_fusion.2
  35.3 11.0 %all-to-all-done.1 = bf16[4,8,128,128]{3,2,1,0:T(8,128)(2,1)} async-done(((bf16[4,8,128,128]{3,2,1,0:T(8,128)(2,1)}), bf16[4,8,128,128]{3,2,1,0:T(8,128)(2,1)}, u32[]{:S(2)}, u32[]{:S(2)}) %all-to-all-start.1) | async-done | bytes 1048608 | tf_op jit(solution)/shard_map/all_to_all | solution.py:22
  46.3 6.0 %collective-permute-start = (bf16[32,128,128]{2,1,0:T(8,128)(2,1)}, bf16[32,128,128]{2,1,0:T(8,128)(2,1)}, u32[]{:S(2)}, u32[]{:S(2)}) collective-permute-start(bf16[32,128,128]{2,1,0:T(8,128)(2,1)} %bitcast.2.own_ref), channel_id=1, source_target_pairs={{0,8},{8,0},{16,24},{24,16},{32,40},{40,32},{48,56},{56,48},{64,72... | collective-permute-start | bytes 3145736 | tf_op jit(solution)/shard_map/ppermute | solution.py:32
  52.3 0.7 iota_compare_fusion.2
  53.1 1.9 gather_fusion
  55.3 8.6 %shard_map.76 = (bf16[768,128]{1,0:T(8,128)(2,1)S(1)}, f32[12,128]{1,0:T(8,128)S(1)}) custom-call(s32[6]{0:T(128)S(1)} %select_reduce_fusion.2.slots_ref, bf16[32,128,128]{2,1,0:T(8,128)(2,1)} %bitcast.2.own_ref, bf16[32,128,128]{2,1,0:T(8,128)(2,1)} %collective-permute-done.other_ref, bf16[768,128]{1,0:T(8,128)(2,1)S(1)} %broadcast_select_fusion.target_ref, ...), custom_call_target="tpu_custom_call" | custom-call | tf_op jit(solution)/shard_map/pallas_call | solution.py:174
  64.0 0.9 broadcast_in_dim.135
  64.8 4.3 %all-to-all-start.2 = ((f32[64,12,128]{2,1,0:T(8,128)}), f32[64,12,128]{2,1,0:T(8,128)S(1)}, u32[]{:S(2)}, u32[]{:S(2)}) async-start(f32[64,12,128]{2,1,0:T(8,128)} %broadcast_in_dim.135), calls=%async_computation.2 | async-start | bytes 1048576 | tf_op jit(solution)/shard_map/all_to_all | solution.py:184
  70.0 16.5 %all-to-all-done.2.stat_ref = f32[64,12,128]{2,1,0:T(8,128)S(1)} async-done(((f32[64,12,128]{2,1,0:T(8,128)}), f32[64,12,128]{2,1,0:T(8,128)S(1)}, u32[]{:S(2)}, u32[]{:S(2)}) %all-to-all-start.2) | async-done | bytes 393248 | tf_op jit(solution)/shard_map/all_to_all | solution.py:184
  86.5 15.8 %shard_map.77 = (bf16[8192,128]{1,0:T(8,128)(2,1)}, bf16[64,128,128]{2,1,0:T(8,128)(2,1)S(1)}, f32[1,128]{1,0:T(1,128)}) custom-call(s32[6]{0:T(128)S(1)} %select_reduce_fusion.2.slots_ref, s32[1]{0:T(128)} %bitcast.1.live_ref, s32[42]{0:T(128)S(1)} %reshape.222.query_ref, f32[64,12,128]{2,1,0:T(8,128)S(1)} %all-to-all-done.2.stat_ref, ...), custom_call_target="tpu_custom_call" | custom-call | tf_op jit(solution)/shard_map/pallas_call | solution.py:185
  102.3 1.2 fusion.7
  103.5 2.2 %collective-permute-start.1 = (bf16[4,8,128,128]{3,2,1,0:T(8,128)(2,1)}, bf16[4,8,128,128]{3,2,1,0:T(8,128)(2,1)S(1)}, u32[]{:S(2)}, u32[]{:S(2)}) collective-permute-start(bf16[4,8,128,128]{3,2,1,0:T(8,128)(2,1)} %bitcast.8), channel_id=1, source_target_pairs={{0,8},{8,0},{16,24},{24,16},{32,40},{40,32},{48,56},{56,48},{64,72... | collective-permute-start | bytes 3145736 | tf_op jit(solution)/shard_map/ppermute | solution.py:36
  105.8 2.5 %collective-permute-done.1 = bf16[4,8,128,128]{3,2,1,0:T(8,128)(2,1)S(1)} collective-permute-done((bf16[4,8,128,128]{3,2,1,0:T(8,128)(2,1)}, bf16[4,8,128,128]{3,2,1,0:T(8,128)(2,1)S(1)}, u32[]{:S(2)}, u32[]{:S(2)}) %collective-permute-start.1) | collective-permute-done | bytes 1048608 | tf_op jit(solution)/shard_map/ppermute | solution.py:36
  108.6 18.8 %all_to_all.40 = bf16[4,8,128,128]{3,2,1,0:T(8,128)(2,1)S(1)} all-to-all(bf16[4,8,128,128]{3,2,1,0:T(8,128)(2,1)S(1)} %fusion.1), channel_id=1, replica_groups={{0,128,256,384},{8,136,264,392},{16,144,272,400},{24,152,280,408},{32,1..., dimensions={0} | all-to-all | bytes 2097152 | tf_op jit(solution)/shard_map/all_to_all | solution.py:22
  127.4 0.9 reduce_sum.104
  128.3 3.4 %all-to-all-start.4 = ((bf16[8,128,128]{2,1,0:T(8,128)(2,1)}), bf16[8,128,128]{2,1,0:T(8,128)(2,1)S(1)}, u32[]{:S(2)}, u32[]{:S(2)}) async-start(bf16[8,128,128]{2,1,0:T(8,128)(2,1)} %reduce_sum.104), calls=%async_computation.5 | async-start | bytes 524288 | tf_op jit(solution)/shard_map/all_to_all | solution.py:22
  131.8 10.0 %all-to-all-done.4 = bf16[8,128,128]{2,1,0:T(8,128)(2,1)S(1)} async-done(((bf16[8,128,128]{2,1,0:T(8,128)(2,1)}), bf16[8,128,128]{2,1,0:T(8,128)(2,1)S(1)}, u32[]{:S(2)}, u32[]{:S(2)}) %all-to-all-start.4) | async-done | bytes 262176 | tf_op jit(solution)/shard_map/all_to_all | solution.py:22
  142.3 0.7 copy.19
  143.0 4.6 %collective-permute-start.2 = (bf16[32,64,128]{2,1,0:T(8,128)(2,1)S(1)}, bf16[32,64,128]{2,1,0:T(8,128)(2,1)S(1)}, u32[]{:S(2)}, u32[]{:S(2)}) collective-permute-start(bf16[32,64,128]{2,1,0:T(8,128)(2,1)S(1)} %dynamic-slice_bitcast_fusion), channel_id=1, source_target_pairs={{0,8},{8,0},{16,24},{24,16},{32,40},{40,32},{48,56},{56,48},{64,72... | collective-permute-start | bytes 1572872 | tf_op jit(solution)/shard_map/ppermute | solution.py:207
  147.6 1.5 collective-permute-done.2
  149.4 11.6 %all_to_all.41 = bf16[4,8,64,128]{3,2,1,0:T(8,128)(2,1)S(1)} all-to-all(bf16[4,8,64,128]{3,2,1,0:T(8,128)(2,1)S(1)} %bitcast.38), channel_id=1, replica_groups={{0,128,256,384},{8,136,264,392},{16,144,272,400},{24,152,280,408},{32,1..., dimensions={0} | all-to-all | bytes 1048576 | tf_op jit(solution)/shard_map/all_to_all | solution.py:22
  161.1 10.3 %all_to_all.42 = bf16[8,64,128]{2,1,0:T(8,128)(2,1)S(1)} all-to-all(bf16[8,64,128]{2,1,0:T(8,128)(2,1)S(1)} %reduce_sum.106), channel_id=1, replica_groups={{0,16,32,48,64,80,96,112},{8,24,40,56,72,88,104,120},{128,144,160,176,1..., dimensions={0} | all-to-all | bytes 262144 | tf_op jit(solution)/shard_map/all_to_all | solution.py:22
  171.4 17.1 %all_to_all.43 = f32[8,8,128]{2,1,0:T(8,128)S(1)} all-to-all(f32[8,8,128]{2,1,0:T(8,128)S(1)} %bitcast.39), channel_id=1, replica_groups=mesh['cls'=64,'dp'=8] {'dp'}, dimensions={0} | all-to-all | bytes 65536 | tf_op jit(solution)/shard_map/all_to_all | solution.py:211
  188.5 0.6 reduce_sum.108
  189.1 1.8 convert_element_type.71
  (41 shorter events, 2.9 us)
Async XLA Ops:
  7.2 1.2 copy-start
  7.2 11.4 %copy-start.3 = (s32[64,1,6]{0,1,2:T(1,128)S(1)}, s32[64,1,6]{0,1,2:T(1,128)}, u32[]{:S(2)}) copy-start(s32[64,1,6]{0,1,2:T(1,128)} %param.8) | copy-start | bytes 4612
  10.8 24.4 %copy-start.2 = (s32[64,1,128]{2,1,0:T(1,128)S(1)}, s32[64,1,128]{2,1,0:T(1,128)}, u32[]{:S(2)}) copy-start(s32[64,1,128]{2,1,0:T(1,128)} %param.9) | copy-start | bytes 98308
  10.8 42.3 %copy-start.1 = (bf16[8192,128]{1,0:T(8,128)(2,1)S(1)}, bf16[8192,128]{1,0:T(8,128)(2,1)}, u32[]{:S(2)}) copy-start(bf16[8192,128]{1,0:T(8,128)(2,1)} %emb_ref.3) | copy-start | bytes 6291460
  10.8 17.2 %all-to-all-start = ((bf16[8,128,128]{2,1,0:T(8,128)(2,1)}), bf16[8,128,128]{2,1,0:T(8,128)(2,1)S(1)}, u32[]{:S(2)}, u32[]{:S(2)}) async-start(bf16[8,128,128]{2,1,0:T(8,128)(2,1)} %broadcast_in_dim.125), calls=%async_computation | async-start | bytes 524288 | tf_op jit(solution)/shard_map/all_to_all | solution.py:22
  29.3 17.1 %all-to-all-start.1 = ((bf16[4,8,128,128]{3,2,1,0:T(8,128)(2,1)}), bf16[4,8,128,128]{3,2,1,0:T(8,128)(2,1)}, u32[]{:S(2)}, u32[]{:S(2)}) async-start(bf16[4,8,128,128]{3,2,1,0:T(8,128)(2,1)} %broadcast_in_dim.126), calls=%async_computation.1 | async-start | bytes 2097152 | tf_op jit(solution)/shard_map/all_to_all | solution.py:22
  46.3 9.0 %collective-permute-start = (bf16[32,128,128]{2,1,0:T(8,128)(2,1)}, bf16[32,128,128]{2,1,0:T(8,128)(2,1)}, u32[]{:S(2)}, u32[]{:S(2)}) collective-permute-start(bf16[32,128,128]{2,1,0:T(8,128)(2,1)} %bitcast.2.own_ref), channel_id=1, source_target_pairs={{0,8},{8,0},{16,24},{24,16},{32,40},{40,32},{48,56},{56,48},{64,72... | collective-permute-start | bytes 3145736 | tf_op jit(solution)/shard_map/ppermute | solution.py:32
  64.8 21.6 %all-to-all-start.2 = ((f32[64,12,128]{2,1,0:T(8,128)}), f32[64,12,128]{2,1,0:T(8,128)S(1)}, u32[]{:S(2)}, u32[]{:S(2)}) async-start(f32[64,12,128]{2,1,0:T(8,128)} %broadcast_in_dim.135), calls=%async_computation.2 | async-start | bytes 1048576 | tf_op jit(solution)/shard_map/all_to_all | solution.py:184
  69.2 119.9 %reduce-scatter.2.cloned.1.call-start = ((), (), s32[]{:S(2)}) async-start(), calls=%async_computation.9 | async-start | bytes 2359296 | tf_op jit(solution)/shard_map/reduce_scatter | solution.py:199
  103.5 4.8 %collective-permute-start.1 = (bf16[4,8,128,128]{3,2,1,0:T(8,128)(2,1)}, bf16[4,8,128,128]{3,2,1,0:T(8,128)(2,1)S(1)}, u32[]{:S(2)}, u32[]{:S(2)}) collective-permute-start(bf16[4,8,128,128]{3,2,1,0:T(8,128)(2,1)} %bitcast.8), channel_id=1, source_target_pairs={{0,8},{8,0},{16,24},{24,16},{32,40},{40,32},{48,56},{56,48},{64,72... | collective-permute-start | bytes 3145736 | tf_op jit(solution)/shard_map/ppermute | solution.py:36
  128.3 13.4 %all-to-all-start.4 = ((bf16[8,128,128]{2,1,0:T(8,128)(2,1)}), bf16[8,128,128]{2,1,0:T(8,128)(2,1)S(1)}, u32[]{:S(2)}, u32[]{:S(2)}) async-start(bf16[8,128,128]{2,1,0:T(8,128)(2,1)} %reduce_sum.104), calls=%async_computation.5 | async-start | bytes 524288 | tf_op jit(solution)/shard_map/all_to_all | solution.py:22
  143.0 6.1 %collective-permute-start.2 = (bf16[32,64,128]{2,1,0:T(8,128)(2,1)S(1)}, bf16[32,64,128]{2,1,0:T(8,128)(2,1)S(1)}, u32[]{:S(2)}, u32[]{:S(2)}) collective-permute-start(bf16[32,64,128]{2,1,0:T(8,128)(2,1)S(1)} %dynamic-slice_bitcast_fusion), channel_id=1, source_target_pairs={{0,8},{8,0},{16,24},{24,16},{32,40},{40,32},{48,56},{56,48},{64,72... | collective-permute-start | bytes 1572872 | tf_op jit(solution)/shard_map/ppermute | solution.py:207
Sparse Core Ops, SparseCore 0:
  105.9 41.3 reduce-scatter.1

commit v5 on v4

--- a/solution.py
+++ b/solution.py
@@ -32,9 +32,7 @@
     return own, lax.ppermute(own, "cls", SWAP_K)
 
 
-def scatter_cls(outbox):
-    swapped = lax.ppermute(outbox[1], "cls", SWAP_K)
-    total = (outbox[0].astype(F32) + swapped.astype(F32)).astype(BF16)
+def scatter_cls(total):
     total = jnp.sum(exchange(total, GROUP_X), axis=0, dtype=F32).astype(BF16)
     return jnp.sum(exchange(total, GROUP_Y), axis=0, dtype=F32).astype(BF16)
 
@@ -43,7 +41,7 @@
     return lax.dot_general(factors, rows, (((1,), (1,)), ((), ())), preferred_element_type=F32)
 
 
-def stats_kernel(slots_ref, own_ref, other_ref, target_ref, emb_ref, rows_ref, stat_ref, peak_ref, mass_ref):
+def stats_kernel(slots_ref, own_ref, other_ref, target_ref, emb_ref, rows_ref, stat_ref, score_ref, peak_ref, mass_ref):
     step = pl.program_id(0)
     width = rows_ref.shape[0] // LIST
 
@@ -73,42 +71,39 @@
         products = rows_ref[...].astype(F32) * target_ref[...].astype(F32)
         ones = jnp.ones((8, products.shape[1]), F32)
         score = lax.dot_general(ones, products, (((1,), (1,)), ((), ())), precision=lax.Precision.HIGHEST, preferred_element_type=F32)
+        stat_ref[...] = jnp.zeros(stat_ref.shape, F32)
+        score_ref[...] = jnp.zeros(score_ref.shape, F32)
         for slot in range(LIST):
             stat_ref[slot:slot + 1, :] = norm[:, slot * width:(slot + 1) * width]
-            stat_ref[LIST + slot:LIST + 1 + slot, :] = score[0:1, slot * width:(slot + 1) * width]
-
-
-def grads_kernel(slots_ref, live_ref, query_ref, stat_ref, label_ref, rows_ref, emb_ref, part_ref, back_ref, loss_ref, norm_ref, total_ref):
+            score_ref[slot:slot + 1, :] = score[0:1, slot * width:(slot + 1) * width]
+
+
+def grads_kernel(live_ref, query_ref, stat_ref, label_ref, rows_ref, emb_ref, part_ref, back_ref, own_ref, norm_ref, total_ref):
     step = pl.program_id(0)
     width = rows_ref.shape[0] // LIST
 
     def combined(which):
-        norms, label_score = [], jnp.zeros((1, width), F32)
+        norms = []
         for entry in range(LIST):
             place = query_ref[which * LIST + entry]
             base = jnp.maximum(place, 0)
-            block, rank = base // (2 * LIST), lax.rem(base, 2 * LIST)
-            norm = stat_ref[block, pl.ds(rank, 1), :]
-            score = stat_ref[block, pl.ds(rank + LIST, 1), :]
+            norm = stat_ref[base // 8, pl.ds(lax.rem(base, 8), 1), :]
             norms.append(jnp.where(place >= 0, norm, NEG))
-            label_score = label_score + jnp.where(place >= 0, score, 0.0)
         peak = norms[0]
         for norm in norms[1:]:
             peak = jnp.maximum(peak, norm)
         mass = jnp.zeros((1, width), F32)
         for norm in norms:
             mass = mass + jnp.exp(norm - peak)
-        return peak + jnp.log(mass), label_score
+        return peak + jnp.log(mass)
 
     @pl.when(step == 0)
     def _():
         for slot in range(LIST):
-            norm, _ = combined(slot)
+            norm = combined(slot)
             norm_ref[0:1, slot * width:(slot + 1) * width] = jnp.where(slot < live_ref[0], norm, -NEG)
-        norm, label_score = combined(LIST)
-        loss_ref[...] = norm - label_score
+        own_ref[...] = combined(LIST)
         total_ref[...] = jnp.zeros(total_ref.shape, F32)
-        back_ref[...] = jnp.zeros(back_ref.shape, BF16)
 
     tile = emb_ref.shape[0]
     rows = rows_ref[...]
@@ -126,9 +121,20 @@
     @pl.when(step == pl.num_programs(0) - 1)
     def _():
         for slot in range(LIST):
-            @pl.when(slot < live_ref[0])
-            def _():
-                back_ref[slots_ref[slot]] = total_ref[:, slot * width:(slot + 1) * width].T.astype(BF16)
+            back_ref[slot] = total_ref[:, slot * width:(slot + 1) * width].T.astype(BF16)
+
+
+def place_kernel(own_ref, other_ref, back_ref, arrived_ref, out_ref):
+    out_ref[...] = jnp.zeros(out_ref.shape, BF16)
+    for slot in range(LIST):
+        @pl.when(own_ref[slot] >= 0)
+        def _():
+            out_ref[own_ref[slot]] = back_ref[slot]
+    for slot in range(LIST):
+        @pl.when(other_ref[slot] >= 0)
+        def _():
+            held = out_ref[other_ref[slot]].astype(F32)
+            out_ref[other_ref[slot]] = (held + arrived_ref[slot].astype(F32)).astype(BF16)
 
 
 def local(features, proj, class_emb, lists, labels):
@@ -150,9 +156,17 @@
     slot_ids = jnp.arange(LIST, dtype=jnp.int32)
     chosen = (list_rank[None, :] == slot_ids[:, None]) & listed_by[None, :]
     slot_places = jnp.sum(jnp.where(chosen, places[None, :], 0), axis=1)
+    core = own_block % NK
+
+    def kept_places(block):
+        listed = jnp.any(table == block, axis=1)
+        rank = jnp.cumsum(listed.astype(jnp.int32)) - 1
+        taken = (rank[None, :] == slot_ids[:, None]) & (listed & (block_ids % NK == core))[None, :]
+        return jnp.sum(jnp.where(taken, block_ids[None, :] // NK + 1, 0), axis=1) - 1
+
     same = (table[:, :, None, None] == table[None, None]) & (block_ids[None, None, :, None] < block_ids[:, None, None, None])
     entry_rank = jnp.sum(same.astype(jnp.int32), axis=(2, 3))
-    entry_place = table * (2 * LIST) + entry_rank
+    entry_place = table * 8 + entry_rank
     entry_place = jnp.where(table >= 0, entry_place, -1)
     asked = jnp.concatenate([chosen, (block_ids == own_block)[None]], axis=0)
     queries = jnp.sum(jnp.where(asked[:, :, None], entry_place[None], 0), axis=1).reshape(-1)
@@ -171,37 +185,44 @@
     tiled = pl.BlockSpec((TILE, rank_width), lambda i: (i, 0))
     fixed = lambda shape: pl.BlockSpec(shape, lambda i: (0,) * len(shape))
     params = pltpu.CompilerParams(vmem_limit_bytes=48 * 1024 * 1024)
-    rows, stats = pl.pallas_call(
+    rows, stats, scores = pl.pallas_call(
         stats_kernel,
         grid=(block_width // STATS_TILE,),
         in_specs=[smem, whole, whole, whole, pl.BlockSpec((STATS_TILE, rank_width), lambda i: (i, 0))],
-        out_specs=[fixed((all_rows, rank_width)), fixed((2 * LIST, width))],
-        out_shape=[jax.ShapeDtypeStruct((all_rows, rank_width), BF16), jax.ShapeDtypeStruct((2 * LIST, width), F32)],
+        out_specs=[fixed((all_rows, rank_width)), fixed((8, width)), fixed((8, width))],
+        out_shape=[jax.ShapeDtypeStruct((all_rows, rank_width), BF16), jax.ShapeDtypeStruct((8, width), F32), jax.ShapeDtypeStruct((8, width), F32)],
         scratch_shapes=[pltpu.VMEM((8, all_rows), F32)] * 2,
         compiler_params=params,
     )(slot_places, near, far, targets, class_emb)
 
+    all_scores = lax.all_gather(scores, "cls")
     all_stats = lax.all_to_all(spread(stats, blocks), "cls", 0, 0, tiled=True)
-    class_part, outbox, loss = pl.pallas_call(
+    class_part, back, own_norm = pl.pallas_call(
         grads_kernel,
         grid=(steps,),
-        in_specs=[smem, smem, smem, whole, whole, whole, tiled],
-        out_specs=[tiled, fixed((blocks, width, rank_width)), fixed((1, width))],
+        in_specs=[smem, smem, whole, whole, whole, tiled],
+        out_specs=[tiled, fixed((LIST, width, rank_width)), fixed((1, width))],
         out_shape=[
             jax.ShapeDtypeStruct((block_width, rank_width), BF16),
-            jax.ShapeDtypeStruct((blocks, width, rank_width), BF16),
+            jax.ShapeDtypeStruct((LIST, width, rank_width), BF16),
             jax.ShapeDtypeStruct((1, width), F32),
         ],
         scratch_shapes=[pltpu.VMEM((8, all_rows), F32), pltpu.VMEM((rank_width, all_rows), F32)],
         compiler_params=params,
-    )(slot_places, live.reshape(1), queries, all_stats, slot_labels, rows, class_emb)
+    )(live.reshape(1), queries, all_stats, slot_labels, rows, class_emb)
 
     class_grad = lax.psum_scatter(class_part, "dp", scatter_dimension=0, tiled=True).astype(F32)
-    row_grad = scatter_cls(outbox.reshape(NK, NX, NY, width, rank_width))
+    merged = pl.pallas_call(
+        place_kernel,
+        in_specs=[smem, smem, whole, whole],
+        out_specs=whole,
+        out_shape=jax.ShapeDtypeStruct((NX * NY, width, rank_width), BF16),
+        compiler_params=params,
+    )(kept_places(own_block), kept_places(own_block ^ 1), back, lax.ppermute(back, "cls", SWAP_K))
+    row_grad = scatter_cls(merged.reshape(NX, NY, width, rank_width))
     proj_part = lax.dot_general(features, row_grad, (((0,), (0,)), ((), ())), preferred_element_type=F32).astype(BF16)
     share = proj_part.shape[0] // (blocks * groups)
     proj_part = proj_part.reshape(NX * NY, NK, groups * share, rank_width)
-    core = own_block % NK
     kept = lax.dynamic_index_in_dim(proj_part, core, 1, keepdims=False)
     given = lax.dynamic_index_in_dim(proj_part, 1 - core, 1, keepdims=False)
     total = (kept.astype(F32) + lax.ppermute(given, "cls", SWAP_K).astype(F32)).astype(BF16)
@@ -209,7 +230,11 @@
     total = exchange(jnp.sum(total, axis=0, dtype=F32).astype(BF16), GROUP_Y)
     total = jnp.sum(total, axis=0, dtype=F32).reshape(groups, share, rank_width)
     proj_grad = jnp.sum(lax.all_to_all(total, "dp", 0, 0, tiled=True), axis=0)
-    return loss.reshape(-1), class_grad, proj_grad
+    own_places = queries[LIST * LIST:]
+    spots = jnp.arange(blocks * 8, dtype=jnp.int32)
+    wanted = jnp.any(spots[:, None] == own_places[None, :], axis=1)
+    label_score = jnp.sum(jnp.where(wanted[:, None], all_scores.reshape(blocks * 8, width), 0.0), axis=0)
+    return own_norm.reshape(-1) - label_score, class_grad, proj_grad
 
 
 def solution(mesh):

time: 200 us -> 231 us (1.16)
  starting transfers between devices: 33.3 us -> 51.2 us
  waiting for transfers between devices: 50.9 us -> 58.9 us
  other arithmetic: 6.66 us -> 10.6 us
  local copies, waits for them, and re-layouts: 8.14 us -> 11.7 us
    all_gather x0 -> x1, blocking collectives: none -> 39.8 us  [local(): all_scores = lax.all_gather(scores, 'cls')]
    all_to_all x3 -> x1, blocking collectives: 40.7 us -> 17.9 us  [exchange(): lax.all_to_all(value, 'cls', 0, 0, axis_index_groups=groups, tiled=True)]
    all_to_all x1 -> x0, blocking collectives: 17.1 us -> none  [local(): proj_grad = jnp.sum(lax.all_to_all(total, 'dp', 0, 0, tiled=True), axis=0)]
    all_to_all x0 -> x1, starting transfers between devices: none -> 10.2 us  [local(): proj_grad = jnp.sum(lax.all_to_all(total, 'dp', 0, 0, tiled=True), axis=0)]
    all_to_all x3 -> x5, waiting for transfers between devices: 30.4 us -> 38.8 us  [exchange(): lax.all_to_all(value, 'cls', 0, 0, axis_index_groups=groups, tiled=True)]
    all_to_all x3 -> x5, starting transfers between devices: 16.2 us -> 23.6 us  [exchange(): lax.all_to_all(value, 'cls', 0, 0, axis_index_groups=groups, tiled=True)]
    all_to_all x0 -> x1, waiting for transfers between devices: none -> 6.36 us  [local(): proj_grad = jnp.sum(lax.all_to_all(total, 'dp', 0, 0, tiled=True), axis=0)]
    all_to_all x1, waiting for transfers between devices: 16.5 us -> 11.2 us  [local(): all_stats = lax.all_to_all(spread(stats, blocks), 'cls', 0, 0, tiled=True)]
  transfers between devices with their start and end apart: 8 -> 11, of which waited for: 6 -> 8; matrix products, arithmetic and copies ran while one was open for 4% -> 5% of each run, Pallas kernels for 0% -> 0%
where the time goes in v5:
time: 231 us; the launch traced here: 230 us
  waiting for transfers between devices  58.9 us (25%)
  blocking collectives  57.6 us (25%)
  starting transfers between devices  51.2 us (22%)
  Pallas kernels  23.5 us (10%)
  between operations  14.3 us (6%)
  local copies, waits for them, and re-layouts  11.7 us (5%)
  other arithmetic  10.6 us (5%)
    all_gather x1, blocking collectives, local(): all_scores = lax.all_gather(scores, 'cls')  39.8 us
    all_to_all x5, waiting for transfers between devices, exchange(): lax.all_to_all(value, 'cls', 0, 0, axis_index_groups=groups, tiled=True)  38.8 us
    all_to_all x5, starting transfers between devices, exchange(): lax.all_to_all(value, 'cls', 0, 0, axis_index_groups=groups, tiled=True)  23.6 us
    all_to_all x1, blocking collectives, exchange(): lax.all_to_all(value, 'cls', 0, 0, axis_index_groups=groups, tiled=True)  17.9 us
    pallas_call x1, Pallas kernels, local(): pl.pallas_call(grads_kernel, grid=(steps,), in_specs=[smem, smem, whole,...  14.1 us
    all_to_all x1, waiting for transfers between devices, local(): all_stats = lax.all_to_all(spread(stats, blocks), 'cls', 0, 0, tiled=True)  11.2 us
    all_to_all x1, starting transfers between devices, local(): proj_grad = jnp.sum(lax.all_to_all(total, 'dp', 0, 0, tiled=True), axis=0)  10.2 us
    pallas_call x1, Pallas kernels, local(): pl.pallas_call(stats_kernel, grid=(block_width // STATS_TILE,), in_specs=...  8.65 us
  transfers between devices with their start and end apart: 11, of which 8 were waited for; matrix products, arithmetic and copies ran while one was open for 5% of the time, Pallas kernels for 0%

profile of v5, /device:TPU:1, one launch (start us, length us, event | category | flops | bytes accessed | tf_op | source)
XLA Modules:
  0.0 230.1 jit_solution(3537095208936956466)
XLA Ops:
  7.2 1.2 copy-done
  8.4 1.6 convolution_convert_fusion.1
  10.8 7.8 %all-to-all-start = ((bf16[8,128,128]{2,1,0:T(8,128)(2,1)}), bf16[8,128,128]{2,1,0:T(8,128)(2,1)S(1)}, u32[]{:S(2)}, u32[]{:S(2)}) async-start(bf16[8,128,128]{2,1,0:T(8,128)(2,1)} %broadcast_in_dim.162), calls=%async_computation | async-start | bytes 524288 | tf_op jit(solution)/shard_map/all_to_all | solution.py:22
  19.4 8.5 %all-to-all-done = bf16[8,128,128]{2,1,0:T(8,128)(2,1)S(1)} async-done(((bf16[8,128,128]{2,1,0:T(8,128)(2,1)}), bf16[8,128,128]{2,1,0:T(8,128)(2,1)S(1)}, u32[]{:S(2)}, u32[]{:S(2)}) %all-to-all-start) | async-done | bytes 262176 | tf_op jit(solution)/shard_map/all_to_all | solution.py:22
  28.0 1.3 broadcast_in_dim.163
  29.3 5.0 %all-to-all-start.1 = ((bf16[4,8,128,128]{3,2,1,0:T(8,128)(2,1)}), bf16[4,8,128,128]{3,2,1,0:T(8,128)(2,1)}, u32[]{:S(2)}, u32[]{:S(2)}) async-start(bf16[4,8,128,128]{3,2,1,0:T(8,128)(2,1)} %broadcast_in_dim.163), calls=%async_computation.1 | async-start | bytes 2097152 | tf_op jit(solution)/shard_map/all_to_all | solution.py:22
  35.2 11.1 %all-to-all-done.1 = bf16[4,8,128,128]{3,2,1,0:T(8,128)(2,1)} async-done(((bf16[4,8,128,128]{3,2,1,0:T(8,128)(2,1)}), bf16[4,8,128,128]{3,2,1,0:T(8,128)(2,1)}, u32[]{:S(2)}, u32[]{:S(2)}) %all-to-all-start.1) | async-done | bytes 1048608 | tf_op jit(solution)/shard_map/all_to_all | solution.py:22
  46.3 6.0 %collective-permute-start = (bf16[32,128,128]{2,1,0:T(8,128)(2,1)}, bf16[32,128,128]{2,1,0:T(8,128)(2,1)}, u32[]{:S(2)}, u32[]{:S(2)}) collective-permute-start(bf16[32,128,128]{2,1,0:T(8,128)(2,1)} %bitcast.2.own_ref), channel_id=1, source_target_pairs={{0,8},{8,0},{16,24},{24,16},{32,40},{40,32},{48,56},{56,48},{64,72... | collective-permute-start | bytes 3145736 | tf_op jit(solution)/shard_map/ppermute | solution.py:32
  52.5 1.9 gather_fusion
  55.0 8.7 %shard_map.76 = (bf16[768,128]{1,0:T(8,128)(2,1)S(1)}, f32[8,128]{1,0:T(8,128)S(1)}, f32[8,128]{1,0:T(8,128)S(1)}) custom-call(s32[6]{0:T(128)S(1)} %get-tuple-element.19.slots_ref, bf16[32,128,128]{2,1,0:T(8,128)(2,1)} %bitcast.2.own_ref, bf16[32,128,128]{2,1,0:T(8,128)(2,1)} %collective-permute-done.other_ref, ...), custom_call_target="tpu_custom_call" | custom-call | tf_op jit(solution)/shard_map/pallas_call | solution.py:188
  65.0 4.5 %all-to-all-start.2 = ((f32[64,8,128]{2,1,0:T(8,128)}), f32[64,8,128]{2,1,0:T(8,128)S(1)}, u32[]{:S(2)}, u32[]{:S(2)}) async-start(f32[64,8,128]{2,1,0:T(8,128)} %broadcast_in_dim.172), calls=%async_computation.2 | async-start | bytes 524288 | tf_op jit(solution)/shard_map/all_to_all | solution.py:199
  70.3 11.2 %all-to-all-done.2.stat_ref = f32[64,8,128]{2,1,0:T(8,128)S(1)} async-done(((f32[64,8,128]{2,1,0:T(8,128)}), f32[64,8,128]{2,1,0:T(8,128)S(1)}, u32[]{:S(2)}, u32[]{:S(2)}) %all-to-all-start.2) | async-done | bytes 262176 | tf_op jit(solution)/shard_map/all_to_all | solution.py:199
  81.5 0.9 copy-done.4
  82.5 14.1 %shard_map.77 = (bf16[8192,128]{1,0:T(8,128)(2,1)S(1)}, bf16[6,128,128]{2,1,0:T(8,128)(2,1)S(1)}, f32[1,128]{1,0:T(1,128)S(1)}) custom-call(s32[1]{0:T(128)} %bitcast.live_ref, s32[42]{0:T(128)S(1)} %reshape.305.query_ref, f32[64,8,128]{2,1,0:T(8,128)S(1)} %all-to-all-done.2.stat_ref, s32[8,768]{1,0:T(8,128)S(1)} %broadcast_in_dim.173.label_ref, ...), custom_call_target="tpu_custom_call" | custom-call | tf_op jit(solution)/shard_map/pallas_call | solution.py:200
  96.6 1.3 copy-done.2
  98.7 0.9 copy-done.6
  99.5 2.3 %collective-permute-start.1 = (bf16[6,128,128]{2,1,0:T(8,128)(2,1)S(1)}, bf16[6,128,128]{2,1,0:T(8,128)(2,1)S(1)}, u32[]{:S(2)}, u32[]{:S(2)}) collective-permute-start(bf16[6,128,128]{2,1,0:T(8,128)(2,1)S(1)} %copy-done.6), channel_id=1, source_target_pairs={{0,8},{8,0},{16,24},{24,16},{32,40},{40,32},{48,56},{56,48},{64,72... | collective-permute-start | bytes 589832 | tf_op jit(solution)/shard_map/ppermute | solution.py:221
  101.9 1.0 collective-permute-done.1.arrived_ref
  103.7 17.9 %all_to_all.40 = bf16[4,8,128,128]{3,2,1,0:T(8,128)(2,1)} all-to-all(bf16[4,8,128,128]{3,2,1,0:T(8,128)(2,1)S(1)} %bitcast.42), channel_id=1, replica_groups={{0,128,256,384},{8,136,264,392},{16,144,272,400},{24,152,280,408},{32,1..., dimensions={0} | all-to-all | bytes 2097152 | tf_op jit(solution)/shard_map/all_to_all | solution.py:22
  121.6 2.2 reduce_sum.134
  123.8 3.9 %all-to-all-start.4 = ((bf16[8,128,128]{2,1,0:T(8,128)(2,1)}), bf16[8,128,128]{2,1,0:T(8,128)(2,1)S(1)}, u32[]{:S(2)}, u32[]{:S(2)}) async-start(bf16[8,128,128]{2,1,0:T(8,128)(2,1)} %reduce_sum.134), calls=%async_computation.5 | async-start | bytes 524288 | tf_op jit(solution)/shard_map/all_to_all | solution.py:22
  127.7 10.2 %all-to-all-done.4 = bf16[8,128,128]{2,1,0:T(8,128)(2,1)S(1)} async-done(((bf16[8,128,128]{2,1,0:T(8,128)(2,1)}), bf16[8,128,128]{2,1,0:T(8,128)(2,1)S(1)}, u32[]{:S(2)}, u32[]{:S(2)}) %all-to-all-start.4) | async-done | bytes 262176 | tf_op jit(solution)/shard_map/all_to_all | solution.py:22
  139.1 4.6 %collective-permute-start.2 = (bf16[32,64,128]{2,1,0:T(8,128)(2,1)S(1)}, bf16[32,64,128]{2,1,0:T(8,128)(2,1)S(1)}, u32[]{:S(2)}, u32[]{:S(2)}) collective-permute-start(bf16[32,64,128]{2,1,0:T(8,128)(2,1)S(1)} %dynamic-slice_bitcast_fusion), channel_id=1, source_target_pairs={{0,8},{8,0},{16,24},{24,16},{32,40},{40,32},{48,56},{56,48},{64,72... | collective-permute-start | bytes 1572872 | tf_op jit(solution)/shard_map/ppermute | solution.py:228
  143.7 1.5 collective-permute-done.2
  145.2 1.0 fusion.1
  146.2 3.5 %all-to-all-start.5 = ((bf16[4,8,64,128]{3,2,1,0:T(8,128)(2,1)}), bf16[4,8,64,128]{3,2,1,0:T(8,128)(2,1)S(1)}, u32[]{:S(2)}, u32[]{:S(2)}) async-start(bf16[4,8,64,128]{3,2,1,0:T(8,128)(2,1)} %bitcast.14), calls=%async_computation.6 | async-start | bytes 1048576 | tf_op jit(solution)/shard_map/all_to_all | solution.py:22
  149.9 9.0 %all-to-all-done.5 = bf16[4,8,64,128]{3,2,1,0:T(8,128)(2,1)S(1)} async-done(((bf16[4,8,64,128]{3,2,1,0:T(8,128)(2,1)}), bf16[4,8,64,128]{3,2,1,0:T(8,128)(2,1)S(1)}, u32[]{:S(2)}, u32[]{:S(2)}) %all-to-all-start.5) | async-done | bytes 524320 | tf_op jit(solution)/shard_map/all_to_all | solution.py:22
  159.6 3.4 %all-to-all-start.6 = ((bf16[8,64,128]{2,1,0:T(8,128)(2,1)}), bf16[8,64,128]{2,1,0:T(8,128)(2,1)S(1)}, u32[]{:S(2)}, u32[]{:S(2)}) async-start(bf16[8,64,128]{2,1,0:T(8,128)(2,1)} %reduce_sum.136), calls=%async_computation.7 | async-start | bytes 262144 | tf_op jit(solution)/shard_map/all_to_all | solution.py:22
  163.2 39.8 %all-gather = f32[512,128]{1,0:T(8,128)S(1)} all-gather(f32[8,128]{1,0:T(8,128)S(1)} %get-tuple-element.12), channel_id=2, replica_groups=mesh['cls'=64,'dp'=8] {'cls'}, dimensions={0}, use_global_device_ids=true | all-gather | bytes 266240 | tf_op jit(solution)/shard_map/all_gather | solution.py:198
  203.8 10.2 %all-to-all-start.7 = ((f32[8,8,128]{2,1,0:T(8,128)}), f32[8,8,128]{2,1,0:T(8,128)S(1)}, u32[]{:S(2)}, u32[]{:S(2)}) async-start(f32[8,8,128]{2,1,0:T(8,128)} %bitcast.15), calls=%async_computation.8 | async-start | bytes 65536 | tf_op jit(solution)/shard_map/all_to_all | solution.py:232
  214.5 6.4 %all-to-all-done.7 = f32[8,8,128]{2,1,0:T(8,128)S(1)} async-done(((f32[8,8,128]{2,1,0:T(8,128)}), f32[8,8,128]{2,1,0:T(8,128)S(1)}, u32[]{:S(2)}, u32[]{:S(2)}) %all-to-all-start.7) | async-done | bytes 32800 | tf_op jit(solution)/shard_map/all_to_all | solution.py:232
  221.4 1.8 convert_element_type.75
  (64 shorter events, 11.2 us)
Async XLA Ops:
  7.2 1.2 copy-start
  7.2 11.4 %copy-start.8 = (s32[64,1,6]{0,1,2:T(1,128)S(1)}, s32[64,1,6]{0,1,2:T(1,128)}, u32[]{:S(2)}) copy-start(s32[64,1,6]{0,1,2:T(1,128)} %param.8) | copy-start | bytes 4612
  10.8 24.2 %copy-start.7 = (s32[64,1,128]{2,1,0:T(1,128)S(1)}, s32[64,1,128]{2,1,0:T(1,128)}, u32[]{:S(2)}) copy-start(s32[64,1,128]{2,1,0:T(1,128)} %param.9) | copy-start | bytes 98308
  10.8 41.7 %copy-start.1 = (bf16[8192,128]{1,0:T(8,128)(2,1)S(1)}, bf16[8192,128]{1,0:T(8,128)(2,1)}, u32[]{:S(2)}) copy-start(bf16[8192,128]{1,0:T(8,128)(2,1)} %emb_ref.3) | copy-start | bytes 6291460
  10.8 17.2 %all-to-all-start = ((bf16[8,128,128]{2,1,0:T(8,128)(2,1)}), bf16[8,128,128]{2,1,0:T(8,128)(2,1)S(1)}, u32[]{:S(2)}, u32[]{:S(2)}) async-start(bf16[8,128,128]{2,1,0:T(8,128)(2,1)} %broadcast_in_dim.162), calls=%async_computation | async-start | bytes 524288 | tf_op jit(solution)/shard_map/all_to_all | solution.py:22
  29.3 17.1 %all-to-all-start.1 = ((bf16[4,8,128,128]{3,2,1,0:T(8,128)(2,1)}), bf16[4,8,128,128]{3,2,1,0:T(8,128)(2,1)}, u32[]{:S(2)}, u32[]{:S(2)}) async-start(bf16[4,8,128,128]{3,2,1,0:T(8,128)(2,1)} %broadcast_in_dim.163), calls=%async_computation.1 | async-start | bytes 2097152 | tf_op jit(solution)/shard_map/all_to_all | solution.py:22
  46.3 8.6 %collective-permute-start = (bf16[32,128,128]{2,1,0:T(8,128)(2,1)}, bf16[32,128,128]{2,1,0:T(8,128)(2,1)}, u32[]{:S(2)}, u32[]{:S(2)}) collective-permute-start(bf16[32,128,128]{2,1,0:T(8,128)(2,1)} %bitcast.2.own_ref), channel_id=1, source_target_pairs={{0,8},{8,0},{16,24},{24,16},{32,40},{40,32},{48,56},{56,48},{64,72... | collective-permute-start | bytes 3145736 | tf_op jit(solution)/shard_map/ppermute | solution.py:32
  63.6 0.7 copy-start.3
  65.0 16.5 %all-to-all-start.2 = ((f32[64,8,128]{2,1,0:T(8,128)}), f32[64,8,128]{2,1,0:T(8,128)S(1)}, u32[]{:S(2)}, u32[]{:S(2)}) async-start(f32[64,8,128]{2,1,0:T(8,128)} %broadcast_in_dim.172), calls=%async_computation.2 | async-start | bytes 524288 | tf_op jit(solution)/shard_map/all_to_all | solution.py:199
  69.5 151.9 %reduce-scatter.2.cloned.1.call-start = ((), (), s32[]{:S(2)}) async-start(), calls=%async_computation.9 | async-start | bytes 2359296 | tf_op jit(solution)/shard_map/reduce_scatter | solution.py:214
  81.5 0.9 copy-start.4
  96.6 1.4 copy-start.2
  97.9 0.7 copy-start.5
  98.6 0.9 copy-start.6
  99.5 3.4 %collective-permute-start.1 = (bf16[6,128,128]{2,1,0:T(8,128)(2,1)S(1)}, bf16[6,128,128]{2,1,0:T(8,128)(2,1)S(1)}, u32[]{:S(2)}, u32[]{:S(2)}) collective-permute-start(bf16[6,128,128]{2,1,0:T(8,128)(2,1)S(1)} %copy-done.6), channel_id=1, source_target_pairs={{0,8},{8,0},{16,24},{24,16},{32,40},{40,32},{48,56},{56,48},{64,72... | collective-permute-start | bytes 589832 | tf_op jit(solution)/shard_map/ppermute | solution.py:221
  123.8 14.1 %all-to-all-start.4 = ((bf16[8,128,128]{2,1,0:T(8,128)(2,1)}), bf16[8,128,128]{2,1,0:T(8,128)(2,1)S(1)}, u32[]{:S(2)}, u32[]{:S(2)}) async-start(bf16[8,128,128]{2,1,0:T(8,128)(2,1)} %reduce_sum.134), calls=%async_computation.5 | async-start | bytes 524288 | tf_op jit(solution)/shard_map/all_to_all | solution.py:22
  139.1 6.1 %collective-permute-start.2 = (bf16[32,64,128]{2,1,0:T(8,128)(2,1)S(1)}, bf16[32,64,128]{2,1,0:T(8,128)(2,1)S(1)}, u32[]{:S(2)}, u32[]{:S(2)}) collective-permute-start(bf16[32,64,128]{2,1,0:T(8,128)(2,1)S(1)} %dynamic-slice_bitcast_fusion), channel_id=1, source_target_pairs={{0,8},{8,0},{16,24},{24,16},{32,40},{40,32},{48,56},{56,48},{64,72... | collective-permute-start | bytes 1572872 | tf_op jit(solution)/shard_map/ppermute | solution.py:228
  146.2 12.7 %all-to-all-start.5 = ((bf16[4,8,64,128]{3,2,1,0:T(8,128)(2,1)}), bf16[4,8,64,128]{3,2,1,0:T(8,128)(2,1)S(1)}, u32[]{:S(2)}, u32[]{:S(2)}) async-start(bf16[4,8,64,128]{3,2,1,0:T(8,128)(2,1)} %bitcast.14), calls=%async_computation.6 | async-start | bytes 1048576 | tf_op jit(solution)/shard_map/all_to_all | solution.py:22
  159.6 43.5 %all-to-all-start.6 = ((bf16[8,64,128]{2,1,0:T(8,128)(2,1)}), bf16[8,64,128]{2,1,0:T(8,128)(2,1)S(1)}, u32[]{:S(2)}, u32[]{:S(2)}) async-start(bf16[8,64,128]{2,1,0:T(8,128)(2,1)} %reduce_sum.136), calls=%async_computation.7 | async-start | bytes 262144 | tf_op jit(solution)/shard_map/all_to_all | solution.py:22
  203.8 17.1 %all-to-all-start.7 = ((f32[8,8,128]{2,1,0:T(8,128)}), f32[8,8,128]{2,1,0:T(8,128)S(1)}, u32[]{:S(2)}, u32[]{:S(2)}) async-start(f32[8,8,128]{2,1,0:T(8,128)} %bitcast.15), calls=%async_computation.8 | async-start | bytes 65536 | tf_op jit(solution)/shard_map/all_to_all | solution.py:232
Sparse Core Ops, SparseCore 0:
  98.8 41.7 reduce-scatter.1

commit v6 on v5

--- a/solution.py
+++ b/solution.py
@@ -10,6 +10,7 @@
 STATS_TILE = 2048
 TILE = 1024
 PIECE = 256
+EXTRA = 16
 NEG = -1e30
 F32 = jnp.float32
 BF16 = jnp.bfloat16
@@ -78,7 +79,7 @@
             score_ref[slot:slot + 1, :] = score[0:1, slot * width:(slot + 1) * width]
 
 
-def grads_kernel(live_ref, query_ref, stat_ref, label_ref, rows_ref, emb_ref, part_ref, back_ref, own_ref, norm_ref, total_ref):
+def grads_kernel(live_ref, query_ref, stat_ref, score_ref, label_ref, rows_ref, emb_ref, part_ref, back_ref, own_ref, norm_ref, total_ref):
     step = pl.program_id(0)
     width = rows_ref.shape[0] // LIST
 
@@ -121,7 +122,14 @@
     @pl.when(step == pl.num_programs(0) - 1)
     def _():
         for slot in range(LIST):
-            back_ref[slot] = total_ref[:, slot * width:(slot + 1) * width].T.astype(BF16)
+            back_ref[slot, 0:width, :] = total_ref[:, slot * width:(slot + 1) * width].T.astype(BF16)
+            score = score_ref[slot:slot + 1, :]
+            high = score.astype(BF16).astype(F32)
+            middle = (score - high).astype(BF16).astype(F32)
+            low = score - high - middle
+            line = lax.broadcasted_iota(jnp.int32, (EXTRA, width), 0)
+            parts = jnp.where(line == 0, high, jnp.where(line == 1, middle, jnp.where(line == 2, low, 0.0)))
+            back_ref[slot, width:width + EXTRA, :] = parts.astype(BF16)
 
 
 def place_kernel(own_ref, other_ref, back_ref, arrived_ref, out_ref):
@@ -195,31 +203,32 @@
         compiler_params=params,
     )(slot_places, near, far, targets, class_emb)
 
-    all_scores = lax.all_gather(scores, "cls")
     all_stats = lax.all_to_all(spread(stats, blocks), "cls", 0, 0, tiled=True)
     class_part, back, own_norm = pl.pallas_call(
         grads_kernel,
         grid=(steps,),
-        in_specs=[smem, smem, whole, whole, whole, tiled],
-        out_specs=[tiled, fixed((LIST, width, rank_width)), fixed((1, width))],
+        in_specs=[smem, smem, whole, whole, whole, whole, tiled],
+        out_specs=[tiled, fixed((LIST, width + EXTRA, rank_width)), fixed((1, width))],
         out_shape=[
             jax.ShapeDtypeStruct((block_width, rank_width), BF16),
-            jax.ShapeDtypeStruct((LIST, width, rank_width), BF16),
+            jax.ShapeDtypeStruct((LIST, width + EXTRA, rank_width), BF16),
             jax.ShapeDtypeStruct((1, width), F32),
         ],
         scratch_shapes=[pltpu.VMEM((8, all_rows), F32), pltpu.VMEM((rank_width, all_rows), F32)],
         compiler_params=params,
-    )(live.reshape(1), queries, all_stats, slot_labels, rows, class_emb)
+    )(live.reshape(1), queries, all_stats, scores, slot_labels, rows, class_emb)
 
     class_grad = lax.psum_scatter(class_part, "dp", scatter_dimension=0, tiled=True).astype(F32)
     merged = pl.pallas_call(
         place_kernel,
         in_specs=[smem, smem, whole, whole],
         out_specs=whole,
-        out_shape=jax.ShapeDtypeStruct((NX * NY, width, rank_width), BF16),
+        out_shape=jax.ShapeDtypeStruct((NX * NY, width + EXTRA, rank_width), BF16),
         compiler_params=params,
     )(kept_places(own_block), kept_places(own_block ^ 1), back, lax.ppermute(back, "cls", SWAP_K))
-    row_grad = scatter_cls(merged.reshape(NX, NY, width, rank_width))
+    summed = scatter_cls(merged.reshape(NX, NY, width + EXTRA, rank_width))
+    row_grad = summed[:width]
+    label_score = jnp.sum(summed[width:width + 3].astype(F32), axis=0)
     proj_part = lax.dot_general(features, row_grad, (((0,), (0,)), ((), ())), preferred_element_type=F32).astype(BF16)
     share = proj_part.shape[0] // (blocks * groups)
     proj_part = proj_part.reshape(NX * NY, NK, groups * share, rank_width)
@@ -230,10 +239,6 @@
     total = exchange(jnp.sum(total, axis=0, dtype=F32).astype(BF16), GROUP_Y)
     total = jnp.sum(total, axis=0, dtype=F32).reshape(groups, share, rank_width)
     proj_grad = jnp.sum(lax.all_to_all(total, "dp", 0, 0, tiled=True), axis=0)
-    own_places = queries[LIST * LIST:]
-    spots = jnp.arange(blocks * 8, dtype=jnp.int32)
-    wanted = jnp.any(spots[:, None] == own_places[None, :], axis=1)
-    label_score = jnp.sum(jnp.where(wanted[:, None], all_scores.reshape(blocks * 8, width), 0.0), axis=0)
     return own_norm.reshape(-1) - label_score, class_grad, proj_grad
 
 

time: 231 us -> 199 us (0.86)
  blocking collectives: 57.6 us -> 30.8 us
  starting transfers between devices: 51.2 us -> 47.8 us
    all_gather x1 -> x0, blocking collectives: 39.8 us -> none  [local(): all_scores = lax.all_gather(scores, 'cls')]
    all_to_all x1 -> x2, blocking collectives: 17.9 us -> 30.8 us  [exchange(): lax.all_to_all(value, 'cls', 0, 0, axis_index_groups=groups, tiled=True)]
    all_to_all x5 -> x4, starting transfers between devices: 23.6 us -> 19.6 us  [exchange(): lax.all_to_all(value, 'cls', 0, 0, axis_index_groups=groups, tiled=True)]
    all_to_all x5 -> x4, waiting for transfers between devices: 38.8 us -> 37.6 us  [exchange(): lax.all_to_all(value, 'cls', 0, 0, axis_index_groups=groups, tiled=True)]
  transfers between devices with their start and end apart: 11 -> 10, of which waited for: 8 -> 8; matrix products, arithmetic and copies ran while one was open for 5% -> 5% of each run, Pallas kernels for 0% -> 0%
where the time goes in v6:
time: 199 us; the launch traced here: 196 us
  waiting for transfers between devices  57.8 us (29%)
  starting transfers between devices  47.8 us (24%)
  blocking collectives  30.8 us (15%)
  Pallas kernels  23.6 us (12%)
  between operations  14.3 us (7%)
  local copies, waits for them, and re-layouts  11.5 us (6%)
  other arithmetic  8.39 us (4%)
  matrix products  2.1 us (1%)
    all_to_all x4, waiting for transfers between devices, exchange(): lax.all_to_all(value, 'cls', 0, 0, axis_index_groups=groups, tiled=True)  37.6 us
    all_to_all x2, blocking collectives, exchange(): lax.all_to_all(value, 'cls', 0, 0, axis_index_groups=groups, tiled=True)  30.8 us
    all_to_all x4, starting transfers between devices, exchange(): lax.all_to_all(value, 'cls', 0, 0, axis_index_groups=groups, tiled=True)  19.6 us
    pallas_call x1, Pallas kernels, local(): pl.pallas_call(grads_kernel, grid=(steps,), in_specs=[smem, smem, whole,...  14.1 us
    all_to_all x1, waiting for transfers between devices, local(): all_stats = lax.all_to_all(spread(stats, blocks), 'cls', 0, 0, tiled=True)  11.2 us
    all_to_all x1, starting transfers between devices, local(): proj_grad = jnp.sum(lax.all_to_all(total, 'dp', 0, 0, tiled=True), axis=0)  10.2 us
    pallas_call x1, Pallas kernels, local(): pl.pallas_call(stats_kernel, grid=(block_width // STATS_TILE,), in_specs=...  8.69 us
    all_to_all x1, waiting for transfers between devices, local(): proj_grad = jnp.sum(lax.all_to_all(total, 'dp', 0, 0, tiled=True), axis=0)  6.36 us
  transfers between devices with their start and end apart: 10, of which 8 were waited for; matrix products, arithmetic and copies ran while one was open for 5% of the time, Pallas kernels for 0%

profile of v6, /device:TPU:1, one launch (start us, length us, event | category | flops | bytes accessed | tf_op | source)
XLA Modules:
  0.0 196.3 jit_solution(2936047627390138536)
XLA Ops:
  7.2 1.2 copy-done
  8.4 1.6 convolution_convert_fusion.1
  10.8 7.6 %all-to-all-start = ((bf16[8,128,128]{2,1,0:T(8,128)(2,1)}), bf16[8,128,128]{2,1,0:T(8,128)(2,1)S(1)}, u32[]{:S(2)}, u32[]{:S(2)}) async-start(bf16[8,128,128]{2,1,0:T(8,128)(2,1)} %broadcast_in_dim.145), calls=%async_computation | async-start | bytes 524288 | tf_op jit(solution)/shard_map/all_to_all | solution.py:23
  19.3 8.5 %all-to-all-done = bf16[8,128,128]{2,1,0:T(8,128)(2,1)S(1)} async-done(((bf16[8,128,128]{2,1,0:T(8,128)(2,1)}), bf16[8,128,128]{2,1,0:T(8,128)(2,1)S(1)}, u32[]{:S(2)}, u32[]{:S(2)}) %all-to-all-start) | async-done | bytes 262176 | tf_op jit(solution)/shard_map/all_to_all | solution.py:23
  27.8 1.3 broadcast_in_dim.146
  29.1 5.1 %all-to-all-start.1 = ((bf16[4,8,128,128]{3,2,1,0:T(8,128)(2,1)}), bf16[4,8,128,128]{3,2,1,0:T(8,128)(2,1)}, u32[]{:S(2)}, u32[]{:S(2)}) async-start(bf16[4,8,128,128]{3,2,1,0:T(8,128)(2,1)} %broadcast_in_dim.146), calls=%async_computation.1 | async-start | bytes 2097152 | tf_op jit(solution)/shard_map/all_to_all | solution.py:23
  35.2 11.1 %all-to-all-done.1 = bf16[4,8,128,128]{3,2,1,0:T(8,128)(2,1)} async-done(((bf16[4,8,128,128]{3,2,1,0:T(8,128)(2,1)}), bf16[4,8,128,128]{3,2,1,0:T(8,128)(2,1)}, u32[]{:S(2)}, u32[]{:S(2)}) %all-to-all-start.1) | async-done | bytes 1048608 | tf_op jit(solution)/shard_map/all_to_all | solution.py:23
  46.3 6.0 %collective-permute-start = (bf16[32,128,128]{2,1,0:T(8,128)(2,1)}, bf16[32,128,128]{2,1,0:T(8,128)(2,1)}, u32[]{:S(2)}, u32[]{:S(2)}) collective-permute-start(bf16[32,128,128]{2,1,0:T(8,128)(2,1)} %bitcast.2.own_ref), channel_id=1, source_target_pairs={{0,8},{8,0},{16,24},{24,16},{32,40},{40,32},{48,56},{56,48},{64,72... | collective-permute-start | bytes 3145736 | tf_op jit(solution)/shard_map/ppermute | solution.py:33
  52.5 1.9 gather_fusion
  55.0 8.7 %shard_map.76 = (bf16[768,128]{1,0:T(8,128)(2,1)S(1)}, f32[8,128]{1,0:T(8,128)S(1)}, f32[8,128]{1,0:T(8,128)S(1)}) custom-call(s32[6]{0:T(128)S(1)} %get-tuple-element.17.slots_ref, bf16[32,128,128]{2,1,0:T(8,128)(2,1)} %bitcast.2.own_ref, bf16[32,128,128]{2,1,0:T(8,128)(2,1)} %collective-permute-done.other_ref, ...), custom_call_target="tpu_custom_call" | custom-call | tf_op jit(solution)/shard_map/pallas_call | solution.py:196
  65.1 4.5 %all-to-all-start.2 = ((f32[64,8,128]{2,1,0:T(8,128)}), f32[64,8,128]{2,1,0:T(8,128)S(1)}, u32[]{:S(2)}, u32[]{:S(2)}) async-start(f32[64,8,128]{2,1,0:T(8,128)} %broadcast_in_dim.155), calls=%async_computation.2 | async-start | bytes 524288 | tf_op jit(solution)/shard_map/all_to_all | solution.py:206
  70.4 11.2 %all-to-all-done.2.stat_ref = f32[64,8,128]{2,1,0:T(8,128)S(1)} async-done(((f32[64,8,128]{2,1,0:T(8,128)}), f32[64,8,128]{2,1,0:T(8,128)S(1)}, u32[]{:S(2)}, u32[]{:S(2)}) %all-to-all-start.2) | async-done | bytes 262176 | tf_op jit(solution)/shard_map/all_to_all | solution.py:206
  81.6 0.9 copy-done.6
  82.5 14.1 %shard_map.77 = (bf16[8192,128]{1,0:T(8,128)(2,1)S(1)}, bf16[6,144,128]{2,1,0:T(8,128)(2,1)S(1)}, f32[1,128]{1,0:T(1,128)S(1)}) custom-call(s32[1]{0:T(128)} %bitcast.live_ref, s32[42]{0:T(128)S(1)} %reshape.296.query_ref, f32[64,8,128]{2,1,0:T(8,128)S(1)} %all-to-all-done.2.stat_ref, f32[8,128]{1,0:T(8,128)S(1)} %get-tuple-element.10.score_ref, ...), custom_call_target="tpu_custom_call" | custom-call | tf_op jit(solution)/shard_map/pallas_call | solution.py:207
  96.6 1.3 copy-done.2
  98.7 0.9 copy-done.4
  99.6 2.3 %collective-permute-start.1 = (bf16[6,144,128]{2,1,0:T(8,128)(2,1)S(1)}, bf16[6,144,128]{2,1,0:T(8,128)(2,1)S(1)}, u32[]{:S(2)}, u32[]{:S(2)}) collective-permute-start(bf16[6,144,128]{2,1,0:T(8,128)(2,1)S(1)} %copy-done.4), channel_id=1, source_target_pairs={{0,8},{8,0},{16,24},{24,16},{32,40},{40,32},{48,56},{56,48},{64,72... | collective-permute-start | bytes 663560 | tf_op jit(solution)/shard_map/ppermute | solution.py:228
  102.0 1.1 collective-permute-done.1.arrived_ref
  103.0 0.8 shard_map.78
  103.8 19.2 %all_to_all.40 = bf16[4,8,144,128]{3,2,1,0:T(8,128)(2,1)S(1)} all-to-all(bf16[4,8,144,128]{3,2,1,0:T(8,128)(2,1)S(1)} %bitcast.37), channel_id=1, replica_groups={{0,128,256,384},{8,136,264,392},{16,144,272,400},{24,152,280,408},{32,1..., dimensions={0} | all-to-all | bytes 2359296 | tf_op jit(solution)/shard_map/all_to_all | solution.py:23
  123.0 0.9 reduce_sum.133
  124.0 3.4 %all-to-all-start.4 = ((bf16[8,144,128]{2,1,0:T(8,128)(2,1)}), bf16[8,144,128]{2,1,0:T(8,128)(2,1)S(1)}, u32[]{:S(2)}, u32[]{:S(2)}) async-start(bf16[8,144,128]{2,1,0:T(8,128)(2,1)} %reduce_sum.133), calls=%async_computation.4 | async-start | bytes 589824 | tf_op jit(solution)/shard_map/all_to_all | solution.py:23
  127.4 10.1 %all-to-all-done.4 = bf16[8,144,128]{2,1,0:T(8,128)(2,1)S(1)} async-done(((bf16[8,144,128]{2,1,0:T(8,128)(2,1)}), bf16[8,144,128]{2,1,0:T(8,128)(2,1)S(1)}, u32[]{:S(2)}, u32[]{:S(2)}) %all-to-all-start.4) | async-done | bytes 294944 | tf_op jit(solution)/shard_map/all_to_all | solution.py:23
  138.8 5.2 %collective-permute-start.2 = (bf16[32,64,128]{2,1,0:T(8,128)(2,1)S(1)}, bf16[32,64,128]{2,1,0:T(8,128)(2,1)S(1)}, u32[]{:S(2)}, u32[]{:S(2)}) collective-permute-start(bf16[32,64,128]{2,1,0:T(8,128)(2,1)S(1)} %dynamic-slice_bitcast_fusion), channel_id=1, source_target_pairs={{0,8},{8,0},{16,24},{24,16},{32,40},{40,32},{48,56},{56,48},{64,72... | collective-permute-start | bytes 1572872 | tf_op jit(solution)/shard_map/ppermute | solution.py:237
  144.0 1.5 collective-permute-done.2
  145.7 11.6 %all_to_all.41 = bf16[4,8,64,128]{3,2,1,0:T(8,128)(2,1)S(1)} all-to-all(bf16[4,8,64,128]{3,2,1,0:T(8,128)(2,1)S(1)} %bitcast.40), channel_id=1, replica_groups={{0,128,256,384},{8,136,264,392},{16,144,272,400},{24,152,280,408},{32,1..., dimensions={0} | all-to-all | bytes 1048576 | tf_op jit(solution)/shard_map/all_to_all | solution.py:23
  157.4 0.7 reduce_sum.136
  158.1 3.4 %all-to-all-start.6 = ((bf16[8,64,128]{2,1,0:T(8,128)(2,1)}), bf16[8,64,128]{2,1,0:T(8,128)(2,1)S(1)}, u32[]{:S(2)}, u32[]{:S(2)}) async-start(bf16[8,64,128]{2,1,0:T(8,128)(2,1)} %reduce_sum.136), calls=%async_computation.7 | async-start | bytes 262144 | tf_op jit(solution)/shard_map/all_to_all | solution.py:23
  161.5 7.8 %all-to-all-done.6 = bf16[8,64,128]{2,1,0:T(8,128)(2,1)S(1)} async-done(((bf16[8,64,128]{2,1,0:T(8,128)(2,1)}), bf16[8,64,128]{2,1,0:T(8,128)(2,1)S(1)}, u32[]{:S(2)}, u32[]{:S(2)}) %all-to-all-start.6) | async-done | bytes 131104 | tf_op jit(solution)/shard_map/all_to_all | solution.py:23
  170.0 10.2 %all-to-all-start.7 = ((f32[8,8,128]{2,1,0:T(8,128)}), f32[8,8,128]{2,1,0:T(8,128)S(1)}, u32[]{:S(2)}, u32[]{:S(2)}) async-start(f32[8,8,128]{2,1,0:T(8,128)} %bitcast.14), calls=%async_computation.8 | async-start | bytes 65536 | tf_op jit(solution)/shard_map/all_to_all | solution.py:241
  180.7 6.4 %all-to-all-done.7 = f32[8,8,128]{2,1,0:T(8,128)S(1)} async-done(((f32[8,8,128]{2,1,0:T(8,128)}), f32[8,8,128]{2,1,0:T(8,128)S(1)}, u32[]{:S(2)}, u32[]{:S(2)}) %all-to-all-start.7) | async-done | bytes 32800 | tf_op jit(solution)/shard_map/all_to_all | solution.py:241
  187.7 1.8 convert_element_type.81
  (59 shorter events, 9.4 us)
Async XLA Ops:
  7.2 1.2 copy-start
  7.2 11.3 %copy-start.8 = (s32[64,1,6]{0,1,2:T(1,128)S(1)}, s32[64,1,6]{0,1,2:T(1,128)}, u32[]{:S(2)}) copy-start(s32[64,1,6]{0,1,2:T(1,128)} %param.8) | copy-start | bytes 4612
  10.8 17.1 %all-to-all-start = ((bf16[8,128,128]{2,1,0:T(8,128)(2,1)}), bf16[8,128,128]{2,1,0:T(8,128)(2,1)S(1)}, u32[]{:S(2)}, u32[]{:S(2)}) async-start(bf16[8,128,128]{2,1,0:T(8,128)(2,1)} %broadcast_in_dim.145), calls=%async_computation | async-start | bytes 524288 | tf_op jit(solution)/shard_map/all_to_all | solution.py:23
  29.1 5.9 %copy-start.7 = (s32[64,1,128]{2,1,0:T(1,128)S(1)}, s32[64,1,128]{2,1,0:T(1,128)}, u32[]{:S(2)}) copy-start(s32[64,1,128]{2,1,0:T(1,128)} %param.9) | copy-start | bytes 98308
  29.1 23.4 %copy-start.1 = (bf16[8192,128]{1,0:T(8,128)(2,1)S(1)}, bf16[8192,128]{1,0:T(8,128)(2,1)}, u32[]{:S(2)}) copy-start(bf16[8192,128]{1,0:T(8,128)(2,1)} %emb_ref.3) | copy-start | bytes 6291460
  29.1 17.2 %all-to-all-start.1 = ((bf16[4,8,128,128]{3,2,1,0:T(8,128)(2,1)}), bf16[4,8,128,128]{3,2,1,0:T(8,128)(2,1)}, u32[]{:S(2)}, u32[]{:S(2)}) async-start(bf16[4,8,128,128]{3,2,1,0:T(8,128)(2,1)} %broadcast_in_dim.146), calls=%async_computation.1 | async-start | bytes 2097152 | tf_op jit(solution)/shard_map/all_to_all | solution.py:23
  46.3 8.6 %collective-permute-start = (bf16[32,128,128]{2,1,0:T(8,128)(2,1)}, bf16[32,128,128]{2,1,0:T(8,128)(2,1)}, u32[]{:S(2)}, u32[]{:S(2)}) collective-permute-start(bf16[32,128,128]{2,1,0:T(8,128)(2,1)} %bitcast.2.own_ref), channel_id=1, source_target_pairs={{0,8},{8,0},{16,24},{24,16},{32,40},{40,32},{48,56},{56,48},{64,72... | collective-permute-start | bytes 3145736 | tf_op jit(solution)/shard_map/ppermute | solution.py:33
  63.7 0.7 copy-start.5
  65.1 16.5 %all-to-all-start.2 = ((f32[64,8,128]{2,1,0:T(8,128)}), f32[64,8,128]{2,1,0:T(8,128)S(1)}, u32[]{:S(2)}, u32[]{:S(2)}) async-start(f32[64,8,128]{2,1,0:T(8,128)} %broadcast_in_dim.155), calls=%async_computation.2 | async-start | bytes 524288 | tf_op jit(solution)/shard_map/all_to_all | solution.py:206
  69.6 118.1 %reduce-scatter.2.cloned.1.call-start = ((), (), s32[]{:S(2)}) async-start(), calls=%async_computation.9 | async-start | bytes 2359296 | tf_op jit(solution)/shard_map/reduce_scatter | solution.py:221
  81.6 0.9 copy-start.6
  96.6 1.4 copy-start.2
  98.0 0.7 copy-start.3
  98.7 0.9 copy-start.4
  99.6 3.4 %collective-permute-start.1 = (bf16[6,144,128]{2,1,0:T(8,128)(2,1)S(1)}, bf16[6,144,128]{2,1,0:T(8,128)(2,1)S(1)}, u32[]{:S(2)}, u32[]{:S(2)}) collective-permute-start(bf16[6,144,128]{2,1,0:T(8,128)(2,1)S(1)} %copy-done.4), channel_id=1, source_target_pairs={{0,8},{8,0},{16,24},{24,16},{32,40},{40,32},{48,56},{56,48},{64,72... | collective-permute-start | bytes 663560 | tf_op jit(solution)/shard_map/ppermute | solution.py:228
  124.0 13.6 %all-to-all-start.4 = ((bf16[8,144,128]{2,1,0:T(8,128)(2,1)}), bf16[8,144,128]{2,1,0:T(8,128)(2,1)S(1)}, u32[]{:S(2)}, u32[]{:S(2)}) async-start(bf16[8,144,128]{2,1,0:T(8,128)(2,1)} %reduce_sum.133), calls=%async_computation.4 | async-start | bytes 589824 | tf_op jit(solution)/shard_map/all_to_all | solution.py:23
  138.8 6.7 %collective-permute-start.2 = (bf16[32,64,128]{2,1,0:T(8,128)(2,1)S(1)}, bf16[32,64,128]{2,1,0:T(8,128)(2,1)S(1)}, u32[]{:S(2)}, u32[]{:S(2)}) collective-permute-start(bf16[32,64,128]{2,1,0:T(8,128)(2,1)S(1)} %dynamic-slice_bitcast_fusion), channel_id=1, source_target_pairs={{0,8},{8,0},{16,24},{24,16},{32,40},{40,32},{48,56},{56,48},{64,72... | collective-permute-start | bytes 1572872 | tf_op jit(solution)/shard_map/ppermute | solution.py:237
  158.1 11.2 %all-to-all-start.6 = ((bf16[8,64,128]{2,1,0:T(8,128)(2,1)}), bf16[8,64,128]{2,1,0:T(8,128)(2,1)S(1)}, u32[]{:S(2)}, u32[]{:S(2)}) async-start(bf16[8,64,128]{2,1,0:T(8,128)(2,1)} %reduce_sum.136), calls=%async_computation.7 | async-start | bytes 262144 | tf_op jit(solution)/shard_map/all_to_all | solution.py:23
  170.0 17.1 %all-to-all-start.7 = ((f32[8,8,128]{2,1,0:T(8,128)}), f32[8,8,128]{2,1,0:T(8,128)S(1)}, u32[]{:S(2)}, u32[]{:S(2)}) async-start(f32[8,8,128]{2,1,0:T(8,128)} %bitcast.14), calls=%async_computation.8 | async-start | bytes 65536 | tf_op jit(solution)/shard_map/all_to_all | solution.py:241
Sparse Core Ops, SparseCore 0:
  98.8 40.8 reduce-scatter.1

commit v7 on v6

--- a/solution.py
+++ b/solution.py
@@ -7,7 +7,7 @@
 
 LIST = 6
 NX, NY, NK = 4, 8, 2
-STATS_TILE = 2048
+STATS_TILE = 4096
 TILE = 1024
 PIECE = 256
 EXTRA = 16

time: 199 us -> 198 us (level)
  no operation moved by 1% of the time
where the time goes in v7:
time: 198 us; the launch traced here: 196 us
  waiting for transfers between devices  57.9 us (29%)
  starting transfers between devices  47.8 us (24%)
  blocking collectives  30.7 us (16%)
  Pallas kernels  23.3 us (12%)
  between operations  14.3 us (7%)
  local copies, waits for them, and re-layouts  11.5 us (6%)
  other arithmetic  8.39 us (4%)
  matrix products  2.11 us (1%)
    all_to_all x4, waiting for transfers between devices, exchange(): lax.all_to_all(value, 'cls', 0, 0, axis_index_groups=groups, tiled=True)  37.7 us
    all_to_all x2, blocking collectives, exchange(): lax.all_to_all(value, 'cls', 0, 0, axis_index_groups=groups, tiled=True)  30.7 us
    all_to_all x4, starting transfers between devices, exchange(): lax.all_to_all(value, 'cls', 0, 0, axis_index_groups=groups, tiled=True)  19.6 us
    pallas_call x1, Pallas kernels, local(): pl.pallas_call(grads_kernel, grid=(steps,), in_specs=[smem, smem, whole,...  14.1 us
    all_to_all x1, waiting for transfers between devices, local(): all_stats = lax.all_to_all(spread(stats, blocks), 'cls', 0, 0, tiled=True)  11.2 us
    all_to_all x1, starting transfers between devices, local(): proj_grad = jnp.sum(lax.all_to_all(total, 'dp', 0, 0, tiled=True), axis=0)  10.3 us
    pallas_call x1, Pallas kernels, local(): pl.pallas_call(stats_kernel, grid=(block_width // STATS_TILE,), in_specs=...  8.41 us
    all_to_all x1, waiting for transfers between devices, local(): proj_grad = jnp.sum(lax.all_to_all(total, 'dp', 0, 0, tiled=True), axis=0)  6.36 us
  transfers between devices with their start and end apart: 10, of which 8 were waited for; matrix products, arithmetic and copies ran while one was open for 5% of the time, Pallas kernels for 0%

profile of v7, /device:TPU:1, one launch (start us, length us, event | category | flops | bytes accessed | tf_op | source)
XLA Modules:
  0.0 196.0 jit_solution(10364645246139332017)
XLA Ops:
  7.2 1.2 copy-done
  8.4 1.6 convolution_convert_fusion.1
  10.8 7.6 %all-to-all-start = ((bf16[8,128,128]{2,1,0:T(8,128)(2,1)}), bf16[8,128,128]{2,1,0:T(8,128)(2,1)S(1)}, u32[]{:S(2)}, u32[]{:S(2)}) async-start(bf16[8,128,128]{2,1,0:T(8,128)(2,1)} %broadcast_in_dim.145), calls=%async_computation | async-start | bytes 524288 | tf_op jit(solution)/shard_map/all_to_all | solution.py:23
  19.3 8.5 %all-to-all-done = bf16[8,128,128]{2,1,0:T(8,128)(2,1)S(1)} async-done(((bf16[8,128,128]{2,1,0:T(8,128)(2,1)}), bf16[8,128,128]{2,1,0:T(8,128)(2,1)S(1)}, u32[]{:S(2)}, u32[]{:S(2)}) %all-to-all-start) | async-done | bytes 262176 | tf_op jit(solution)/shard_map/all_to_all | solution.py:23
  27.8 1.3 broadcast_in_dim.146
  29.1 5.1 %all-to-all-start.1 = ((bf16[4,8,128,128]{3,2,1,0:T(8,128)(2,1)}), bf16[4,8,128,128]{3,2,1,0:T(8,128)(2,1)}, u32[]{:S(2)}, u32[]{:S(2)}) async-start(bf16[4,8,128,128]{3,2,1,0:T(8,128)(2,1)} %broadcast_in_dim.146), calls=%async_computation.1 | async-start | bytes 2097152 | tf_op jit(solution)/shard_map/all_to_all | solution.py:23
  35.2 11.1 %all-to-all-done.1 = bf16[4,8,128,128]{3,2,1,0:T(8,128)(2,1)} async-done(((bf16[4,8,128,128]{3,2,1,0:T(8,128)(2,1)}), bf16[4,8,128,128]{3,2,1,0:T(8,128)(2,1)}, u32[]{:S(2)}, u32[]{:S(2)}) %all-to-all-start.1) | async-done | bytes 1048608 | tf_op jit(solution)/shard_map/all_to_all | solution.py:23
  46.3 6.0 %collective-permute-start = (bf16[32,128,128]{2,1,0:T(8,128)(2,1)}, bf16[32,128,128]{2,1,0:T(8,128)(2,1)}, u32[]{:S(2)}, u32[]{:S(2)}) collective-permute-start(bf16[32,128,128]{2,1,0:T(8,128)(2,1)} %bitcast.2.own_ref), channel_id=1, source_target_pairs={{0,8},{8,0},{16,24},{24,16},{32,40},{40,32},{48,56},{56,48},{64,72... | collective-permute-start | bytes 3145736 | tf_op jit(solution)/shard_map/ppermute | solution.py:33
  52.5 1.9 gather_fusion
  55.0 8.4 %shard_map.76 = (bf16[768,128]{1,0:T(8,128)(2,1)S(1)}, f32[8,128]{1,0:T(8,128)S(1)}, f32[8,128]{1,0:T(8,128)S(1)}) custom-call(s32[6]{0:T(128)S(1)} %get-tuple-element.17.slots_ref, bf16[32,128,128]{2,1,0:T(8,128)(2,1)} %bitcast.2.own_ref, bf16[32,128,128]{2,1,0:T(8,128)(2,1)} %collective-permute-done.other_ref, ...), custom_call_target="tpu_custom_call" | custom-call | tf_op jit(solution)/shard_map/pallas_call | solution.py:196
  64.8 4.5 %all-to-all-start.2 = ((f32[64,8,128]{2,1,0:T(8,128)}), f32[64,8,128]{2,1,0:T(8,128)S(1)}, u32[]{:S(2)}, u32[]{:S(2)}) async-start(f32[64,8,128]{2,1,0:T(8,128)} %broadcast_in_dim.155), calls=%async_computation.2 | async-start | bytes 524288 | tf_op jit(solution)/shard_map/all_to_all | solution.py:206
  70.1 11.2 %all-to-all-done.2.stat_ref = f32[64,8,128]{2,1,0:T(8,128)S(1)} async-done(((f32[64,8,128]{2,1,0:T(8,128)}), f32[64,8,128]{2,1,0:T(8,128)S(1)}, u32[]{:S(2)}, u32[]{:S(2)}) %all-to-all-start.2) | async-done | bytes 262176 | tf_op jit(solution)/shard_map/all_to_all | solution.py:206
  81.3 0.9 copy-done.6
  82.2 14.1 %shard_map.77 = (bf16[8192,128]{1,0:T(8,128)(2,1)S(1)}, bf16[6,144,128]{2,1,0:T(8,128)(2,1)S(1)}, f32[1,128]{1,0:T(1,128)S(1)}) custom-call(s32[1]{0:T(128)} %bitcast.live_ref, s32[42]{0:T(128)S(1)} %reshape.296.query_ref, f32[64,8,128]{2,1,0:T(8,128)S(1)} %all-to-all-done.2.stat_ref, f32[8,128]{1,0:T(8,128)S(1)} %get-tuple-element.10.score_ref, ...), custom_call_target="tpu_custom_call" | custom-call | tf_op jit(solution)/shard_map/pallas_call | solution.py:207
  96.4 1.3 copy-done.2
  98.4 0.9 copy-done.4
  99.3 2.3 %collective-permute-start.1 = (bf16[6,144,128]{2,1,0:T(8,128)(2,1)S(1)}, bf16[6,144,128]{2,1,0:T(8,128)(2,1)S(1)}, u32[]{:S(2)}, u32[]{:S(2)}) collective-permute-start(bf16[6,144,128]{2,1,0:T(8,128)(2,1)S(1)} %copy-done.4), channel_id=1, source_target_pairs={{0,8},{8,0},{16,24},{24,16},{32,40},{40,32},{48,56},{56,48},{64,72... | collective-permute-start | bytes 663560 | tf_op jit(solution)/shard_map/ppermute | solution.py:228
  101.7 1.1 collective-permute-done.1.arrived_ref
  102.8 0.8 shard_map.78
  103.6 19.1 %all_to_all.40 = bf16[4,8,144,128]{3,2,1,0:T(8,128)(2,1)S(1)} all-to-all(bf16[4,8,144,128]{3,2,1,0:T(8,128)(2,1)S(1)} %bitcast.37), channel_id=1, replica_groups={{0,128,256,384},{8,136,264,392},{16,144,272,400},{24,152,280,408},{32,1..., dimensions={0} | all-to-all | bytes 2359296 | tf_op jit(solution)/shard_map/all_to_all | solution.py:23
  122.7 0.9 reduce_sum.133
  123.6 3.4 %all-to-all-start.4 = ((bf16[8,144,128]{2,1,0:T(8,128)(2,1)}), bf16[8,144,128]{2,1,0:T(8,128)(2,1)S(1)}, u32[]{:S(2)}, u32[]{:S(2)}) async-start(bf16[8,144,128]{2,1,0:T(8,128)(2,1)} %reduce_sum.133), calls=%async_computation.4 | async-start | bytes 589824 | tf_op jit(solution)/shard_map/all_to_all | solution.py:23
  127.1 10.2 %all-to-all-done.4 = bf16[8,144,128]{2,1,0:T(8,128)(2,1)S(1)} async-done(((bf16[8,144,128]{2,1,0:T(8,128)(2,1)}), bf16[8,144,128]{2,1,0:T(8,128)(2,1)S(1)}, u32[]{:S(2)}, u32[]{:S(2)}) %all-to-all-start.4) | async-done | bytes 294944 | tf_op jit(solution)/shard_map/all_to_all | solution.py:23
  138.6 5.1 %collective-permute-start.2 = (bf16[32,64,128]{2,1,0:T(8,128)(2,1)S(1)}, bf16[32,64,128]{2,1,0:T(8,128)(2,1)S(1)}, u32[]{:S(2)}, u32[]{:S(2)}) collective-permute-start(bf16[32,64,128]{2,1,0:T(8,128)(2,1)S(1)} %dynamic-slice_bitcast_fusion), channel_id=1, source_target_pairs={{0,8},{8,0},{16,24},{24,16},{32,40},{40,32},{48,56},{56,48},{64,72... | collective-permute-start | bytes 1572872 | tf_op jit(solution)/shard_map/ppermute | solution.py:237
  143.7 1.5 collective-permute-done.2
  145.4 11.6 %all_to_all.41 = bf16[4,8,64,128]{3,2,1,0:T(8,128)(2,1)S(1)} all-to-all(bf16[4,8,64,128]{3,2,1,0:T(8,128)(2,1)S(1)} %bitcast.40), channel_id=1, replica_groups={{0,128,256,384},{8,136,264,392},{16,144,272,400},{24,152,280,408},{32,1..., dimensions={0} | all-to-all | bytes 1048576 | tf_op jit(solution)/shard_map/all_to_all | solution.py:23
  157.1 0.7 reduce_sum.136
  157.8 3.4 %all-to-all-start.6 = ((bf16[8,64,128]{2,1,0:T(8,128)(2,1)}), bf16[8,64,128]{2,1,0:T(8,128)(2,1)S(1)}, u32[]{:S(2)}, u32[]{:S(2)}) async-start(bf16[8,64,128]{2,1,0:T(8,128)(2,1)} %reduce_sum.136), calls=%async_computation.7 | async-start | bytes 262144 | tf_op jit(solution)/shard_map/all_to_all | solution.py:23
  161.2 7.8 %all-to-all-done.6 = bf16[8,64,128]{2,1,0:T(8,128)(2,1)S(1)} async-done(((bf16[8,64,128]{2,1,0:T(8,128)(2,1)}), bf16[8,64,128]{2,1,0:T(8,128)(2,1)S(1)}, u32[]{:S(2)}, u32[]{:S(2)}) %all-to-all-start.6) | async-done | bytes 131104 | tf_op jit(solution)/shard_map/all_to_all | solution.py:23
  169.7 10.3 %all-to-all-start.7 = ((f32[8,8,128]{2,1,0:T(8,128)}), f32[8,8,128]{2,1,0:T(8,128)S(1)}, u32[]{:S(2)}, u32[]{:S(2)}) async-start(f32[8,8,128]{2,1,0:T(8,128)} %bitcast.14), calls=%async_computation.8 | async-start | bytes 65536 | tf_op jit(solution)/shard_map/all_to_all | solution.py:241
  180.5 6.4 %all-to-all-done.7 = f32[8,8,128]{2,1,0:T(8,128)S(1)} async-done(((f32[8,8,128]{2,1,0:T(8,128)}), f32[8,8,128]{2,1,0:T(8,128)S(1)}, u32[]{:S(2)}, u32[]{:S(2)}) %all-to-all-start.7) | async-done | bytes 32800 | tf_op jit(solution)/shard_map/all_to_all | solution.py:241
  187.4 1.8 convert_element_type.81
  (59 shorter events, 9.4 us)
Async XLA Ops:
  7.2 1.2 copy-start
  7.2 11.3 %copy-start.8 = (s32[64,1,6]{0,1,2:T(1,128)S(1)}, s32[64,1,6]{0,1,2:T(1,128)}, u32[]{:S(2)}) copy-start(s32[64,1,6]{0,1,2:T(1,128)} %param.8) | copy-start | bytes 4612
  10.8 17.1 %all-to-all-start = ((bf16[8,128,128]{2,1,0:T(8,128)(2,1)}), bf16[8,128,128]{2,1,0:T(8,128)(2,1)S(1)}, u32[]{:S(2)}, u32[]{:S(2)}) async-start(bf16[8,128,128]{2,1,0:T(8,128)(2,1)} %broadcast_in_dim.145), calls=%async_computation | async-start | bytes 524288 | tf_op jit(solution)/shard_map/all_to_all | solution.py:23
  29.1 5.9 %copy-start.7 = (s32[64,1,128]{2,1,0:T(1,128)S(1)}, s32[64,1,128]{2,1,0:T(1,128)}, u32[]{:S(2)}) copy-start(s32[64,1,128]{2,1,0:T(1,128)} %param.9) | copy-start | bytes 98308
  29.1 23.4 %copy-start.1 = (bf16[8192,128]{1,0:T(8,128)(2,1)S(1)}, bf16[8192,128]{1,0:T(8,128)(2,1)}, u32[]{:S(2)}) copy-start(bf16[8192,128]{1,0:T(8,128)(2,1)} %emb_ref.3) | copy-start | bytes 6291460
  29.1 17.2 %all-to-all-start.1 = ((bf16[4,8,128,128]{3,2,1,0:T(8,128)(2,1)}), bf16[4,8,128,128]{3,2,1,0:T(8,128)(2,1)}, u32[]{:S(2)}, u32[]{:S(2)}) async-start(bf16[4,8,128,128]{3,2,1,0:T(8,128)(2,1)} %broadcast_in_dim.146), calls=%async_computation.1 | async-start | bytes 2097152 | tf_op jit(solution)/shard_map/all_to_all | solution.py:23
  46.3 8.6 %collective-permute-start = (bf16[32,128,128]{2,1,0:T(8,128)(2,1)}, bf16[32,128,128]{2,1,0:T(8,128)(2,1)}, u32[]{:S(2)}, u32[]{:S(2)}) collective-permute-start(bf16[32,128,128]{2,1,0:T(8,128)(2,1)} %bitcast.2.own_ref), channel_id=1, source_target_pairs={{0,8},{8,0},{16,24},{24,16},{32,40},{40,32},{48,56},{56,48},{64,72... | collective-permute-start | bytes 3145736 | tf_op jit(solution)/shard_map/ppermute | solution.py:33
  63.4 0.7 copy-start.5
  64.8 16.5 %all-to-all-start.2 = ((f32[64,8,128]{2,1,0:T(8,128)}), f32[64,8,128]{2,1,0:T(8,128)S(1)}, u32[]{:S(2)}, u32[]{:S(2)}) async-start(f32[64,8,128]{2,1,0:T(8,128)} %broadcast_in_dim.155), calls=%async_computation.2 | async-start | bytes 524288 | tf_op jit(solution)/shard_map/all_to_all | solution.py:206
  69.3 118.1 %reduce-scatter.2.cloned.1.call-start = ((), (), s32[]{:S(2)}) async-start(), calls=%async_computation.9 | async-start | bytes 2359296 | tf_op jit(solution)/shard_map/reduce_scatter | solution.py:221
  81.3 0.9 copy-start.6
  96.3 1.4 copy-start.2
  97.7 0.7 copy-start.3
  98.4 0.9 copy-start.4
  99.3 3.4 %collective-permute-start.1 = (bf16[6,144,128]{2,1,0:T(8,128)(2,1)S(1)}, bf16[6,144,128]{2,1,0:T(8,128)(2,1)S(1)}, u32[]{:S(2)}, u32[]{:S(2)}) collective-permute-start(bf16[6,144,128]{2,1,0:T(8,128)(2,1)S(1)} %copy-done.4), channel_id=1, source_target_pairs={{0,8},{8,0},{16,24},{24,16},{32,40},{40,32},{48,56},{56,48},{64,72... | collective-permute-start | bytes 663560 | tf_op jit(solution)/shard_map/ppermute | solution.py:228
  123.6 13.7 %all-to-all-start.4 = ((bf16[8,144,128]{2,1,0:T(8,128)(2,1)}), bf16[8,144,128]{2,1,0:T(8,128)(2,1)S(1)}, u32[]{:S(2)}, u32[]{:S(2)}) async-start(bf16[8,144,128]{2,1,0:T(8,128)(2,1)} %reduce_sum.133), calls=%async_computation.4 | async-start | bytes 589824 | tf_op jit(solution)/shard_map/all_to_all | solution.py:23
  138.6 6.7 %collective-permute-start.2 = (bf16[32,64,128]{2,1,0:T(8,128)(2,1)S(1)}, bf16[32,64,128]{2,1,0:T(8,128)(2,1)S(1)}, u32[]{:S(2)}, u32[]{:S(2)}) collective-permute-start(bf16[32,64,128]{2,1,0:T(8,128)(2,1)S(1)} %dynamic-slice_bitcast_fusion), channel_id=1, source_target_pairs={{0,8},{8,0},{16,24},{24,16},{32,40},{40,32},{48,56},{56,48},{64,72... | collective-permute-start | bytes 1572872 | tf_op jit(solution)/shard_map/ppermute | solution.py:237
  157.8 11.2 %all-to-all-start.6 = ((bf16[8,64,128]{2,1,0:T(8,128)(2,1)}), bf16[8,64,128]{2,1,0:T(8,128)(2,1)S(1)}, u32[]{:S(2)}, u32[]{:S(2)}) async-start(bf16[8,64,128]{2,1,0:T(8,128)(2,1)} %reduce_sum.136), calls=%async_computation.7 | async-start | bytes 262144 | tf_op jit(solution)/shard_map/all_to_all | solution.py:23
  169.7 17.1 %all-to-all-start.7 = ((f32[8,8,128]{2,1,0:T(8,128)}), f32[8,8,128]{2,1,0:T(8,128)S(1)}, u32[]{:S(2)}, u32[]{:S(2)}) async-start(f32[8,8,128]{2,1,0:T(8,128)} %bitcast.14), calls=%async_computation.8 | async-start | bytes 65536 | tf_op jit(solution)/shard_map/all_to_all | solution.py:241
Sparse Core Ops, SparseCore 0:
  98.5 40.9 reduce-scatter.1
